TPU v7x, 32 devices: a whole 2x2x4 slice. The times are simulated.
32 devices in a mesh: lon: 16 (over z, y, core), lat: 2 (over x).
Axes of the slice: x: 2, y: 2, z: 4, core: 2. Of those that a mesh axis runs over, the one named last changes fastest.
Arguments:
- slab_features: bfloat16 [24, 256, 1024], P('lat', 'lon'), may hold values from -5 to 5
- upstream_gradient: bfloat16 [24, 256, 1024], P('lat', 'lon'), may hold values from -4 to 4
- rim_feature_rows: bfloat16 [2, 6, 256, 1024], P(None, None, 'lon'), may hold values from -5 to 5
- rim_presence_flags: int32 [2, 6], replicated, may hold values 0 or 1
- feature_rescaling_coefficients: float32 [1024], replicated, may hold values from 0.1 to 1.9
- triple_projection_matrix: bfloat16 [1024, 3072], replicated, may hold values from -0.1875 to 0.1875
- final_projection_matrix: bfloat16 [1024, 1024], replicated, may hold values from -0.75 to 0.75
- score_sharpness: float32 [16], replicated, may hold values from 3 to 12
- column_group_decoder_longitude: int32 [24, 64], P('lat', 'lon'), may hold values from 0 to 15, as said below
Outputs:
- decoder_rows: bfloat16 [2, 16, 16, 6, 4, 1024], P('lat', 'lon')
- input_grad: bfloat16 [24, 256, 1024], P('lat', 'lon')
Inputs may be any that keep to these rules, and one draw needn't show every extreme that they name: `column_group_decoder_longitude`: the 48 segments of one device name any one owner at most 6 times; one owner, drawn anew for every draw, is named exactly 6 times by the segments of every device.
All inputs are finite; a program needn't handle non-finite values.
Results may differ from a plain program's by a relative error of at most 0.0085.
Values may be sent and summed in bfloat16 or wider, within the bound.
No kernel may reach another device: no remote copies, remote signals or barrier semaphores. Data moves between devices by JAX's collectives and lax.ppermute only.
A program may use at most 128 MiB of HBM per device.

v0:
```python
import functools

import jax
import jax.numpy as jnp
import numpy as np
from jax import lax
from jax.experimental import pallas as pl
from jax.experimental.pallas import tpu as pltpu
from jax.sharding import PartitionSpec as P

HEADS = 16
HALO = 6
ROWS = 12
COLS = 16
SEG = 4
D = 1024
HEAD_DIM = D // HEADS
TOKENS = ROWS * COLS
HALF = TOKENS // 2
BAND = HALO * COLS
SIDE = ROWS * HALO
CORNER = 40
QUAD = 256
QUAD_HEADS = QUAD // HEAD_DIM
STEPS = D // QUAD
STACK = QUAD_HEADS * HALF
PAD_SIDE = BAND + 2 * CORNER
MIDDLE = TOKENS + 2 * SIDE
SPAN = PAD_SIDE + MIDDLE
KEYS = SPAN + PAD_SIDE
HALO_ROWS = 2 * PAD_SIDE + 2 * SIDE - BAND
VMEM = 40 * 1024 * 1024
BF = jnp.bfloat16
F32 = jnp.float32


def dot(a, b):
    return jnp.dot(a, b, preferred_element_type=F32)


def dot_nt(a, b):
    return lax.dot_general(a, b, (((1,), (1,)), ((), ())), preferred_element_type=F32)


def dot_tn(a, b):
    return lax.dot_general(a, b, (((0,), (0,)), ((), ())), preferred_element_type=F32)


def selection_table():
    table = np.zeros((2, 2 * (SIDE + CORNER) + 2 * CORNER, TOKENS + BAND), np.float32)
    for lat in range(2):
        for side, first in ((0, COLS - HALO), (1, 0)):
            base = side * (SIDE + CORNER)
            for c in range(HALO):
                for r in range(ROWS):
                    table[lat, base + r * HALO + c, r * COLS + first + c] = 1
                for i in range(HALO):
                    table[lat, base + SIDE + i * HALO + c, TOKENS + i * COLS + first + c] = 1
                    row = i + HALO * (1 - lat)
                    corner = 2 * (SIDE + CORNER) + side * CORNER
                    table[lat, corner + i * HALO + c, row * COLS + first + c] = 1
    return table


def key_table():
    far = 1000
    table = np.full((8, KEYS), far, np.int32)
    table[3] = -1

    def put(at, count, width, first_col, kind):
        for k in range(count * width):
            i, c = divmod(k, width)
            for lat in range(2):
                low = {"lat": ROWS if lat == 0 else -HALO, "own": 0, "rim": -HALO if lat == 0 else ROWS}
                table[lat, at + k] = low[kind] + i
            table[2, at + k] = first_col + c
            if kind == "rim":
                table[3, at + k] = i

    put(0, HALO, COLS, 0, "lat")
    put(BAND, HALO, HALO, -HALO, "lat")
    put(BAND + CORNER, HALO, HALO, COLS, "lat")
    put(PAD_SIDE, ROWS, COLS, 0, "own")
    put(PAD_SIDE + TOKENS, ROWS, HALO, -HALO, "own")
    put(PAD_SIDE + TOKENS + SIDE, ROWS, HALO, COLS, "own")
    put(SPAN, HALO, COLS, 0, "rim")
    put(SPAN + BAND, HALO, HALO, -HALO, "rim")
    put(SPAN + BAND + CORNER, HALO, HALO, COLS, "rim")
    return table


def head_mask(h, dtype):
    lane = lax.broadcasted_iota(jnp.int32, (1, QUAD), 1)
    return jnp.where(lane // HEAD_DIM == h, 1.0, 0.0).astype(dtype)


def head_mean(values):
    a = lax.broadcasted_iota(jnp.int32, (QUAD, QUAD), 0) // HEAD_DIM
    b = lax.broadcasted_iota(jnp.int32, (QUAD, QUAD), 1) // HEAD_DIM
    block = jnp.where(a == b, 1.0 / HEAD_DIM, 0.0).astype(BF)
    high = values.astype(BF)
    low = (values - high.astype(F32)).astype(BF)
    return dot(high, block) + dot(low, block)


def inverse_rms(raw):
    return lax.rsqrt(head_mean(raw * raw) + 1e-06)


def normed(tokens, gain):
    tokens = tokens.astype(F32)
    return tokens * lax.rsqrt(jnp.mean(tokens * tokens, axis=-1, keepdims=True) + 1e-05) * gain


def multiplier(sharp_ref, j):
    out = jnp.zeros((1, QUAD), F32)
    for h in range(QUAD_HEADS):
        out = out + head_mask(h, F32) * (sharp_ref[j * QUAD_HEADS + h] / HEAD_DIM)
    return out


def stacked(block):
    return jnp.concatenate([block * head_mask(h, BF) for h in range(QUAD_HEADS)], axis=0)


def unstacked(stack):
    out = jnp.zeros((HALF, QUAD), F32)
    for h in range(QUAD_HEADS):
        out = out + stack[h * HALF : (h + 1) * HALF] * head_mask(h, F32)
    return out


def half_start(lat, half):
    return pl.multiple_of(HALF * ((1 - lat) if half == 0 else lat), 16)


def pack_kernel(lat_ref, x_ref, rim_ref, sel_ref, fwd_ref, bwd_ref, band_ref, cfwd_ref, cbwd_ref):
    lat = lat_ref[0]
    source = jnp.concatenate([x_ref[...], rim_ref[0]], axis=0)
    picked = dot(sel_ref[0], source)
    at = 0
    for ref in (fwd_ref, bwd_ref, cfwd_ref, cbwd_ref):
        count = ref.shape[0]
        ref[...] = picked[at : at + count].astype(BF)
        at += count
    band_ref[...] = x_ref[pl.ds(half_start(lat, 0), BAND), :]


def own_kernel(
    lat_ref, sharp_ref, x_ref, rim_ref, up_ref, gain_ref, wq_ref, wk_ref, wv_ref, wo_ref,
    qhat_ref, rawq_ref, rawk_ref, kv_ref, dout_ref, xn_ref,
):
    j = pl.program_id(0)

    @pl.when(j == 0)
    def _():
        xn_ref[:TOKENS] = normed(x_ref[...], gain_ref[...]).astype(BF)
        xn_ref[TOKENS:] = normed(rim_ref[0], gain_ref[...]).astype(BF)

    xn = xn_ref[...]
    raw_q = dot(xn[:TOKENS], wq_ref[...])
    rawq_ref[...] = raw_q
    qhat_ref[...] = (raw_q * inverse_rms(raw_q) * multiplier(sharp_ref, j)).astype(BF)
    raw_k = dot(xn, wk_ref[...])
    rawk_ref[...] = raw_k[:TOKENS]
    kv_ref[0] = (raw_k * inverse_rms(raw_k)).astype(BF)
    kv_ref[1] = dot(xn, wv_ref[...]).astype(BF)
    dout_ref[...] = dot_nt(up_ref[...], wo_ref[...]).astype(BF)


def forward_kernel(
    lat_ref, owner_ref, flag_ref, x_ref, band_ref, left_ref, right_ref, cleft_ref, cright_ref, gain_ref, tab_ref,
    wk_ref, wv_ref, wo_ref, qhat_ref, kv_ref,
    key_ref, value_ref, weight_ref, mixed_ref, linv_ref, going_ref,
    xn_ref, mask_ref, acc_ref, count_ref,
):
    j = pl.program_id(0)
    lat = lat_ref[0]

    @pl.when(j == 0)
    def _():
        gain = gain_ref[...]
        left, right = normed(left_ref[...], gain), normed(right_ref[...], gain)
        pieces = [
            normed(band_ref[...], gain), normed(cleft_ref[...], gain), normed(cright_ref[...], gain),
            left[:SIDE], right[:SIDE], left[SIDE:], right[SIDE:],
        ]
        xn_ref[...] = jnp.concatenate(pieces, axis=0).astype(BF)
        acc_ref[...] = x_ref[...].astype(F32)
        rows = jnp.where(lat == 0, tab_ref[0:1], tab_ref[1:2])
        cols, place = tab_ref[2:3], tab_ref[3:4]
        keep = jnp.where(place < 0, 1.0, 0.0)
        for i in range(HALO):
            keep = keep + jnp.where(place == i, flag_ref[lat, i].astype(F32), 0.0)
        for half in range(2):
            at = half * PAD_SIDE
            token = lax.broadcasted_iota(jnp.int32, (HALF, SPAN), 0) + half_start(lat, half)
            near = (jnp.abs(rows[:, at : at + SPAN] - token // COLS) <= HALO) & (
                jnp.abs(cols[:, at : at + SPAN] - token % COLS) <= HALO
            )
            mask_ref[half] = jnp.where(near, keep[:, at : at + SPAN], 0.0)

    xn = xn_ref[...]
    raw_k = dot(xn, wk_ref[...])
    halo_k = (raw_k * inverse_rms(raw_k)).astype(BF)
    halo_v = dot(xn, wv_ref[...]).astype(BF)
    for ref, halo, kind in ((key_ref, halo_k, 0), (value_ref, halo_v, 1)):
        ref[:PAD_SIDE] = halo[:PAD_SIDE]
        ref[PAD_SIDE : PAD_SIDE + TOKENS] = kv_ref[kind, :TOKENS]
        ref[PAD_SIDE + TOKENS : SPAN] = halo[PAD_SIDE : PAD_SIDE + 2 * SIDE]
        ref[SPAN : SPAN + BAND] = kv_ref[kind, TOKENS:]
        ref[SPAN + BAND :] = halo[PAD_SIDE + 2 * SIDE :]
    for half in range(2):
        at, start = half * PAD_SIDE, half_start(lat, half)
        scores = dot_nt(stacked(qhat_ref[pl.ds(start, HALF), :]), key_ref[at : at + SPAN])
        weights = jnp.exp(scores) * jnp.concatenate([mask_ref[half]] * QUAD_HEADS, axis=0)
        inverse = 1.0 / jnp.sum(weights, axis=-1, keepdims=True)
        low = weights.astype(BF)
        weight_ref[0, half] = low
        mixed = dot(low, value_ref[at : at + SPAN]) * inverse
        mixed_ref[pl.ds(start, HALF), :] = unstacked(mixed)
        linv_ref[pl.ds(start, HALF), :] = unstacked(jnp.broadcast_to(inverse, (STACK, QUAD)))
    acc_ref[...] += dot(mixed_ref[...].astype(BF), wo_ref[...])

    @pl.when(j == STEPS - 1)
    def _():
        going_ref[...] = jnp.zeros_like(going_ref)
        for o in range(going_ref.shape[0]):
            count_ref[o] = 0
        for s in range(TOKENS // SEG):
            owner = owner_ref[s // (COLS // SEG), s % (COLS // SEG)]
            slot = count_ref[owner]
            count_ref[owner] = slot + 1
            going_ref[owner, slot] = acc_ref[s * SEG : (s + 1) * SEG, :].astype(BF)


def backward_kernel(
    lat_ref, sharp_ref, weight_ref, key_ref, value_ref, qhat_ref, dout_ref, mixed_ref, linv_ref, rawq_ref, wq_ref,
    gqn_ref, own_ref, band_ref, left_ref, right_ref, cleft_ref, cright_ref,
    dq_ref, acc_ref,
):
    j = pl.program_id(0)
    lat = lat_ref[0]
    for half in range(2):
        at, start = half * PAD_SIDE, half_start(lat, half)
        piece = pl.ds(start, HALF)
        query = stacked(qhat_ref[piece, :])
        grad = dout_ref[piece, :].astype(F32) * linv_ref[piece, :]
        inner = grad * mixed_ref[piece, :]
        inner = jnp.concatenate(
            [jnp.sum(inner * head_mask(h, F32), axis=-1, keepdims=True) for h in range(QUAD_HEADS)], axis=0
        )
        grad = stacked(grad.astype(BF))
        keys = key_ref[at : at + SPAN]
        weights = weight_ref[0, half]
        grad_probs = dot_nt(grad, value_ref[at : at + SPAN])
        grad_scores = (weights.astype(F32) * (grad_probs - inner)).astype(BF)
        dq_ref[piece, :] = unstacked(dot(grad_scores, keys))
        if half == 0:
            acc_ref[0] = dot_tn(grad_scores, query)
            acc_ref[1] = dot_tn(weights, grad)
        else:
            used = 384
            acc_ref[0, PAD_SIDE:] += dot_tn(grad_scores[:, :used], query)[:MIDDLE]
            acc_ref[1, PAD_SIDE:] += dot_tn(weights[:, :used], grad)[:MIDDLE]
    own_ref[...] = acc_ref[:, PAD_SIDE : PAD_SIDE + TOKENS]
    at = 0
    for ref in (band_ref, cleft_ref, cright_ref):
        ref[...] = acc_ref[:, at : at + ref.shape[1]].astype(BF)
        at += ref.shape[1]
    left_ref[...] = acc_ref[:, PAD_SIDE + TOKENS : PAD_SIDE + TOKENS + SIDE].astype(BF)
    right_ref[...] = acc_ref[:, PAD_SIDE + TOKENS + SIDE :].astype(BF)
    grad_query = unit_back(rawq_ref[...], dq_ref[...] * multiplier(sharp_ref, j))
    part = dot_nt(grad_query.astype(BF), wq_ref[...])

    @pl.when(j == 0)
    def _():
        gqn_ref[...] = part

    @pl.when(j > 0)
    def _():
        gqn_ref[...] += part


def unit_back(raw, grad):
    inverse = inverse_rms(raw)
    unit = raw * inverse
    return inverse * (grad - unit * head_mean(unit * grad))


def final_kernel(
    lat_ref, x_ref, up_ref, gain_ref, unsel_ref, own_ref, band_ref, left_ref, right_ref, cleft_ref, cright_ref,
    rawk_ref, wk_ref, wv_ref, gqn_ref, out_ref, acc_ref, sum_ref,
):
    j = pl.program_id(0)
    lat = lat_ref[0]

    @pl.when(j == 0)
    def _():
        acc_ref[...] = gqn_ref[...]

    for kind in range(2):
        arrived = [ref[kind].astype(F32) for ref in (right_ref, left_ref, cright_ref, cleft_ref)]
        arrived = jnp.concatenate(arrived, axis=0).astype(BF)
        sum_ref[kind] = own_ref[kind] + dot(unsel_ref[0], arrived)
        piece = pl.ds(half_start(lat, 0), BAND)
        sum_ref[kind, piece, :] += band_ref[kind].astype(F32)
    grad_keys = unit_back(rawk_ref[...], sum_ref[0]).astype(BF)
    acc_ref[...] += dot_nt(grad_keys, wk_ref[...]) + dot_nt(sum_ref[1].astype(BF), wv_ref[...])

    @pl.when(j == STEPS - 1)
    def _():
        tokens = x_ref[...].astype(F32)
        inverse = lax.rsqrt(jnp.mean(tokens * tokens, axis=-1, keepdims=True) + 1e-05)
        grad = acc_ref[...] * gain_ref[...]
        unit = tokens * inverse
        back = inverse * (grad - unit * jnp.mean(unit * grad, axis=-1, keepdims=True))
        out_ref[...] = (up_ref[...].astype(F32) + back).astype(BF)


SMEM = functools.partial(pl.BlockSpec, memory_space=pltpu.SMEM)


def whole(*shape):
    return pl.BlockSpec(shape, lambda j, lat: (0,) * len(shape))


def by_lat(*shape):
    return pl.BlockSpec((1,) + shape, lambda j, lat: (lat[0],) + (0,) * len(shape))


def lanes(*shape, at=0):
    return pl.BlockSpec(shape + (QUAD,), lambda j, lat: (0,) * len(shape) + (at + j,))


def call(kernel, steps, in_specs, out_specs, out_shape, scratch=(), flops=0, name=None):
    return pl.pallas_call(
        kernel,
        grid_spec=pltpu.PrefetchScalarGridSpec(
            num_scalar_prefetch=1, grid=(steps,), in_specs=in_specs, out_specs=out_specs, scratch_shapes=list(scratch)
        ),
        out_shape=out_shape,
        compiler_params=pltpu.CompilerParams(vmem_limit_bytes=VMEM, dimension_semantics=("arbitrary",)),
        cost_estimate=pl.CostEstimate(flops=flops, bytes_accessed=8 << 20, transcendentals=0),
        name=name,
    )


def like(*shape, dtype=BF):
    return jax.ShapeDtypeStruct(shape, dtype)


def exchange(count, forward, backward, band, corner_forward, corner_backward):
    right = [(i, (i + 1) % count) for i in range(count)]
    left = [(b, a) for a, b in right]

    def across(pairs):
        return [(2 * a + lat, 2 * b + 1 - lat) for a, b in pairs for lat in range(2)]

    return (
        lax.ppermute(forward, "lon", right),
        lax.ppermute(backward, "lon", left),
        lax.ppermute(band, "lat", [(0, 1), (1, 0)]),
        lax.ppermute(corner_forward, ("lon", "lat"), across(right)),
        lax.ppermute(corner_backward, ("lon", "lat"), across(left)),
    )


def per_device(
    slab_features, upstream_gradient, rim_feature_rows, rim_presence_flags, feature_rescaling_coefficients,
    triple_projection_matrix, final_projection_matrix, score_sharpness, column_group_decoder_longitude,
):
    count = lax.axis_size("lon")
    cap = max(2, (2 * (TOKENS // SEG) + count - 1) // count)
    lat = lax.axis_index("lat").astype(jnp.int32).reshape(1)
    x = slab_features.reshape(TOKENS, D)
    up = upstream_gradient.reshape(TOKENS, D)
    rim = rim_feature_rows.reshape(2, BAND, D)
    gain = feature_rescaling_coefficients.reshape(1, D)
    w3, wo = triple_projection_matrix, final_projection_matrix
    table = selection_table()
    selection = jnp.asarray(table, BF)
    edge = SIDE + CORNER
    places = np.concatenate([table[:, :SIDE], table[:, edge : edge + SIDE], table[:, 2 * edge :]], axis=1)
    unselection = jnp.asarray(places[:, :, :TOKENS].transpose(0, 2, 1), BF)

    packed = call(
        pack_kernel, 1,
        [whole(TOKENS, D), by_lat(BAND, D), by_lat(*table.shape[1:])],
        [whole(edge, D), whole(edge, D), whole(BAND, D), whole(CORNER, D), whole(CORNER, D)],
        [like(edge, D), like(edge, D), like(BAND, D), like(CORNER, D), like(CORNER, D)],
        name="edge_tokens",
    )(lat, x, rim, selection)
    halo_left, halo_right, halo_band, corner_left, corner_right = exchange(count, *packed)

    qhat, rawq, rawk, kv, dout = call(
        own_kernel, STEPS,
        [SMEM(), whole(TOKENS, D), by_lat(BAND, D), whole(TOKENS, D), whole(1, D),
         lanes(D), lanes(D, at=STEPS), lanes(D, at=2 * STEPS), pl.BlockSpec((QUAD, D), lambda j, lat: (j, 0))],
        [lanes(TOKENS), lanes(TOKENS), lanes(TOKENS), lanes(2, TOKENS + BAND), lanes(TOKENS)],
        [like(TOKENS, D), like(TOKENS, D, dtype=F32), like(TOKENS, D, dtype=F32), like(2, TOKENS + BAND, D), like(TOKENS, D)],
        [pltpu.VMEM((TOKENS + BAND, D), BF)],
        flops=2 * 1024 * 1024 * (192 * 2 + 288 * 2),
        name="own_projections",
    )(lat, score_sharpness, x, rim, up, gain, w3, w3, w3, wo)

    keys, values, weights, mixed, linv, going = call(
        forward_kernel, STEPS,
        [SMEM(), SMEM(), whole(TOKENS, D), whole(BAND, D), whole(edge, D), whole(edge, D), whole(CORNER, D), whole(CORNER, D),
         whole(1, D), whole(8, KEYS), lanes(D, at=STEPS), lanes(D, at=2 * STEPS),
         pl.BlockSpec((QUAD, D), lambda j, lat: (j, 0)), lanes(TOKENS), lanes(2, TOKENS + BAND)],
        [lanes(KEYS), lanes(KEYS), pl.BlockSpec((1, 2, STACK, SPAN), lambda j, lat: (j, 0, 0, 0)), lanes(TOKENS), lanes(TOKENS),
         whole(count, cap, SEG, D)],
        [like(KEYS, D), like(KEYS, D), like(STEPS, 2, STACK, SPAN), like(TOKENS, D, dtype=F32), like(TOKENS, D, dtype=F32),
         like(count, cap, SEG, D)],
        [pltpu.VMEM((HALO_ROWS, D), BF), pltpu.VMEM((2, HALF, SPAN), F32), pltpu.VMEM((TOKENS, D), F32),
         pltpu.SMEM((count,), jnp.int32)],
        flops=2 * 1024 * 1024 * 2000,
        name="attention_forward",
    )(lat, column_group_decoder_longitude, rim_presence_flags, x, halo_band, halo_left, halo_right, corner_left, corner_right,
      gain, jnp.asarray(key_table()), w3, w3, wo, qhat, kv)

    arrived = lax.all_to_all(going, "lon", split_axis=0, concat_axis=0, tiled=True)

    gqn, own, band, left, right, cleft, cright = call(
        backward_kernel, STEPS,
        [SMEM(), pl.BlockSpec((1, 2, STACK, SPAN), lambda j, lat: (j, 0, 0, 0)), lanes(KEYS), lanes(KEYS)]
        + [lanes(TOKENS)] * 5 + [lanes(D)],
        [whole(TOKENS, D), lanes(2, TOKENS), lanes(2, BAND), lanes(2, SIDE), lanes(2, SIDE), lanes(2, CORNER), lanes(2, CORNER)],
        [like(TOKENS, D, dtype=F32), like(2, TOKENS, D, dtype=F32), like(2, BAND, D), like(2, SIDE, D), like(2, SIDE, D),
         like(2, CORNER, D), like(2, CORNER, D)],
        [pltpu.VMEM((TOKENS, QUAD), F32), pltpu.VMEM((2, SPAN, QUAD), F32)],
        flops=2 * 1024 * 1024 * 2000,
        name="attention_backward",
    )(lat, score_sharpness, weights, keys, values, qhat, dout, mixed, linv, rawq, w3)
    from_left, from_right, from_band, from_cleft, from_cright = exchange(count, right, left, band, cright, cleft)

    input_grad = call(
        final_kernel, STEPS,
        [whole(TOKENS, D), whole(TOKENS, D), whole(1, D), by_lat(*unselection.shape[1:]), lanes(2, TOKENS), lanes(2, BAND),
         lanes(2, SIDE), lanes(2, SIDE), lanes(2, CORNER), lanes(2, CORNER), lanes(TOKENS), lanes(D, at=STEPS),
         lanes(D, at=2 * STEPS), whole(TOKENS, D)],
        whole(TOKENS, D),
        like(TOKENS, D),
        [pltpu.VMEM((TOKENS, D), F32), pltpu.VMEM((2, TOKENS, QUAD), F32)],
        flops=2 * 1024 * 1024 * 400,
        name="input_gradient",
    )(lat, x, up, gain, unselection, own, from_band, from_left, from_right, from_cleft, from_cright, rawk, w3, w3, gqn)
    return (
        arrived.reshape(1, 1, count, cap, SEG, D),
        input_grad.reshape(ROWS, COLS, D),
    )


def solution(mesh):
    return jax.shard_map(
        per_device,
        mesh=mesh,
        in_specs=(
            P("lat", "lon", None),
            P("lat", "lon", None),
            P(None, None, "lon", None),
            P(),
            P(),
            P(),
            P(),
            P(),
            P("lat", "lon"),
        ),
        out_specs=(P("lat", "lon", None, None, None, None), P("lat", "lon", None)),
        check_vma=False,
    )
```

profile of v0, /device:TPU:0, one launch (start us, length us, event | category | flops | bytes accessed | tf_op | source)
XLA Modules:
  0.0 103.9 jit_solution(10067980479233217137)
XLA Ops:
  0.6 0.0 copy-start.3
  0.6 1.0 copy-done.3
  1.6 1.0 copy-done.5
  2.6 1.0 copy-done.11
  3.7 1.3 %edge_tokens.1 = (bf16[112,1024]{1,0:T(8,128)(2,1)}, bf16[112,1024]{1,0:T(8,128)(2,1)}, bf16[96,1024]{1,0:T(8,128)(2,1)}, bf16[40,1024]{1,0:T(8,128)(2,1)}, bf16[40,1024]{1,0:T(8,128)(2,1)}) custom-call(s32[1]{0:T(128)} %bitcast.lat_ref, bf16[192,1024]{1,0:T(8,128)(2,1)S(1)} %bitcast.9, bf16[2,96,1024]{2,1,0:T(8,128)(2,1)S(1)} %bitcast.13, ...), custom_call_target="tpu_custom_call" | custom-call | bytes 8388608 | tf_op jit(solution)/shard_map/edge_tokens/pallas_call | solution.py:387
  5.0 0.5 collective-permute-start.1
  5.4 5.0 %collective-permute-start.2 = (bf16[112,1024]{1,0:T(8,128)(2,1)}, bf16[112,1024]{1,0:T(8,128)(2,1)}, u32[]{:S(2)}, u32[]{:S(2)}) collective-permute-start(bf16[112,1024]{1,0:T(8,128)(2,1)} %get-tuple-element.27), channel_id=1, source_target_pairs={{2,0},{4,2},{6,4},{8,6},{10,8},{12,10},{14,12},{16,14},{18,16},{20... | collective-permute-start | bytes 688136 | tf_op jit(solution)/shard_map/ppermute | solution.py:362
  10.4 1.9 %collective-permute-start = (bf16[96,1024]{1,0:T(8,128)(2,1)}, bf16[96,1024]{1,0:T(8,128)(2,1)}, u32[]{:S(2)}, u32[]{:S(2)}) collective-permute-start(bf16[96,1024]{1,0:T(8,128)(2,1)} %get-tuple-element.25), channel_id=1, source_target_pairs={{0,1},{1,0},{2,3},{3,2},{4,5},{5,4},{6,7},{7,6},{8,9},{9,8},{10,11... | collective-permute-start | bytes 589832 | tf_op jit(solution)/shard_map/ppermute | solution.py:363
  12.4 5.3 %collective-permute-start.4 = (bf16[40,1024]{1,0:T(8,128)(2,1)}, bf16[40,1024]{1,0:T(8,128)(2,1)}, u32[]{:S(2)}, u32[]{:S(2)}) collective-permute-start(bf16[40,1024]{1,0:T(8,128)(2,1)} %get-tuple-element.29), channel_id=1, source_target_pairs={{2,1},{3,0},{4,3},{5,2},{6,5},{7,4},{8,7},{9,6},{10,9},{11,8},{12,... | collective-permute-start | bytes 245768 | tf_op jit(solution)/shard_map/ppermute | solution.py:365
  17.7 2.8 %copy-done = bf16[1024,3072]{1,0:T(8,128)(2,1)S(1)} copy-done((bf16[1024,3072]{1,0:T(8,128)(2,1)S(1)}, bf16[1024,3072]{1,0:T(8,128)(2,1)}, u32[]{:S(2)}) %copy-start) | copy-done | bytes 6291480
  20.5 1.6 %copy-done.1 = bf16[1024,1024]{1,0:T(8,128)(2,1)S(1)} copy-done((bf16[1024,1024]{1,0:T(8,128)(2,1)S(1)}, bf16[1024,1024]{1,0:T(8,128)(2,1)}, u32[]{:S(2)}) %copy-start.1) | copy-done | bytes 2097176
  22.1 1.0 copy-done.6
  23.1 0.7 copy-done.16
  23.8 0.7 copy-done.20
  24.4 0.0 copy-start.18
  24.4 7.3 %own_projections.1 = (bf16[192,1024]{1,0:T(8,128)(2,1)S(1)}, f32[192,1024]{1,0:T(8,128)S(1)}, f32[192,1024]{1,0:T(8,128)S(1)}, bf16[2,288,1024]{2,1,0:T(8,128)(2,1)S(1)}, bf16[192,1024]{1,0:T(8,128)(2,1)S(1)}) custom-call(s32[1]{0:T(128)} %bitcast.lat_ref, f32[16]{0:T(128)S(1)} %copy-done.20, bf16[192,1024]{1,0:T(8,128)(2,1)S(1)} %bitcast.10, ...), custom_call_target="tpu_custom_call" | custom-call | flops 2013265920 | bytes 8388608 | tf_op jit(solution)/shard_map/own_projections/pallas_call | solution.py:396
  31.8 1.1 %copy-done.8 = bf16[2,288,1024]{2,1,0:T(8,128)(2,1)} copy-done((bf16[2,288,1024]{2,1,0:T(8,128)(2,1)}, bf16[2,288,1024]{2,1,0:T(8,128)(2,1)S(1)}, u32[]{:S(2)}) %copy-start.8) | copy-done | bytes 1179672
  32.9 0.7 copy-done.12
  33.6 0.9 copy-done.28
  34.5 0.7 copy-done.34
  35.2 0.1 copy.14.owner_ref
  35.4 1.3 %copy-done.9 = bf16[2,288,1024]{2,1,0:T(8,128)(2,1)S(1)} copy-done((bf16[2,288,1024]{2,1,0:T(8,128)(2,1)S(1)}, bf16[2,288,1024]{2,1,0:T(8,128)(2,1)}, u32[]{:S(2)}) %copy-start.9) | copy-done | bytes 1179672
  36.7 1.0 copy-done.13
  37.7 11.5 %attention_forward.1 = (bf16[688,1024]{1,0:T(8,128)(2,1)S(1)}, bf16[688,1024]{1,0:T(8,128)(2,1)S(1)}, bf16[4,2,384,512]{3,2,1,0:T(8,128)(2,1)S(1)}, f32[192,1024...) custom-call(s32[1]{0:T(128)} %bitcast.lat_ref, s32[12,4]{1,0:T(8,128)S(1)} %copy.14.owner_ref, ...), custom_call_target="tpu_custom_call" | custom-call | flops 4194304000 | bytes 8388608 | tf_op jit(solution)/shard_map/attention_forward/pallas_call | solution.py:407
  49.2 0.0 copy-start.10
  49.2 0.9 copy-done.10
  50.1 1.6 %copy-done.22 = bf16[4,2,384,512]{3,2,1,0:T(8,128)(2,1)} copy-done((bf16[4,2,384,512]{3,2,1,0:T(8,128)(2,1)}, bf16[4,2,384,512]{3,2,1,0:T(8,128)(2,1)S(1)}, u32[]{:S(2)}) %copy-start.22) | copy-done | bytes 3145752
  51.7 1.1 %copy-done.24 = bf16[688,1024]{1,0:T(8,128)(2,1)} copy-done((bf16[688,1024]{1,0:T(8,128)(2,1)}, bf16[688,1024]{1,0:T(8,128)(2,1)S(1)}, u32[]{:S(2)}) %copy-start.24) | copy-done | bytes 1409048
  52.8 1.2 %copy-done.26 = bf16[688,1024]{1,0:T(8,128)(2,1)} copy-done((bf16[688,1024]{1,0:T(8,128)(2,1)}, bf16[688,1024]{1,0:T(8,128)(2,1)S(1)}, u32[]{:S(2)}) %copy-start.26) | copy-done | bytes 1409048
  53.9 0.9 copy-done.30
  54.9 0.9 copy-done.32
  55.7 4.4 %all-to-all-start = ((bf16[16,6,4,1024]{3,2,1,0:T(4,128)(2,1)}), bf16[16,6,4,1024]{3,2,1,0:T(4,128)(2,1)}, u32[]{:S(2)}, u32[]{:S(2)}) async-start(bf16[16,6,4,1024]{3,2,1,0:T(4,128)(2,1)} %copy-done.10), calls=%async_computation | async-start | bytes 1572864 | tf_op jit(solution)/shard_map/all_to_all | solution.py:423
  60.2 0.0 slice-start
  60.2 2.0 %copy-done.23 = bf16[4,2,384,512]{3,2,1,0:T(8,128)(2,1)S(1)} copy-done((bf16[4,2,384,512]{3,2,1,0:T(8,128)(2,1)S(1)}, bf16[4,2,384,512]{3,2,1,0:T(8,128)(2,1)}, u32[]{:S(2)}) %copy-start.23) | copy-done | bytes 3145752
  62.3 1.5 %copy-done.25 = bf16[688,1024]{1,0:T(8,128)(2,1)S(1)} copy-done((bf16[688,1024]{1,0:T(8,128)(2,1)S(1)}, bf16[688,1024]{1,0:T(8,128)(2,1)}, u32[]{:S(2)}) %copy-start.25) | copy-done | bytes 1409048
  63.7 1.3 %copy-done.27 = bf16[688,1024]{1,0:T(8,128)(2,1)S(1)} copy-done((bf16[688,1024]{1,0:T(8,128)(2,1)S(1)}, bf16[688,1024]{1,0:T(8,128)(2,1)}, u32[]{:S(2)}) %copy-start.27) | copy-done | bytes 1409048
  65.1 1.1 %copy-done.31 = f32[192,1024]{1,0:T(8,128)S(1)} copy-done((f32[192,1024]{1,0:T(8,128)S(1)}, f32[192,1024]{1,0:T(8,128)}, u32[]{:S(2)}) %copy-start.31) | copy-done | bytes 786456
  66.2 1.1 %copy-done.33 = f32[192,1024]{1,0:T(8,128)S(1)} copy-done((f32[192,1024]{1,0:T(8,128)S(1)}, f32[192,1024]{1,0:T(8,128)}, u32[]{:S(2)}) %copy-start.33) | copy-done | bytes 786456
  67.4 1.0 copy-done.35
  68.4 9.3 %attention_backward.1 = (f32[192,1024]{1,0:T(8,128)S(1)}, f32[2,192,1024]{2,1,0:T(8,128)S(1)}, bf16[2,96,1024]{2,1,0:T(8,128)(2,1)S(1)}, bf16[2,72,1024]{2,1,0:T...) custom-call(s32[1]{0:T(128)} %bitcast.lat_ref, ...), custom_call_target="tpu_custom_call" | custom-call | flops 4194304000 | bytes 8388608 | tf_op jit(solution)/shard_map/attention_backward/pallas_call | solution.py:425
  77.7 0.2 collective-permute-start.5
  77.9 0.2 collective-permute-start.6
  78.1 4.2 %collective-permute-start.7 = (bf16[2,72,1024]{2,1,0:T(8,128)(2,1)S(1)}, bf16[2,72,1024]{2,1,0:T(8,128)(2,1)S(1)}, u32[]{:S(2)}, u32[]{:S(2)}) collective-permute-start(bf16[2,72,1024]{2,1,0:T(8,128)(2,1)S(1)} %get-tuple-element.43), channel_id=1, source_target_pairs={{2,0},{4,2},{6,4},{8,6},{10,8},{12,10},{14,12},{16,14},{18,16},{20... | collective-permute-start | bytes 884744 | tf_op jit(solution)/shard_map/ppermute | solution.py:362
  82.3 5.3 %collective-permute-start.9 = (bf16[2,40,1024]{2,1,0:T(8,128)(2,1)S(1)}, bf16[2,40,1024]{2,1,0:T(8,128)(2,1)S(1)}, u32[]{:S(2)}, u32[]{:S(2)}) collective-permute-start(bf16[2,40,1024]{2,1,0:T(8,128)(2,1)S(1)} %get-tuple-element.45), channel_id=1, source_target_pairs={{2,1},{3,0},{4,3},{5,2},{6,5},{7,4},{8,7},{9,6},{10,9},{11,8},{12,... | collective-permute-start | bytes 491528 | tf_op jit(solution)/shard_map/ppermute | solution.py:365
  87.6 5.0 %collective-permute-done.8.cleft_ref = bf16[2,40,1024]{2,1,0:T(8,128)(2,1)S(1)} collective-permute-done((bf16[2,40,1024]{2,1,0:T(8,128)(2,1)S(1)}, bf16[2,40,1024]{2,1,0:T(8,128)(2,1)S(1)}, u32[]{:S(2)}, u32[]{:S(2)}) %collective-permute-start.8) | collective-permute-done | bytes 163872 | tf_op jit(solution)/shard_map/ppermute | solution.py:364
  92.6 3.4 %collective-permute-done.9.cright_ref = bf16[2,40,1024]{2,1,0:T(8,128)(2,1)S(1)} collective-permute-done((bf16[2,40,1024]{2,1,0:T(8,128)(2,1)S(1)}, bf16[2,40,1024]{2,1,0:T(8,128)(2,1)S(1)}, u32[]{:S(2)}, u32[]{:S(2)}) %collective-permute-start.9) | collective-permute-done | bytes 163872 | tf_op jit(solution)/shard_map/ppermute | solution.py:365
  96.1 5.5 %input_gradient.1 = bf16[192,1024]{1,0:T(8,128)(2,1)} custom-call(s32[1]{0:T(128)} %bitcast.lat_ref, bf16[192,1024]{1,0:T(8,128)(2,1)S(1)} %bitcast.12, bf16[192,1024]{1,0:T(8,128)(2,1)S(1)} %bitcast.16, f32[1,1024]{1,0:T(1,128)S(1)} %bitcast.19, bf16[2,192,224]{2,1,0:T(8,128)(2,1)S(1)} %copy-done.15, f32[2,192,1024]{2,1,0:T(8,128)S(1)} %get-tuple-element.40.own_ref, ...), custom_call_target="tpu_custom_call" | custom-call | flops 838860800 | bytes 8388608 | tf_op jit(solution)/shard_map/input_gradient/pallas_call | solution.py:438
  101.6 2.3 %copy.16 = bf16[1,1,16,6,4,1024]{5,4,3,2,1,0:T(4,128)(2,1)} copy(bf16[1,1,16,6,4,1024]{5,4,3,2,1,0:T(4,128)(2,1)} %bitcast.5) | data formatting | bytes 1572864
  (60 shorter events, 0.1 us)
Async XLA Ops:
  0.6 1.0 copy-start.3
  1.6 1.0 copy-start.5
  2.6 1.0 copy-start.11
  5.0 30.4 %collective-permute-start.1 = (bf16[112,1024]{1,0:T(8,128)(2,1)}, bf16[112,1024]{1,0:T(8,128)(2,1)S(1)}, u32[]{:S(2)}, u32[]{:S(2)}) collective-permute-start(bf16[112,1024]{1,0:T(8,128)(2,1)} %get-tuple-element.26), channel_id=1, source_target_pairs={{0,2},{2,4},{4,6},{6,8},{8,10},{10,12},{12,14},{14,16},{16,18},{18... | collective-permute-start | bytes 688136 | tf_op jit(solution)/shard_map/ppermute | solution.py:361
  5.4 29.9 %collective-permute-start.2 = (bf16[112,1024]{1,0:T(8,128)(2,1)}, bf16[112,1024]{1,0:T(8,128)(2,1)}, u32[]{:S(2)}, u32[]{:S(2)}) collective-permute-start(bf16[112,1024]{1,0:T(8,128)(2,1)} %get-tuple-element.27), channel_id=1, source_target_pairs={{2,0},{4,2},{6,4},{8,6},{10,8},{12,10},{14,12},{16,14},{18,16},{20... | collective-permute-start | bytes 688136 | tf_op jit(solution)/shard_map/ppermute | solution.py:362
  10.4 24.9 %collective-permute-start = (bf16[96,1024]{1,0:T(8,128)(2,1)}, bf16[96,1024]{1,0:T(8,128)(2,1)}, u32[]{:S(2)}, u32[]{:S(2)}) collective-permute-start(bf16[96,1024]{1,0:T(8,128)(2,1)} %get-tuple-element.25), channel_id=1, source_target_pairs={{0,1},{1,0},{2,3},{3,2},{4,5},{5,4},{6,7},{7,6},{8,9},{9,8},{10,11... | collective-permute-start | bytes 589832 | tf_op jit(solution)/shard_map/ppermute | solution.py:363
  12.3 23.0 %collective-permute-start.3 = (bf16[40,1024]{1,0:T(8,128)(2,1)}, bf16[40,1024]{1,0:T(8,128)(2,1)}, u32[]{:S(2)}, u32[]{:S(2)}) collective-permute-start(bf16[40,1024]{1,0:T(8,128)(2,1)} %get-tuple-element.28), channel_id=1, source_target_pairs={{0,3},{1,2},{2,5},{3,4},{4,7},{5,6},{6,9},{7,8},{8,11},{9,10},{10,... | collective-permute-start | bytes 245768 | tf_op jit(solution)/shard_map/ppermute | solution.py:364
  12.4 23.0 %collective-permute-start.4 = (bf16[40,1024]{1,0:T(8,128)(2,1)}, bf16[40,1024]{1,0:T(8,128)(2,1)}, u32[]{:S(2)}, u32[]{:S(2)}) collective-permute-start(bf16[40,1024]{1,0:T(8,128)(2,1)} %get-tuple-element.29), channel_id=1, source_target_pairs={{2,1},{3,0},{4,3},{5,2},{6,5},{7,4},{8,7},{9,6},{10,9},{11,8},{12,... | collective-permute-start | bytes 245768 | tf_op jit(solution)/shard_map/ppermute | solution.py:365
  17.7 2.8 %copy-start = (bf16[1024,3072]{1,0:T(8,128)(2,1)S(1)}, bf16[1024,3072]{1,0:T(8,128)(2,1)}, u32[]{:S(2)}) copy-start(bf16[1024,3072]{1,0:T(8,128)(2,1)} %wv_ref.5) | copy-start | bytes 18874372
  20.5 1.6 %copy-start.1 = (bf16[1024,1024]{1,0:T(8,128)(2,1)S(1)}, bf16[1024,1024]{1,0:T(8,128)(2,1)}, u32[]{:S(2)}) copy-start(bf16[1024,1024]{1,0:T(8,128)(2,1)} %wo_ref.3) | copy-start | bytes 6291460
  22.1 1.0 copy-start.6
  24.4 10.8 %copy-start.36 = (s32[12,4]{0,1:T(4,128)S(1)}, s32[12,4]{0,1:T(4,128)}, u32[]{:S(2)}) copy-start(s32[12,4]{0,1:T(4,128)} %param.20) | copy-start | bytes 580
  24.4 11.0 %copy-start.2 = (bf16[1024,1024]{1,0:T(8,128)(2,1)S(1)}, bf16[1024,1024]{1,0:T(8,128)(2,1)}, u32[]{:S(2)}) copy-start(bf16[1024,1024]{1,0:T(8,128)(2,1)} %wo_ref.3) | copy-start | bytes 6291460
  24.4 11.0 %copy-start.4 = (bf16[12,16,1024]{2,1,0:T(8,128)(2,1)S(1)}, bf16[12,16,1024]{2,1,0:T(8,128)(2,1)}, u32[]{:S(2)}) copy-start(bf16[12,16,1024]{2,1,0:T(8,128)(2,1)} %param.12) | copy-start | bytes 1179652
  24.4 11.0 %copy-start.17 = (f32[1024]{0:T(1024)S(1)}, f32[1024]{0:T(1024)}, u32[]{:S(2)}) copy-start(f32[1024]{0:T(1024)} %param.16) | copy-start | bytes 12292
  24.4 11.0 %copy-start.18 = (s32[8,688]{1,0:T(8,128)S(1)}, s32[8,688]{1,0:T(8,128)}, u32[]{:S(2)}) copy-start(s32[8,688]{1,0:T(8,128)} %constant.12.clone.tab_ref) | copy-start | bytes 66052
  24.4 11.0 %copy-start.19 = (s32[2,6]{1,0:T(2,128)S(1)}, s32[2,6]{1,0:T(2,128)}, u32[]{:S(2)}) copy-start(s32[2,6]{1,0:T(2,128)} %flag_ref.1) | copy-start | bytes 148
  31.8 1.1 %copy-start.8 = (bf16[2,288,1024]{2,1,0:T(8,128)(2,1)}, bf16[2,288,1024]{2,1,0:T(8,128)(2,1)S(1)}, u32[]{:S(2)}) copy-start(bf16[2,288,1024]{2,1,0:T(8,128)(2,1)S(1)} %get-tuple-element.31.kv_ref) | copy-start | bytes 3538948
  32.9 0.7 copy-start.12
  33.6 0.9 copy-start.28
  34.5 0.7 copy-start.34
  35.4 1.3 %copy-start.9 = (bf16[2,288,1024]{2,1,0:T(8,128)(2,1)S(1)}, bf16[2,288,1024]{2,1,0:T(8,128)(2,1)}, u32[]{:S(2)}) copy-start(bf16[2,288,1024]{2,1,0:T(8,128)(2,1)} %copy-done.8) | copy-start | bytes 3538948
  36.7 1.0 copy-start.13
  49.2 0.9 copy-start.10
  50.0 1.6 %copy-start.22 = (bf16[4,2,384,512]{3,2,1,0:T(8,128)(2,1)}, bf16[4,2,384,512]{3,2,1,0:T(8,128)(2,1)S(1)}, u32[]{:S(2)}) copy-start(bf16[4,2,384,512]{3,2,1,0:T(8,128)(2,1)S(1)} %get-tuple-element.33.weight_ref) | copy-start | bytes 9437188
  51.7 1.1 %copy-start.24 = (bf16[688,1024]{1,0:T(8,128)(2,1)}, bf16[688,1024]{1,0:T(8,128)(2,1)S(1)}, u32[]{:S(2)}) copy-start(bf16[688,1024]{1,0:T(8,128)(2,1)S(1)} %get-tuple-element.34.key_ref) | copy-start | bytes 4227076
  52.8 1.2 %copy-start.26 = (bf16[688,1024]{1,0:T(8,128)(2,1)}, bf16[688,1024]{1,0:T(8,128)(2,1)S(1)}, u32[]{:S(2)}) copy-start(bf16[688,1024]{1,0:T(8,128)(2,1)S(1)} %get-tuple-element.35.value_ref) | copy-start | bytes 4227076
  53.9 0.9 copy-start.30
  54.9 0.9 copy-start.32
  55.7 4.4 %copy-start.14 = (bf16[192,1024]{1,0:T(8,128)(2,1)S(1)}, bf16[192,1024]{1,0:T(8,128)(2,1)}, u32[]{:S(2)}) copy-start(bf16[192,1024]{1,0:T(8,128)(2,1)} %copy-done.12) | copy-start | bytes 1179652
  55.7 4.5 %copy-start.21 = (f32[16]{0:T(128)S(1)}, f32[16]{0:T(128)}, u32[]{:S(2)}) copy-start(f32[16]{0:T(128)} %sharp_ref.3) | copy-start | bytes 196
  55.7 4.5 %copy-start.29 = (f32[192,1024]{1,0:T(8,128)S(1)}, f32[192,1024]{1,0:T(8,128)}, u32[]{:S(2)}) copy-start(f32[192,1024]{1,0:T(8,128)} %copy-done.28) | copy-start | bytes 2359300
  55.7 45.9 %all-to-all-start = ((bf16[16,6,4,1024]{3,2,1,0:T(4,128)(2,1)}), bf16[16,6,4,1024]{3,2,1,0:T(4,128)(2,1)}, u32[]{:S(2)}, u32[]{:S(2)}) async-start(bf16[16,6,4,1024]{3,2,1,0:T(4,128)(2,1)} %copy-done.10), calls=%async_computation | async-start | bytes 1572864 | tf_op jit(solution)/shard_map/all_to_all | solution.py:423
  60.2 35.9 %slice-start = ((s8[6291456]{0:T(1024)(128)(4,1)}), s8[4194304]{0:T(1024)(128)(4,1)S(1)}, s32[]{:S(2)}) async-start(s8[6291456]{0:T(1024)(128)(4,1)} %bitcast.7), calls=%async_computation.1 | async-start | bytes 8388608
  60.2 2.0 %copy-start.23 = (bf16[4,2,384,512]{3,2,1,0:T(8,128)(2,1)S(1)}, bf16[4,2,384,512]{3,2,1,0:T(8,128)(2,1)}, u32[]{:S(2)}) copy-start(bf16[4,2,384,512]{3,2,1,0:T(8,128)(2,1)} %copy-done.22) | copy-start | bytes 9437188
  62.3 1.5 %copy-start.25 = (bf16[688,1024]{1,0:T(8,128)(2,1)S(1)}, bf16[688,1024]{1,0:T(8,128)(2,1)}, u32[]{:S(2)}) copy-start(bf16[688,1024]{1,0:T(8,128)(2,1)} %copy-done.24) | copy-start | bytes 4227076
  63.7 1.4 %copy-start.27 = (bf16[688,1024]{1,0:T(8,128)(2,1)S(1)}, bf16[688,1024]{1,0:T(8,128)(2,1)}, u32[]{:S(2)}) copy-start(bf16[688,1024]{1,0:T(8,128)(2,1)} %copy-done.26) | copy-start | bytes 4227076
  65.1 1.1 %copy-start.31 = (f32[192,1024]{1,0:T(8,128)S(1)}, f32[192,1024]{1,0:T(8,128)}, u32[]{:S(2)}) copy-start(f32[192,1024]{1,0:T(8,128)} %copy-done.30) | copy-start | bytes 2359300
  66.2 1.1 %copy-start.33 = (f32[192,1024]{1,0:T(8,128)S(1)}, f32[192,1024]{1,0:T(8,128)}, u32[]{:S(2)}) copy-start(f32[192,1024]{1,0:T(8,128)} %copy-done.32) | copy-start | bytes 2359300
  67.4 1.0 copy-start.35
  68.3 27.7 %slice-start.1 = ((s8[6291456]{0:T(1024)(128)(4,1)}), s8[2097152]{0:T(1024)(128)(4,1)S(1)}, s32[]{:S(2)}) async-start(s8[6291456]{0:T(1024)(128)(4,1)} %bitcast.7), calls=%async_computation.2 | async-start | bytes 4194304
  68.3 27.7 %copy-start.7 = (bf16[12,16,1024]{2,1,0:T(8,128)(2,1)S(1)}, bf16[12,16,1024]{2,1,0:T(8,128)(2,1)}, u32[]{:S(2)}) copy-start(bf16[12,16,1024]{2,1,0:T(8,128)(2,1)} %param.13) | copy-start | bytes 1179652
  68.4 27.7 %copy-start.15 = (bf16[2,192,224]{2,1,0:T(8,128)(2,1)S(1)}, bf16[2,192,224]{2,1,0:T(8,128)(2,1)}, u32[]{:S(2)}) copy-start(bf16[2,192,224]{2,1,0:T(8,128)(2,1)} %constant.11.clone.unsel_ref) | copy-start | bytes 516100
  77.7 18.3 %collective-permute-start.5 = (bf16[2,96,1024]{2,1,0:T(8,128)(2,1)S(1)}, bf16[2,96,1024]{2,1,0:T(8,128)(2,1)S(1)}, u32[]{:S(2)}, u32[]{:S(2)}) collective-permute-start(bf16[2,96,1024]{2,1,0:T(8,128)(2,1)S(1)} %get-tuple-element.41), channel_id=1, source_target_pairs={{0,1},{1,0},{2,3},{3,2},{4,5},{5,4},{6,7},{7,6},{8,9},{9,8},{10,11... | collective-permute-start | bytes 1179656 | tf_op jit(solution)/shard_map/ppermute | solution.py:363
  77.9 18.2 %collective-permute-start.6 = (bf16[2,72,1024]{2,1,0:T(8,128)(2,1)S(1)}, bf16[2,72,1024]{2,1,0:T(8,128)(2,1)S(1)}, u32[]{:S(2)}, u32[]{:S(2)}) collective-permute-start(bf16[2,72,1024]{2,1,0:T(8,128)(2,1)S(1)} %get-tuple-element.42), channel_id=1, source_target_pairs={{0,2},{2,4},{4,6},{6,8},{8,10},{10,12},{12,14},{14,16},{16,18},{18... | collective-permute-start | bytes 884744 | tf_op jit(solution)/shard_map/ppermute | solution.py:361
  78.1 18.0 %collective-permute-start.7 = (bf16[2,72,1024]{2,1,0:T(8,128)(2,1)S(1)}, bf16[2,72,1024]{2,1,0:T(8,128)(2,1)S(1)}, u32[]{:S(2)}, u32[]{:S(2)}) collective-permute-start(bf16[2,72,1024]{2,1,0:T(8,128)(2,1)S(1)} %get-tuple-element.43), channel_id=1, source_target_pairs={{2,0},{4,2},{6,4},{8,6},{10,8},{12,10},{14,12},{16,14},{18,16},{20... | collective-permute-start | bytes 884744 | tf_op jit(solution)/shard_map/ppermute | solution.py:362
  82.3 10.3 %collective-permute-start.8 = (bf16[2,40,1024]{2,1,0:T(8,128)(2,1)S(1)}, bf16[2,40,1024]{2,1,0:T(8,128)(2,1)S(1)}, u32[]{:S(2)}, u32[]{:S(2)}) collective-permute-start(bf16[2,40,1024]{2,1,0:T(8,128)(2,1)S(1)} %get-tuple-element.44), channel_id=1, source_target_pairs={{0,3},{1,2},{2,5},{3,4},{4,7},{5,6},{6,9},{7,8},{8,11},{9,10},{10,... | collective-permute-start | bytes 491528 | tf_op jit(solution)/shard_map/ppermute | solution.py:364
  82.3 13.7 %collective-permute-start.9 = (bf16[2,40,1024]{2,1,0:T(8,128)(2,1)S(1)}, bf16[2,40,1024]{2,1,0:T(8,128)(2,1)S(1)}, u32[]{:S(2)}, u32[]{:S(2)}) collective-permute-start(bf16[2,40,1024]{2,1,0:T(8,128)(2,1)S(1)} %get-tuple-element.45), channel_id=1, source_target_pairs={{2,1},{3,0},{4,3},{5,2},{6,5},{7,4},{8,7},{9,6},{10,9},{11,8},{12,... | collective-permute-start | bytes 491528 | tf_op jit(solution)/shard_map/ppermute | solution.py:365
  (2 other events, 1.3 us)
where the time goes:
time: 105 us; the launch traced here: 104 us
  Pallas kernels  35 us (33%)
  local copies, waits for them, and re-layouts  32.6 us (31%)
  starting transfers between devices  27.1 us (26%)
  waiting for transfers between devices  8.41 us (8%)
    unnamed x80, local copies, waits for them, and re-layouts  32.6 us
    pallas_call x1, Pallas kernels, per_device(): call(forward_kernel, STEPS, [SMEM(), SMEM(), whole(TOKENS, D), whole(BAND...  11.5 us
    ppermute x2, starting transfers between devices, exchange(): lax.ppermute(corner_backward, ('lon', 'lat'), across(left))  10.7 us
    pallas_call x1, Pallas kernels, per_device(): call(backward_kernel, STEPS, [SMEM(), pl.BlockSpec((1, 2, STACK, SPAN), l...  9.33 us
    ppermute x2, starting transfers between devices, exchange(): lax.ppermute(backward, 'lon', left)  9.24 us
    pallas_call x1, Pallas kernels, per_device(): call(own_kernel, STEPS, [SMEM(), whole(TOKENS, D), by_lat(BAND, D), whole...  7.33 us
    pallas_call x1, Pallas kernels, per_device(): call(final_kernel, STEPS, [whole(TOKENS, D), whole(TOKENS, D), whole(1, D...  5.51 us
    ppermute x2, waiting for transfers between devices, exchange(): lax.ppermute(corner_forward, ('lon', 'lat'), across(right))  5 us
  transfers between devices with their start and end apart: 11, of which 2 were waited for; matrix products, arithmetic and copies ran while one was open for 0% of the time, Pallas kernels for 21%

commit v1 on v0

v1 whole, which is shorter than its diff:
```python
import functools

import jax
import jax.numpy as jnp
import numpy as np
from jax import lax
from jax.experimental import pallas as pl
from jax.experimental.pallas import tpu as pltpu
from jax.sharding import PartitionSpec as P

HEADS = 16
HALO = 6
ROWS = 12
COLS = 16
SEG = 4
D = 1024
HEAD_DIM = D // HEADS
TOKENS = ROWS * COLS
HALF = TOKENS // 2
BAND = HALO * COLS
SIDE = ROWS * HALO
CORNER = 40
QUAD = 256
QUAD_HEADS = QUAD // HEAD_DIM
STEPS = D // QUAD
STACK = QUAD_HEADS * HALF
PAD_SIDE = BAND + 2 * CORNER
MIDDLE = TOKENS + 2 * SIDE
SPAN = PAD_SIDE + MIDDLE
KEYS = SPAN + PAD_SIDE
QUERIES = SPAN
HALO_ROWS = 2 * PAD_SIDE + 2 * SIDE - BAND
HALO_QUERIES = PAD_SIDE + 2 * SIDE
EDGE = SIDE + CORNER
STATS = 128
VMEM = 62 * 1024 * 1024
BF = jnp.bfloat16
F32 = jnp.float32


def dot(a, b):
    return jnp.dot(a, b, preferred_element_type=F32)


def dot_nt(a, b):
    return lax.dot_general(a, b, (((1,), (1,)), ((), ())), preferred_element_type=F32)


def dot_tn(a, b):
    return lax.dot_general(a, b, (((0,), (0,)), ((), ())), preferred_element_type=F32)


def first_column(side, parity):
    return COLS - HALO if side == parity else 0


def selection_table():
    table = np.zeros((4, 2 * EDGE + 2 * CORNER, TOKENS + BAND), np.float32)
    for lat in range(2):
        for parity in range(2):
            for side in range(2):
                first, base = first_column(side, parity), side * EDGE
                picks = table[2 * lat + parity]
                for c in range(HALO):
                    for r in range(ROWS):
                        picks[base + r * HALO + c, r * COLS + first + c] = 1
                    for i in range(HALO):
                        picks[base + SIDE + i * HALO + c, TOKENS + i * COLS + first + c] = 1
                        row = i + HALO * (1 - lat)
                        picks[2 * EDGE + side * CORNER + i * HALO + c, row * COLS + first + c] = 1
    return table


def key_table():
    table = np.full((4, 8, KEYS), 1000, np.int32)
    table[:, 2] = -1
    for lat in range(2):
        for parity in range(2):
            picks = table[2 * lat + parity]
            low = {"lat": ROWS if lat == 0 else -HALO, "own": 0, "rim": -HALO if lat == 0 else ROWS}

            def put(at, count, width, first_col, kind):
                for k in range(count * width):
                    i, c = divmod(k, width)
                    picks[0, at + k] = low[kind] + i
                    picks[1, at + k] = first_col + c
                    if kind == "rim":
                        picks[2, at + k] = i

            put(0, HALO, COLS, 0, "lat")
            put(PAD_SIDE, ROWS, COLS, 0, "own")
            put(SPAN, HALO, COLS, 0, "rim")
            for side in range(2):
                col = COLS if side == parity else -HALO
                put(BAND + side * CORNER, HALO, HALO, col, "lat")
                put(PAD_SIDE + TOKENS + side * SIDE, ROWS, HALO, col, "own")
                put(SPAN + BAND + side * CORNER, HALO, HALO, col, "rim")
    return table


def head_mask(h, dtype):
    lane = lax.broadcasted_iota(jnp.int32, (1, QUAD), 1)
    return jnp.where(lane // HEAD_DIM == h, 1.0, 0.0).astype(dtype)


def head_mean(values):
    a = lax.broadcasted_iota(jnp.int32, (QUAD, QUAD), 0) // HEAD_DIM
    b = lax.broadcasted_iota(jnp.int32, (QUAD, QUAD), 1) // HEAD_DIM
    block = jnp.where(a == b, 1.0 / HEAD_DIM, 0.0).astype(BF)
    return dot(values.astype(BF), block)


def unit(raw):
    return raw * lax.rsqrt(head_mean(raw * raw) + 1e-06)


def unit_back(raw, grad):
    inverse = lax.rsqrt(head_mean(raw * raw) + 1e-06)
    value = raw * inverse
    return inverse * (grad - value * head_mean(value * grad))


def normed(tokens, gain):
    tokens = tokens.astype(F32)
    return tokens * lax.rsqrt(jnp.mean(tokens * tokens, axis=-1, keepdims=True) + 1e-05) * gain


def multiplier(sharp_ref, j):
    out = jnp.zeros((1, QUAD), F32)
    for h in range(QUAD_HEADS):
        out = out + head_mask(h, F32) * (sharp_ref[j * QUAD_HEADS + h] / HEAD_DIM)
    return out


def stacked(block):
    return jnp.concatenate([block * head_mask(h, BF) for h in range(QUAD_HEADS)], axis=0)


def unstacked(stack):
    out = stack[:HALF] * head_mask(0, F32)
    for h in range(1, QUAD_HEADS):
        out = out + stack[h * HALF : (h + 1) * HALF] * head_mask(h, F32)
    return out


def repeated(block):
    return jnp.concatenate([block] * QUAD_HEADS, axis=0)


def stat_lane(lane):
    return jnp.where(lax.broadcasted_iota(jnp.int32, (1, STATS), 1) == lane, 1.0, 0.0)


def half_start(lat, half):
    return pl.multiple_of(HALF * ((1 - lat) if half == 0 else lat), 16)


def near_mask(mask_ref, tab_ref, flag_ref, lat):
    rows, cols, place = tab_ref[0, 0:1], tab_ref[0, 1:2], tab_ref[0, 2:3]
    keep = jnp.where(place < 0, 1.0, 0.0)
    for i in range(HALO):
        keep = keep + jnp.where(place == i, flag_ref[lat, i].astype(F32), 0.0)
    for half in range(2):
        at = half * PAD_SIDE
        token = lax.broadcasted_iota(jnp.int32, (HALF, SPAN), 0) + half_start(lat, half)
        near = (jnp.abs(rows[:, at : at + SPAN] - token // COLS) <= HALO) & (
            jnp.abs(cols[:, at : at + SPAN] - token % COLS) <= HALO
        )
        mask_ref[half] = jnp.where(near, keep[:, at : at + SPAN], 0.0)


def lay_keys(ref, own, halo):
    ref[:PAD_SIDE] = halo[:PAD_SIDE]
    ref[PAD_SIDE : PAD_SIDE + TOKENS] = own[:TOKENS]
    ref[PAD_SIDE + TOKENS : SPAN] = halo[PAD_SIDE:HALO_QUERIES]
    ref[SPAN : SPAN + BAND] = own[TOKENS:]
    ref[SPAN + BAND :] = halo[HALO_QUERIES:]


class Copies:
    def __init__(self, sems):
        self.sems, self.used = sems, 0

    def start(self, source, target):
        copy = pltpu.make_async_copy(source, target, self.sems.at[self.used])
        self.used += 1
        copy.start()
        return copy

    def start_steps(self, pair):
        base = self.used
        self.used += STEPS
        for j in range(STEPS):
            pltpu.make_async_copy(*pair(j), self.sems.at[base + j]).start()
        return lambda j: pltpu.make_async_copy(*pair(j), self.sems.at[base + j]).wait()


def lane_block(at, j):
    return pl.ds(pl.multiple_of((at + j) * QUAD, QUAD), QUAD)


def pack_kernel(
    place_ref, x_hbm, up_hbm, rim_hbm, sel_hbm, edge_a_hbm, edge_b_hbm, band_hbm, corner_a_hbm, corner_b_hbm,
    x_ref, up_ref, rim_ref, sel_ref, edge_a_ref, edge_b_ref, corner_a_ref, corner_b_ref, sems,
):
    lat = place_ref[0]
    copies = Copies(sems)
    loads = [
        copies.start(x_hbm, x_ref),
        copies.start(rim_hbm.at[lat], rim_ref),
        copies.start(sel_hbm.at[2 * lat + place_ref[1]], sel_ref),
        copies.start(up_hbm, up_ref),
    ]
    for copy in loads:
        copy.wait()
    piece = pl.ds(half_start(lat, 0), BAND)
    stores = [
        copies.start(x_ref.at[piece], band_hbm.at[pl.ds(0, BAND)]),
        copies.start(up_ref.at[piece], band_hbm.at[pl.ds(BAND, BAND)]),
    ]
    picks = sel_ref[...]
    features = dot(picks, jnp.concatenate([x_ref[...], rim_ref[...]], axis=0))
    grads = dot(picks[:, :TOKENS], up_ref[...])
    for side, (ref, hbm) in enumerate(((edge_a_ref, edge_a_hbm), (edge_b_ref, edge_b_hbm))):
        at = side * EDGE
        ref[...] = jnp.concatenate([features[at : at + EDGE], grads[at : at + SIDE]], axis=0).astype(BF)
        stores.append(copies.start(ref, hbm))
    for side, (ref, hbm) in enumerate(((corner_a_ref, corner_a_hbm), (corner_b_ref, corner_b_hbm))):
        at = 2 * EDGE + side * CORNER
        ref[...] = jnp.concatenate([features[at : at + CORNER], grads[at : at + CORNER]], axis=0).astype(BF)
        stores.append(copies.start(ref, hbm))
    for copy in stores:
        copy.wait()


def own_kernel(
    place_ref, sharp_ref, x_ref, rim_ref, up_ref, gain_ref, wq_ref, wk_ref, wv_ref, wo_ref,
    qhat_ref, rawq_ref, rawk_ref, kv_ref, dout_ref, xn_ref,
):
    j = pl.program_id(0)

    @pl.when(j == 0)
    def _():
        xn_ref[:TOKENS] = normed(x_ref[...], gain_ref[...]).astype(BF)
        xn_ref[TOKENS:] = normed(rim_ref[0], gain_ref[...]).astype(BF)

    xn = xn_ref[...]
    raw_q = dot(xn[:TOKENS], wq_ref[...])
    rawq_ref[0] = raw_q
    qhat_ref[0] = (unit(raw_q) * multiplier(sharp_ref, j)).astype(BF)
    raw_k = dot(xn, wk_ref[...])
    rawk_ref[0] = raw_k[:TOKENS]
    kv_ref[0, 0] = unit(raw_k).astype(BF)
    kv_ref[0, 1] = dot(xn, wv_ref[...]).astype(BF)
    dout_ref[0] = dot_nt(up_ref[...], wo_ref[...]).astype(BF)


def forward_kernel(
    place_ref, flag_ref, band_hbm, edge_a_hbm, edge_b_hbm, corner_a_hbm, corner_b_hbm, gain_hbm, tab_hbm, sel_hbm, w3_hbm,
    qhat_hbm, kv_hbm, dout_hbm,
    halo_hbm, mixed_hbm, stat_hbm, stat_a_hbm, stat_b_hbm, stat_band_hbm, stat_ca_hbm, stat_cb_hbm,
    band_ref, edge_a_ref, edge_b_ref, corner_a_ref, corner_b_ref, gain_ref, tab_ref, sel_ref, wk_ref, wv_ref,
    qhat_ref, kv_ref, dout_ref, halo_ref, mixed_ref, stat_ref, picked_ref, xn_ref, mask_ref, key_ref, value_ref, sems,
):
    lat = place_ref[0]
    spot = 2 * lat + place_ref[1]
    copies = Copies(sems)
    first = [
        copies.start(gain_hbm, gain_ref),
        copies.start(band_hbm.at[pl.ds(0, BAND)], band_ref),
        copies.start(corner_a_hbm, corner_a_ref),
        copies.start(corner_b_hbm, corner_b_ref),
        copies.start(edge_a_hbm.at[pl.ds(0, EDGE)], edge_a_ref),
        copies.start(edge_b_hbm.at[pl.ds(0, EDGE)], edge_b_ref),
        copies.start(tab_hbm.at[spot], tab_ref.at[0]),
    ]
    weight_copies = lambda j: [
        (w3_hbm.at[:, lane_block(STEPS, j)], wk_ref.at[j], 2 * j),
        (w3_hbm.at[:, lane_block(2 * STEPS, j)], wv_ref.at[j], 2 * j + 1),
    ]
    at_weights = copies.used
    copies.used += 2 * STEPS

    def start_weights(j):
        for source, target, k in weight_copies(j):
            pltpu.make_async_copy(source, target, sems.at[at_weights + k]).start()

    start_weights(0)
    second = [copies.start(qhat_hbm, qhat_ref), copies.start(kv_hbm, kv_ref), copies.start(dout_hbm, dout_ref)]
    for j in range(1, STEPS):
        start_weights(j)
    third = copies.start(sel_hbm.at[spot], sel_ref)
    for copy in first:
        copy.wait()
    gain = gain_ref[...]
    edge_a, edge_b = normed(edge_a_ref[...], gain), normed(edge_b_ref[...], gain)
    pieces = [normed(band_ref[...], gain), normed(corner_a_ref[...], gain)[:CORNER], normed(corner_b_ref[...], gain)[:CORNER]]
    pieces += [edge_a[:SIDE], edge_b[:SIDE], edge_a[SIDE:], edge_b[SIDE:]]
    xn_ref[...] = jnp.concatenate(pieces, axis=0).astype(BF)
    stat_ref[...] = jnp.zeros_like(stat_ref)
    near_mask(mask_ref, tab_ref, flag_ref, lat)
    base = copies.used

    def store_halo(j):
        return pltpu.make_async_copy(halo_ref.at[j], halo_hbm.at[j], sems.at[base + j])

    def store_mixed(j):
        return pltpu.make_async_copy(mixed_ref.at[j], mixed_hbm.at[:, lane_block(0, j)], sems.at[base + STEPS + j])

    def step(j, carry):
        for source, target, k in weight_copies(j):
            pltpu.make_async_copy(source, target, sems.at[at_weights + k]).wait()
        xn = xn_ref[...]
        halo_k = unit(dot(xn, wk_ref[j])).astype(BF)
        halo_v = dot(xn, wv_ref[j]).astype(BF)
        halo_ref[j, 0] = halo_k
        halo_ref[j, 1] = halo_v
        store_halo(j).start()

        @pl.when(j == 0)
        def _():
            for copy in second:
                copy.wait()

        lay_keys(key_ref, kv_ref[j, 0], halo_k)
        lay_keys(value_ref, kv_ref[j, 1], halo_v)
        for half in range(2):
            at, piece = half * PAD_SIDE, pl.ds(half_start(lat, half), HALF)
            scores = dot_nt(stacked(qhat_ref[j, piece, :]), key_ref[at : at + SPAN])
            weights = jnp.exp(scores) * repeated(mask_ref[half])
            inverse = 1.0 / jnp.sum(weights, axis=-1, keepdims=True)
            mixed = unstacked(dot(weights.astype(BF), value_ref[at : at + SPAN]) * inverse)
            mixed_ref[j, piece, :] = mixed.astype(BF)
            inner = dout_ref[j, piece, :].astype(F32) * mixed
            stat = stat_ref[piece, :]
            for h in range(QUAD_HEADS):
                head = j * QUAD_HEADS + h
                stat = stat + stat_lane(head) * inverse[h * HALF : (h + 1) * HALF]
                stat = stat + stat_lane(HEADS + head) * jnp.sum(inner * head_mask(h, F32), axis=-1, keepdims=True)
            stat_ref[piece, :] = stat
        store_mixed(j).start()
        return carry

    lax.fori_loop(0, STEPS, step, 0)
    copies.used = base + 2 * STEPS
    third.wait()
    stat = stat_ref[...]
    high = stat.astype(BF)
    low = (stat - high.astype(F32)).astype(BF)
    picks = sel_ref[:, :TOKENS]
    picked_ref[...] = dot(picks, high) + dot(picks, low)
    last = [
        copies.start(stat_ref, stat_hbm),
        copies.start(picked_ref.at[pl.ds(0, SIDE)], stat_a_hbm),
        copies.start(picked_ref.at[pl.ds(EDGE, SIDE)], stat_b_hbm),
        copies.start(stat_ref.at[pl.ds(half_start(lat, 0), BAND)], stat_band_hbm),
        copies.start(picked_ref.at[pl.ds(2 * EDGE, CORNER)], stat_ca_hbm),
        copies.start(picked_ref.at[pl.ds(2 * EDGE + CORNER, CORNER)], stat_cb_hbm),
    ]
    for j in range(STEPS):
        store_halo(j).wait()
        store_mixed(j).wait()
    for copy in last:
        copy.wait()


def output_kernel(place_ref, owner_ref, x_ref, mixed_ref, wo_ref, going_ref, acc_ref, count_ref):
    acc_ref[...] = x_ref[...].astype(F32) + dot(mixed_ref[...], wo_ref[...])
    going_ref[...] = jnp.zeros_like(going_ref)
    for o in range(going_ref.shape[0]):
        count_ref[o] = 0
    for s in range(TOKENS // SEG):
        owner = owner_ref[s // (COLS // SEG), s % (COLS // SEG)]
        slot = count_ref[owner]
        count_ref[owner] = slot + 1
        going_ref[owner, slot] = acc_ref[s * SEG : (s + 1) * SEG, :].astype(BF)


def backward_kernel(
    place_ref, sharp_ref, flag_ref, x_ref, up_ref, band_ref, edge_a_ref, edge_b_ref, corner_a_ref, corner_b_ref, gain_ref,
    tab_ref, wq_ref, wk_ref, wv_ref, wo_ref, qhat_ref, kv_ref, halo_ref, dout_ref, rawq_ref, rawk_ref,
    stat_ref, stat_a_ref, stat_b_ref, stat_band_ref, stat_ca_ref, stat_cb_ref,
    out_ref,
    xn_ref, upn_ref, mask_ref, acc_ref, key_ref, value_ref, query_ref, grad_ref, row_ref, dq_ref, dk_ref, dv_ref,
):
    j = pl.program_id(0)
    lat = place_ref[0]

    @pl.when(j == 0)
    def _():
        gain = gain_ref[...]
        band, edge_a, edge_b = (ref[...].astype(F32) for ref in (band_ref, edge_a_ref, edge_b_ref))
        corner_a, corner_b = (ref[...].astype(F32) for ref in (corner_a_ref, corner_b_ref))
        pieces = [band[:BAND], corner_a[:CORNER], corner_b[:CORNER], edge_a[:SIDE], edge_b[:SIDE]]
        xn_ref[...] = normed(jnp.concatenate(pieces, axis=0), gain).astype(BF)
        pieces = [band[BAND:], corner_a[CORNER:], corner_b[CORNER:], edge_a[EDGE:], edge_b[EDGE:]]
        upn_ref[...] = jnp.concatenate(pieces, axis=0).astype(BF)
        pieces = [stat_band_ref, stat_ca_ref, stat_cb_ref, stat_ref, stat_a_ref, stat_b_ref]
        row_ref[...] = jnp.concatenate([ref[...] for ref in pieces], axis=0).T
        near_mask(mask_ref, tab_ref, flag_ref, lat)

    lay_keys(key_ref, kv_ref[0, 0], halo_ref[0, 0])
    lay_keys(value_ref, kv_ref[0, 1], halo_ref[0, 1])
    halo_q = (unit(dot(xn_ref[...], wq_ref[...])) * multiplier(sharp_ref, j)).astype(BF)
    halo_g = dot_nt(upn_ref[...], wo_ref[...]).astype(BF)
    for ref, own, halo in ((query_ref, qhat_ref, halo_q), (grad_ref, dout_ref, halo_g)):
        ref[:PAD_SIDE] = halo[:PAD_SIDE]
        ref[PAD_SIDE : PAD_SIDE + TOKENS] = own[0]
        ref[PAD_SIDE + TOKENS :] = halo[PAD_SIDE:]

    for half in range(2):
        at, piece = half * PAD_SIDE, pl.ds(half_start(lat, half), HALF)
        stat = stat_ref[piece, :]
        columns = [
            jnp.concatenate(
                [jnp.sum(stat * stat_lane(base + j * QUAD_HEADS + h), axis=-1, keepdims=True) for h in range(QUAD_HEADS)],
                axis=0,
            )
            for base in (0, HEADS)
        ]
        keys = key_ref[at : at + SPAN]
        scores = dot_nt(stacked(qhat_ref[0, piece, :]), keys)
        probs = jnp.exp(scores) * repeated(mask_ref[half]) * columns[0]
        grad_probs = dot_nt(stacked(dout_ref[0, piece, :]), value_ref[at : at + SPAN])
        grad_scores = probs * (grad_probs - columns[1])
        dq_ref[piece, :] = unstacked(dot(grad_scores.astype(BF), keys))

    for half in range(2):
        at, piece = half * PAD_SIDE, pl.ds(half_start(lat, half), HALF)
        width = SPAN - at
        queries, grads = query_ref[at:], grad_ref[at:]
        rows = [
            jnp.concatenate(
                [
                    jnp.broadcast_to(row_ref[pl.ds(base + j * QUAD_HEADS + h, 1), at:], (HALF, width))
                    for h in range(QUAD_HEADS)
                ],
                axis=0,
            )
            for base in (0, HEADS)
        ]
        scores = dot_nt(stacked(kv_ref[0, 0, piece, :]), queries)
        probs = jnp.exp(scores) * repeated(mask_ref[half, :, :width]) * rows[0]
        grad_probs = dot_nt(stacked(kv_ref[0, 1, piece, :]), grads)
        grad_scores = probs * (grad_probs - rows[1])
        dk_ref[piece, :] = unstacked(dot(grad_scores.astype(BF), queries))
        dv_ref[piece, :] = unstacked(dot(probs.astype(BF), grads))

    grad_q = unit_back(rawq_ref[0], dq_ref[...] * multiplier(sharp_ref, j)).astype(BF)
    grad_k = unit_back(rawk_ref[0], dk_ref[...]).astype(BF)
    part = dot_nt(grad_q, wq_ref[...]) + dot_nt(grad_k, wk_ref[...]) + dot_nt(dv_ref[...].astype(BF), wv_ref[...])

    @pl.when(j == 0)
    def _():
        acc_ref[...] = part

    @pl.when(j > 0)
    def _():
        acc_ref[...] += part

    @pl.when(j == STEPS - 1)
    def _():
        tokens = x_ref[...].astype(F32)
        inverse = lax.rsqrt(jnp.mean(tokens * tokens, axis=-1, keepdims=True) + 1e-05)
        grad = acc_ref[...] * gain_ref[...]
        value = tokens * inverse
        back = inverse * (grad - value * jnp.mean(value * grad, axis=-1, keepdims=True))
        out_ref[...] = (up_ref[...].astype(F32) + back).astype(BF)


SMEM = functools.partial(pl.BlockSpec, memory_space=pltpu.SMEM)
HBM = functools.partial(pl.BlockSpec, memory_space=pl.ANY)


def whole(*shape):
    return pl.BlockSpec(shape, lambda j, place: (0,) * len(shape))


def by_lat(*shape):
    return pl.BlockSpec((1,) + shape, lambda j, place: (place[0],) + (0,) * len(shape))


def by_place(*shape):
    return pl.BlockSpec((1,) + shape, lambda j, place: (2 * place[0] + place[1],) + (0,) * len(shape))


def lanes(*shape, at=0):
    return pl.BlockSpec(shape + (QUAD,), lambda j, place: (0,) * len(shape) + (at + j,))


def rows_of(width):
    return pl.BlockSpec((QUAD, width), lambda j, place: (j, 0))


def steps_of(*shape):
    return pl.BlockSpec((1,) + shape + (QUAD,), lambda j, place: (j,) + (0,) * (len(shape) + 1))


def call(kernel, steps, in_specs, out_specs, out_shape, scratch=(), flops=0, name=None):
    return pl.pallas_call(
        kernel,
        grid_spec=pltpu.PrefetchScalarGridSpec(
            num_scalar_prefetch=1, grid=(steps,), in_specs=in_specs, out_specs=out_specs, scratch_shapes=list(scratch)
        ),
        out_shape=out_shape,
        compiler_params=pltpu.CompilerParams(vmem_limit_bytes=VMEM, dimension_semantics=("arbitrary",)),
        cost_estimate=pl.CostEstimate(flops=flops, bytes_accessed=8 << 20, transcendentals=0),
        name=name,
    )


def like(*shape, dtype=BF):
    return jax.ShapeDtypeStruct(shape, dtype)


def exchange(count, edge_a, edge_b, band, corner_a, corner_b):
    pairs_a = [(i, i + 1 - 2 * (i % 2)) for i in range(count)]
    pairs_b = [(i, (i - 1 + 2 * (i % 2)) % count) for i in range(count)]

    def across(pairs):
        return [(2 * a + lat, 2 * b + 1 - lat) for a, b in pairs for lat in range(2)]

    return (
        lax.ppermute(edge_a, "lon", pairs_a),
        lax.ppermute(edge_b, "lon", pairs_b),
        lax.ppermute(band, "lat", [(0, 1), (1, 0)]),
        lax.ppermute(corner_a, ("lon", "lat"), across(pairs_a)),
        lax.ppermute(corner_b, ("lon", "lat"), across(pairs_b)),
    )


def per_device(
    slab_features, upstream_gradient, rim_feature_rows, rim_presence_flags, feature_rescaling_coefficients,
    triple_projection_matrix, final_projection_matrix, score_sharpness, column_group_decoder_longitude,
):
    count = lax.axis_size("lon")
    cap = max(2, (2 * (TOKENS // SEG) + count - 1) // count)
    place = jnp.stack([lax.axis_index("lat"), lax.axis_index("lon") % 2]).astype(jnp.int32)
    x = slab_features.reshape(TOKENS, D)
    up = upstream_gradient.reshape(TOKENS, D)
    rim = rim_feature_rows.reshape(2, BAND, D)
    gain = feature_rescaling_coefficients.reshape(1, D)
    w3, wo = triple_projection_matrix, final_projection_matrix
    table = selection_table()
    selection = jnp.asarray(table, BF)
    keys = jnp.asarray(key_table())
    flags = rim_presence_flags

    sizes = (EDGE + SIDE, EDGE + SIDE, 2 * BAND, 2 * CORNER, 2 * CORNER)
    packed = call(
        pack_kernel, 1, [HBM()] * 4, [HBM()] * 5,
        [like(size, D) for size in sizes],
        [pltpu.VMEM((TOKENS, D), BF), pltpu.VMEM((TOKENS, D), BF), pltpu.VMEM((BAND, D), BF), pltpu.VMEM(table.shape[1:], BF)]
        + [pltpu.VMEM((size, D), BF) for size in sizes if size != 2 * BAND] + [pltpu.SemaphoreType.DMA((10,))],
        name="edge_tokens",
    )(place, x, up, rim, selection)
    edge_a, edge_b, band, corner_a, corner_b = exchange(count, *packed)

    qhat, rawq, rawk, kv, dout = call(
        own_kernel, STEPS,
        [SMEM(), whole(TOKENS, D), by_lat(BAND, D), whole(TOKENS, D), whole(1, D),
         lanes(D), lanes(D, at=STEPS), lanes(D, at=2 * STEPS), rows_of(D)],
        [steps_of(TOKENS), steps_of(TOKENS), steps_of(TOKENS), steps_of(2, TOKENS + BAND), steps_of(TOKENS)],
        [like(STEPS, TOKENS, QUAD), like(STEPS, TOKENS, QUAD, dtype=F32), like(STEPS, TOKENS, QUAD, dtype=F32),
         like(STEPS, 2, TOKENS + BAND, QUAD), like(STEPS, TOKENS, QUAD)],
        [pltpu.VMEM((TOKENS + BAND, D), BF)],
        flops=2 * 1024 * 1024 * (192 * 2 + 288 * 2),
        name="own_projections",
    )(place, score_sharpness, x, rim, up, gain, w3, w3, w3, wo)

    stat_sizes = (TOKENS, SIDE, SIDE, BAND, CORNER, CORNER)
    halo_kv, mixed, stat, *edges = call(
        forward_kernel, 1,
        [SMEM()] + [HBM()] * 12, [HBM()] * 8,
        [like(STEPS, 2, HALO_ROWS, QUAD), like(TOKENS, D)] + [like(size, STATS, dtype=F32) for size in stat_sizes],
        [pltpu.VMEM((BAND, D), BF), pltpu.VMEM((EDGE, D), BF), pltpu.VMEM((EDGE, D), BF), pltpu.VMEM((2 * CORNER, D), BF),
         pltpu.VMEM((2 * CORNER, D), BF), pltpu.VMEM((1, D), F32), pltpu.VMEM((1, 8, KEYS), jnp.int32),
         pltpu.VMEM(table.shape[1:], BF), pltpu.VMEM((STEPS, D, QUAD), BF), pltpu.VMEM((STEPS, D, QUAD), BF),
         pltpu.VMEM((STEPS, TOKENS, QUAD), BF), pltpu.VMEM((STEPS, 2, TOKENS + BAND, QUAD), BF),
         pltpu.VMEM((STEPS, TOKENS, QUAD), BF), pltpu.VMEM((STEPS, 2, HALO_ROWS, QUAD), BF),
         pltpu.VMEM((STEPS, TOKENS, QUAD), BF), pltpu.VMEM((TOKENS, STATS), F32), pltpu.VMEM((table.shape[1], STATS), F32),
         pltpu.VMEM((HALO_ROWS, D), BF), pltpu.VMEM((2, HALF, SPAN), F32), pltpu.VMEM((KEYS, QUAD), BF),
         pltpu.VMEM((KEYS, QUAD), BF), pltpu.SemaphoreType.DMA((33,))],
        flops=2 * 1024 * 1024 * 2000,
        name="attention_forward",
    )(place, flags, band, edge_a, edge_b, corner_a, corner_b, gain, keys, selection, w3, qhat, kv, dout)
    stat_a, stat_b, stat_band, stat_ca, stat_cb = exchange(count, *edges)

    going = call(
        output_kernel, 1,
        [SMEM(), whole(TOKENS, D), whole(TOKENS, D), whole(D, D)], whole(count, cap, SEG, D), like(count, cap, SEG, D),
        [pltpu.VMEM((TOKENS, D), F32), pltpu.SMEM((count,), jnp.int32)],
        flops=2 * 1024 * 1024 * 200,
        name="output_segments",
    )(place, column_group_decoder_longitude, x, mixed, wo)
    going, stat_a, stat_b, stat_band, stat_ca, stat_cb = lax.optimization_barrier(
        (going, stat_a, stat_b, stat_band, stat_ca, stat_cb)
    )
    arrived = lax.all_to_all(going, "lon", split_axis=0, concat_axis=0, tiled=True)

    input_grad = call(
        backward_kernel, STEPS,
        [SMEM(), SMEM(), whole(TOKENS, D), whole(TOKENS, D), whole(2 * BAND, D), whole(EDGE + SIDE, D), whole(EDGE + SIDE, D),
         whole(2 * CORNER, D), whole(2 * CORNER, D), whole(1, D), by_place(8, KEYS), lanes(D), lanes(D, at=STEPS),
         lanes(D, at=2 * STEPS), rows_of(D), steps_of(TOKENS), steps_of(2, TOKENS + BAND), steps_of(2, HALO_ROWS),
         steps_of(TOKENS), steps_of(TOKENS), steps_of(TOKENS)] + [whole(size, STATS) for size in stat_sizes],
        whole(TOKENS, D),
        like(TOKENS, D),
        [pltpu.VMEM((HALO_QUERIES, D), BF), pltpu.VMEM((HALO_QUERIES, D), BF), pltpu.VMEM((2, HALF, SPAN), F32),
         pltpu.VMEM((TOKENS, D), F32), pltpu.VMEM((KEYS, QUAD), BF), pltpu.VMEM((KEYS, QUAD), BF),
         pltpu.VMEM((QUERIES, QUAD), BF), pltpu.VMEM((QUERIES, QUAD), BF), pltpu.VMEM((STATS, QUERIES), F32),
         pltpu.VMEM((TOKENS, QUAD), F32), pltpu.VMEM((TOKENS, QUAD), F32), pltpu.VMEM((TOKENS, QUAD), F32)],
        flops=2 * 1024 * 1024 * 4000,
        name="attention_backward",
    )(place, score_sharpness, flags, x, up, band, edge_a, edge_b, corner_a, corner_b, gain, keys, w3, w3, w3, wo,
      qhat, kv, halo_kv, dout, rawq, rawk, stat, stat_a, stat_b, stat_band, stat_ca, stat_cb)
    return (
        arrived.reshape(1, 1, count, cap, SEG, D),
        input_grad.reshape(ROWS, COLS, D),
    )


def solution(mesh):
    return jax.shard_map(
        per_device,
        mesh=mesh,
        in_specs=(
            P("lat", "lon", None),
            P("lat", "lon", None),
            P(None, None, "lon", None),
            P(),
            P(),
            P(),
            P(),
            P(),
            P("lat", "lon"),
        ),
        out_specs=(P("lat", "lon", None, None, None, None), P("lat", "lon", None)),
        check_vma=False,
    )
```

time: 105 us -> 76.3 us (0.73)
  local copies, waits for them, and re-layouts: 32.6 us -> 2.65 us
  Pallas kernels: 35 us -> 48.2 us
  waiting for transfers between devices: 8.41 us -> 1.88 us
  starting transfers between devices: 27.1 us -> 21.6 us
    unnamed x80 -> x24, local copies, waits for them, and re-layouts: 32.6 us -> 2.65 us
    pallas_call x4, Pallas kernels: 27.6 us -> 39 us  [the longest x1 19 us: per_device(): call(backward_kernel, STEPS, [SMEM(), SMEM(), whole(TOKENS, D), whole(TOK...]
    ppermute x8, waiting for transfers between devices: 8.4 us -> 1.88 us  [the longest x2 1.86 us: exchange(): lax.ppermute(edge_b, 'lon', pairs_b)]
    ppermute x8, starting transfers between devices: 20.6 us -> 14.3 us  [the longest x2 6.74 us: exchange(): lax.ppermute(corner_b, ('lon', 'lat'), across(pairs_b))]
    pallas_call x1, Pallas kernels: 7.33 us -> 9.22 us  [per_device(): call(own_kernel, STEPS, [SMEM(), whole(TOKENS, D), by_lat(BAND, D), whole...]
    ppermute x2, starting transfers between devices: 2.1 us -> 3.62 us  [exchange(): lax.ppermute(band, 'lat', [(0, 1), (1, 0)])]
  transfers between devices with their start and end apart: 11 -> 11, of which waited for: 2 -> 1; matrix products, arithmetic and copies ran while one was open for 0% -> 1% of each run, Pallas kernels for 21% -> 43%
where the time goes in v1:
time: 76.3 us; the launch traced here: 75.8 us
  Pallas kernels  48.2 us (63%)
  starting transfers between devices  21.6 us (28%)
  local copies, waits for them, and re-layouts  2.65 us (3%)
  waiting for transfers between devices  1.88 us (2%)
  between operations  0.83 us (1%)
    pallas_call x1, Pallas kernels, per_device(): call(backward_kernel, STEPS, [SMEM(), SMEM(), whole(TOKENS, D), whole(TOK...  19 us
    pallas_call x1, Pallas kernels, per_device(): call(forward_kernel, 1, [SMEM()] + [HBM()] * 12, [HBM()] * 8, [like(STEPS...  12.4 us
    pallas_call x1, Pallas kernels, per_device(): call(own_kernel, STEPS, [SMEM(), whole(TOKENS, D), by_lat(BAND, D), whole...  9.22 us
    ppermute x2, starting transfers between devices, exchange(): lax.ppermute(corner_b, ('lon', 'lat'), across(pairs_b))  6.74 us
    ppermute x2, starting transfers between devices, exchange(): lax.ppermute(edge_b, 'lon', pairs_b)  4.98 us
    pallas_call x1, Pallas kernels, per_device(): call(output_kernel, 1, [SMEM(), whole(TOKENS, D), whole(TOKENS, D), whole...  4.07 us
    all_to_all x1, starting transfers between devices, per_device(): lax.all_to_all(going, 'lon', split_axis=0, concat_axis=0, tiled=True)  3.7 us
    ppermute x2, starting transfers between devices, exchange(): lax.ppermute(band, 'lat', [(0, 1), (1, 0)])  3.62 us
  transfers between devices with their start and end apart: 11, of which 1 were waited for; matrix products, arithmetic and copies ran while one was open for 1% of the time, Pallas kernels for 43%

profile of v1, /device:TPU:0, one launch (start us, length us, event | category | flops | bytes accessed | tf_op | source)
XLA Modules:
  0.0 75.8 jit_solution(11791599813205493975)
XLA Ops:
  0.6 0.7 pad_add_fusion.place_ref
  1.3 3.6 %edge_tokens.1 = (bf16[184,1024]{1,0:T(8,128)(2,1)}, bf16[184,1024]{1,0:T(8,128)(2,1)}, bf16[192,1024]{1,0:T(8,128)(2,1)}, bf16[80,1024]{1,0:T(8,128)(2,1)}, bf16[80,1024]{1,0:T(8,128)(2,1)}) custom-call(s32[2]{0:T(128)} %pad_add_fusion.place_ref, bf16[192,1024]{1,0:T(8,128)(2,1)} %bitcast.8, bf16[192,1024]{1,0:T(8,128)(2,1)} %bitcast.15, ...), custom_call_target="tpu_custom_call" | custom-call | bytes 8388608 | tf_op jit(solution)/shard_map/edge_tokens/pallas_call | solution.py:550
  4.9 3.0 %collective-permute-start = (bf16[192,1024]{1,0:T(8,128)(2,1)}, bf16[192,1024]{1,0:T(8,128)(2,1)S(1)}, u32[]{:S(2)}, u32[]{:S(2)}) collective-permute-start(bf16[192,1024]{1,0:T(8,128)(2,1)} %get-tuple-element.26), channel_id=1, source_target_pairs={{0,1},{1,0},{2,3},{3,2},{4,5},{5,4},{6,7},{7,6},{8,9},{9,8},{10,11... | collective-permute-start | bytes 1179656 | tf_op jit(solution)/shard_map/ppermute | solution.py:526
  7.9 0.0 collective-permute-start.1
  7.9 4.7 %collective-permute-start.2 = (bf16[184,1024]{1,0:T(8,128)(2,1)}, bf16[184,1024]{1,0:T(8,128)(2,1)S(1)}, u32[]{:S(2)}, u32[]{:S(2)}) collective-permute-start(bf16[184,1024]{1,0:T(8,128)(2,1)} %get-tuple-element.28), channel_id=1, source_target_pairs={{0,30},{2,4},{4,2},{6,8},{8,6},{10,12},{12,10},{14,16},{16,14},{18... | collective-permute-start | bytes 1130504 | tf_op jit(solution)/shard_map/ppermute | solution.py:525
  12.6 0.0 collective-permute-start.3
  12.6 1.7 %collective-permute-start.4 = (bf16[80,1024]{1,0:T(8,128)(2,1)}, bf16[80,1024]{1,0:T(8,128)(2,1)S(1)}, u32[]{:S(2)}, u32[]{:S(2)}) collective-permute-start(bf16[80,1024]{1,0:T(8,128)(2,1)} %get-tuple-element.30), channel_id=1, source_target_pairs={{0,31},{1,30},{2,5},{3,4},{4,3},{5,2},{6,9},{7,8},{8,7},{9,6},{10,... | collective-permute-start | bytes 491528 | tf_op jit(solution)/shard_map/ppermute | solution.py:528
  14.2 9.2 %own_projections.1 = (bf16[4,192,256]{2,1,0:T(8,128)(2,1)}, f32[4,192,256]{2,1,0:T(8,128)}, f32[4,192,256]{2,1,0:T(8,128)}, bf16[4,2,288,256]{3,2,1,0:T(8,128)(2,1)}, bf16[4,192,256]{2,1,0:T(8,128)(2,1)}) custom-call(s32[2]{0:T(128)} %pad_add_fusion.place_ref, f32[16]{0:T(128)} %sharp_ref.3, bf16[192,1024]{1,0:T(8,128)(2,1)} %bitcast.9, ...), custom_call_target="tpu_custom_call" | custom-call | flops 2013265920 | bytes 8388608 | tf_op jit(solution)/shard_map/own_projections/pallas_call | solution.py:559
  23.5 0.0 collective-permute-done.3.corner_a_hbm.corner_a_ref
  23.5 0.0 copy-start.4
  23.5 0.0 collective-permute-done.4.corner_b_hbm.corner_b_ref
  23.5 0.0 copy-start.5
  23.5 0.0 collective-permute-done.1.edge_a_hbm.edge_a_ref
  23.5 0.0 copy-start.2
  23.5 0.0 collective-permute-done.2.edge_b_hbm.edge_b_ref
  23.5 0.0 copy-start.3
  23.5 0.0 collective-permute-done.band_hbm.band_ref
  23.6 0.0 copy-start.1
  23.6 0.6 copy-done.4
  24.1 0.1 copy-done.5
  24.2 0.1 copy-done.2
  24.3 0.1 copy-done.3
  24.5 0.2 copy-done.1
  24.6 12.4 %attention_forward.1 = (bf16[4,2,400,256]{3,2,1,0:T(8,128)(2,1)}, bf16[192,1024]{1,0:T(8,128)(2,1)}, f32[192,128]{1,0:T(8,128)}, f32[72,128]{1,0:T(8,128)}, f32[...) custom-call(s32[2]{0:T(128)} %pad_add_fusion.place_ref, s32[2,6]{1,0:T(2,128)} %flag_ref.3, ...), custom_call_target="tpu_custom_call" | custom-call | flops 4194304000 | bytes 8388608 | tf_op jit(solution)/shard_map/attention_forward/pallas_call | solution.py:572
  37.0 0.6 collective-permute-start.7
  37.6 0.0 copy-done
  37.6 0.7 copy.13.owner_ref
  38.3 2.5 %collective-permute-start.8 = (f32[40,128]{1,0:T(8,128)}, f32[40,128]{1,0:T(8,128)S(1)}, u32[]{:S(2)}, u32[]{:S(2)}) collective-permute-start(f32[40,128]{1,0:T(8,128)} %get-tuple-element.38), channel_id=1, source_target_pairs={{0,3},{1,2},{2,1},{3,0},{4,7},{5,6},{6,5},{7,4},{8,11},{9,10},{10,... | collective-permute-start | bytes 61448 | tf_op jit(solution)/shard_map/ppermute | solution.py:527
  40.9 5.1 %collective-permute-start.9 = (f32[40,128]{1,0:T(8,128)}, f32[40,128]{1,0:T(8,128)S(1)}, u32[]{:S(2)}, u32[]{:S(2)}) collective-permute-start(f32[40,128]{1,0:T(8,128)} %get-tuple-element.39), channel_id=1, source_target_pairs={{0,31},{1,30},{2,5},{3,4},{4,3},{5,2},{6,9},{7,8},{8,7},{9,6},{10,... | collective-permute-start | bytes 61448 | tf_op jit(solution)/shard_map/ppermute | solution.py:528
  45.9 0.0 collective-permute-start.5
  45.9 0.3 collective-permute-start.6
  46.2 4.1 %output_segments.1 = bf16[16,6,4,1024]{3,2,1,0:T(4,128)(2,1)} custom-call(s32[2]{0:T(128)} %pad_add_fusion.place_ref, s32[12,4]{1,0:T(8,128)} %copy.13.owner_ref, bf16[192,1024]{1,0:T(8,128)(2,1)} %bitcast.10, bf16[192,1024]{1,0:T(8,128)(2,1)} %get-tuple-element.34.mixed_ref, bf16[1024,1024]{1,0:T(8,128)(2,1)} %wo_ref.5), custom_call_target="tpu_custom_call" | custom-call | flops 419430400 | bytes 8388608 | tf_op jit(solution)/shard_map/output_segments/pallas_call | solution.py:589
  50.3 0.0 collective-permute-done.8.stat_ca_ref
  50.3 0.0 collective-permute-done.9.stat_cb_ref
  50.3 0.0 copy-start.10
  50.3 0.0 collective-permute-done.5.stat_a_ref
  50.3 0.0 copy-start.7
  50.4 1.9 %collective-permute-done.6.stat_b_ref = f32[72,128]{1,0:T(8,128)S(1)} collective-permute-done((f32[72,128]{1,0:T(8,128)}, f32[72,128]{1,0:T(8,128)S(1)}, u32[]{:S(2)}, u32[]{:S(2)}) %collective-permute-start.6) | collective-permute-done | bytes 36896 | tf_op jit(solution)/shard_map/ppermute | solution.py:525
  52.2 0.0 collective-permute-done.7.stat_band_ref
  52.2 3.7 %all-to-all-start = ((bf16[16,6,4,1024]{3,2,1,0:T(4,128)(2,1)}), bf16[16,6,4,1024]{3,2,1,0:T(4,128)(2,1)S(1)}, u32[]{:S(2)}, u32[]{:S(2)}) async-start(bf16[16,6,4,1024]{3,2,1,0:T(4,128)(2,1)} %output_segments.1), calls=%async_computation | async-start | bytes 1572864 | tf_op jit(solution)/shard_map/all_to_all | solution.py:599
  55.9 0.0 copy-done.9
  55.9 0.0 copy-done.10
  55.9 0.0 copy-done.7
  56.0 0.0 copy-done.8
  56.0 0.0 copy-done.6
  56.0 19.0 %attention_backward.1 = bf16[192,1024]{1,0:T(8,128)(2,1)} custom-call(s32[2]{0:T(128)} %pad_add_fusion.place_ref, f32[16]{0:T(128)} %sharp_ref.3, s32[2,6]{1,0:T(2,128)} %flag_ref.3, bf16[192,1024]{1,0:T(8,128)(2,1)} %bitcast.11, bf16[192,1024]{1,0:T(8,128)(2,1)} %bitcast.17, bf16[192,1024]{1,0:T(8,128)(2,1)} %copy-done.1, bf16[184,1024]{1,0:T(8,128)(2,1)} %copy-done.2, ...), custom_call_target="tpu_custom_call" | custom-call | flops 8388608000 | bytes 8388608 | tf_op jit(solution)/shard_map/attention_backward/pallas_call | solution.py:601
  74.9 0.0 all-to-all-done
  74.9 0.9 %copy.15 = bf16[1,1,16,6,4,1024]{5,4,3,2,1,0:T(4,128)(2,1)} copy(bf16[1,1,16,6,4,1024]{5,4,3,2,1,0:T(4,128)(2,1)S(1)} %bitcast.12) | data formatting | bytes 1572864
  (4 shorter events, 0.0 us)
Async XLA Ops:
  4.9 18.7 %collective-permute-start = (bf16[192,1024]{1,0:T(8,128)(2,1)}, bf16[192,1024]{1,0:T(8,128)(2,1)S(1)}, u32[]{:S(2)}, u32[]{:S(2)}) collective-permute-start(bf16[192,1024]{1,0:T(8,128)(2,1)} %get-tuple-element.26), channel_id=1, source_target_pairs={{0,1},{1,0},{2,3},{3,2},{4,5},{5,4},{6,7},{7,6},{8,9},{9,8},{10,11... | collective-permute-start | bytes 1179656 | tf_op jit(solution)/shard_map/ppermute | solution.py:526
  7.9 15.6 %collective-permute-start.1 = (bf16[184,1024]{1,0:T(8,128)(2,1)}, bf16[184,1024]{1,0:T(8,128)(2,1)S(1)}, u32[]{:S(2)}, u32[]{:S(2)}) collective-permute-start(bf16[184,1024]{1,0:T(8,128)(2,1)} %get-tuple-element.27), channel_id=1, source_target_pairs={{0,2},{2,0},{4,6},{6,4},{8,10},{10,8},{12,14},{14,12},{16,18},{18,... | collective-permute-start | bytes 1130504 | tf_op jit(solution)/shard_map/ppermute | solution.py:524
  7.9 15.6 %collective-permute-start.2 = (bf16[184,1024]{1,0:T(8,128)(2,1)}, bf16[184,1024]{1,0:T(8,128)(2,1)S(1)}, u32[]{:S(2)}, u32[]{:S(2)}) collective-permute-start(bf16[184,1024]{1,0:T(8,128)(2,1)} %get-tuple-element.28), channel_id=1, source_target_pairs={{0,30},{2,4},{4,2},{6,8},{8,6},{10,12},{12,10},{14,16},{16,14},{18... | collective-permute-start | bytes 1130504 | tf_op jit(solution)/shard_map/ppermute | solution.py:525
  12.6 10.9 %collective-permute-start.3 = (bf16[80,1024]{1,0:T(8,128)(2,1)}, bf16[80,1024]{1,0:T(8,128)(2,1)S(1)}, u32[]{:S(2)}, u32[]{:S(2)}) collective-permute-start(bf16[80,1024]{1,0:T(8,128)(2,1)} %get-tuple-element.29), channel_id=1, source_target_pairs={{0,3},{1,2},{2,1},{3,0},{4,7},{5,6},{6,5},{7,4},{8,11},{9,10},{10,... | collective-permute-start | bytes 491528 | tf_op jit(solution)/shard_map/ppermute | solution.py:527
  12.6 10.9 %collective-permute-start.4 = (bf16[80,1024]{1,0:T(8,128)(2,1)}, bf16[80,1024]{1,0:T(8,128)(2,1)S(1)}, u32[]{:S(2)}, u32[]{:S(2)}) collective-permute-start(bf16[80,1024]{1,0:T(8,128)(2,1)} %get-tuple-element.30), channel_id=1, source_target_pairs={{0,31},{1,30},{2,5},{3,4},{4,3},{5,2},{6,9},{7,8},{8,7},{9,6},{10,... | collective-permute-start | bytes 491528 | tf_op jit(solution)/shard_map/ppermute | solution.py:528
  23.5 0.7 copy-start.4
  23.5 0.7 copy-start.5
  23.5 0.8 %copy-start.2 = (bf16[184,1024]{1,0:T(8,128)(2,1)}, bf16[184,1024]{1,0:T(8,128)(2,1)S(1)}, u32[]{:S(2)}) copy-start(bf16[184,1024]{1,0:T(8,128)(2,1)S(1)} %collective-permute-done.1.edge_a_hbm.edge_a_ref) | copy-start | bytes 1130500
  23.5 0.9 %copy-start.3 = (bf16[184,1024]{1,0:T(8,128)(2,1)}, bf16[184,1024]{1,0:T(8,128)(2,1)S(1)}, u32[]{:S(2)}) copy-start(bf16[184,1024]{1,0:T(8,128)(2,1)S(1)} %collective-permute-done.2.edge_b_hbm.edge_b_ref) | copy-start | bytes 1130500
  23.6 1.1 %copy-start.1 = (bf16[192,1024]{1,0:T(8,128)(2,1)}, bf16[192,1024]{1,0:T(8,128)(2,1)S(1)}, u32[]{:S(2)}) copy-start(bf16[192,1024]{1,0:T(8,128)(2,1)S(1)} %collective-permute-done.band_hbm.band_ref) | copy-start | bytes 1179652
  24.6 13.0 %copy-start = (s32[12,4]{0,1:T(4,128)S(1)}, s32[12,4]{0,1:T(4,128)}, u32[]{:S(2)}) copy-start(s32[12,4]{0,1:T(4,128)} %param.19) | copy-start | bytes 580
  37.0 15.2 %collective-permute-start.7 = (f32[96,128]{1,0:T(8,128)}, f32[96,128]{1,0:T(8,128)S(1)}, u32[]{:S(2)}, u32[]{:S(2)}) collective-permute-start(f32[96,128]{1,0:T(8,128)} %get-tuple-element.37), channel_id=1, source_target_pairs={{0,1},{1,0},{2,3},{3,2},{4,5},{5,4},{6,7},{7,6},{8,9},{9,8},{10,11... | collective-permute-start | bytes 147464 | tf_op jit(solution)/shard_map/ppermute | solution.py:526
  38.3 12.0 %collective-permute-start.8 = (f32[40,128]{1,0:T(8,128)}, f32[40,128]{1,0:T(8,128)S(1)}, u32[]{:S(2)}, u32[]{:S(2)}) collective-permute-start(f32[40,128]{1,0:T(8,128)} %get-tuple-element.38), channel_id=1, source_target_pairs={{0,3},{1,2},{2,1},{3,0},{4,7},{5,6},{6,5},{7,4},{8,11},{9,10},{10,... | collective-permute-start | bytes 61448 | tf_op jit(solution)/shard_map/ppermute | solution.py:527
  40.9 9.5 %collective-permute-start.9 = (f32[40,128]{1,0:T(8,128)}, f32[40,128]{1,0:T(8,128)S(1)}, u32[]{:S(2)}, u32[]{:S(2)}) collective-permute-start(f32[40,128]{1,0:T(8,128)} %get-tuple-element.39), channel_id=1, source_target_pairs={{0,31},{1,30},{2,5},{3,4},{4,3},{5,2},{6,9},{7,8},{8,7},{9,6},{10,... | collective-permute-start | bytes 61448 | tf_op jit(solution)/shard_map/ppermute | solution.py:528
  45.9 4.4 %collective-permute-start.5 = (f32[72,128]{1,0:T(8,128)}, f32[72,128]{1,0:T(8,128)S(1)}, u32[]{:S(2)}, u32[]{:S(2)}) collective-permute-start(f32[72,128]{1,0:T(8,128)} %get-tuple-element.35), channel_id=1, source_target_pairs={{0,2},{2,0},{4,6},{6,4},{8,10},{10,8},{12,14},{14,12},{16,18},{18,... | collective-permute-start | bytes 110600 | tf_op jit(solution)/shard_map/ppermute | solution.py:524
  45.9 6.3 %collective-permute-start.6 = (f32[72,128]{1,0:T(8,128)}, f32[72,128]{1,0:T(8,128)S(1)}, u32[]{:S(2)}, u32[]{:S(2)}) collective-permute-start(f32[72,128]{1,0:T(8,128)} %get-tuple-element.36), channel_id=1, source_target_pairs={{0,30},{2,4},{4,2},{6,8},{8,6},{10,12},{12,10},{14,16},{16,14},{18... | collective-permute-start | bytes 110600 | tf_op jit(solution)/shard_map/ppermute | solution.py:525
  50.3 5.6 %copy-start.9 = (f32[40,128]{1,0:T(8,128)}, f32[40,128]{1,0:T(8,128)S(1)}, u32[]{:S(2)}) copy-start(f32[40,128]{1,0:T(8,128)S(1)} %collective-permute-done.8.stat_ca_ref) | copy-start | bytes 61444
  50.3 5.6 %copy-start.10 = (f32[40,128]{1,0:T(8,128)}, f32[40,128]{1,0:T(8,128)S(1)}, u32[]{:S(2)}) copy-start(f32[40,128]{1,0:T(8,128)S(1)} %collective-permute-done.9.stat_cb_ref) | copy-start | bytes 61444
  50.3 5.6 %copy-start.7 = (f32[72,128]{1,0:T(8,128)}, f32[72,128]{1,0:T(8,128)S(1)}, u32[]{:S(2)}) copy-start(f32[72,128]{1,0:T(8,128)S(1)} %collective-permute-done.5.stat_a_ref) | copy-start | bytes 110596
  52.2 3.7 %copy-start.8 = (f32[72,128]{1,0:T(8,128)}, f32[72,128]{1,0:T(8,128)S(1)}, u32[]{:S(2)}) copy-start(f32[72,128]{1,0:T(8,128)S(1)} %collective-permute-done.6.stat_b_ref) | copy-start | bytes 110596
  52.2 3.7 %copy-start.6 = (f32[96,128]{1,0:T(8,128)}, f32[96,128]{1,0:T(8,128)S(1)}, u32[]{:S(2)}) copy-start(f32[96,128]{1,0:T(8,128)S(1)} %collective-permute-done.7.stat_band_ref) | copy-start | bytes 147460
  52.2 22.7 %all-to-all-start = ((bf16[16,6,4,1024]{3,2,1,0:T(4,128)(2,1)}), bf16[16,6,4,1024]{3,2,1,0:T(4,128)(2,1)S(1)}, u32[]{:S(2)}, u32[]{:S(2)}) async-start(bf16[16,6,4,1024]{3,2,1,0:T(4,128)(2,1)} %output_segments.1), calls=%async_computation | async-start | bytes 1572864 | tf_op jit(solution)/shard_map/all_to_all | solution.py:599

commit v2 on v1

v2 whole, which is shorter than its diff:
```python
import functools

import jax
import jax.numpy as jnp
import numpy as np
from jax import lax
from jax.experimental import pallas as pl
from jax.experimental.pallas import tpu as pltpu
from jax.sharding import PartitionSpec as P

HEADS = 16
HALO = 6
ROWS = 12
COLS = 16
SEG = 4
D = 1024
HEAD_DIM = D // HEADS
TOKENS = ROWS * COLS
HALF = TOKENS // 2
BAND = HALO * COLS
SIDE = ROWS * HALO
CORNER = 40
QUAD = 256
QUAD_HEADS = QUAD // HEAD_DIM
STEPS = D // QUAD
STACK = QUAD_HEADS * HALF
PAD_SIDE = BAND + 2 * CORNER
MIDDLE = TOKENS + 2 * SIDE
SPAN = PAD_SIDE + MIDDLE
KEYS = SPAN + PAD_SIDE
HALO_ROWS = 2 * PAD_SIDE + 2 * SIDE - BAND
HALO_QUERIES = PAD_SIDE + 2 * SIDE
EDGE = SIDE + CORNER
STATS = 128
MESSAGE = D + 2 * STATS
MIB = 1024 * 1024
BF = jnp.bfloat16
F32 = jnp.float32


def dot(a, b):
    return jnp.dot(a, b, preferred_element_type=F32)


def dot_nt(a, b):
    return lax.dot_general(a, b, (((1,), (1,)), ((), ())), preferred_element_type=F32)


def dot_tn(a, b):
    return lax.dot_general(a, b, (((0,), (0,)), ((), ())), preferred_element_type=F32)


def first_column(side, parity):
    return COLS - HALO if side == parity else 0


def selection_table():
    table = np.zeros((4, 2 * EDGE + 2 * CORNER, TOKENS + BAND), np.float32)
    for lat in range(2):
        for parity in range(2):
            for side in range(2):
                first, base = first_column(side, parity), side * EDGE
                picks = table[2 * lat + parity]
                for c in range(HALO):
                    for r in range(ROWS):
                        picks[base + r * HALO + c, r * COLS + first + c] = 1
                    for i in range(HALO):
                        picks[base + SIDE + i * HALO + c, TOKENS + i * COLS + first + c] = 1
                        row = i + HALO * (1 - lat)
                        picks[2 * EDGE + side * CORNER + i * HALO + c, row * COLS + first + c] = 1
    return table


def key_table():
    table = np.full((4, 8, KEYS), 1000, np.int32)
    table[:, 2] = -1
    for lat in range(2):
        for parity in range(2):
            picks = table[2 * lat + parity]
            low = {"lat": ROWS if lat == 0 else -HALO, "own": 0, "rim": -HALO if lat == 0 else ROWS}

            def put(at, count, width, first_col, kind):
                for k in range(count * width):
                    i, c = divmod(k, width)
                    picks[0, at + k] = low[kind] + i
                    picks[1, at + k] = first_col + c
                    if kind == "rim":
                        picks[2, at + k] = i

            put(0, HALO, COLS, 0, "lat")
            put(PAD_SIDE, ROWS, COLS, 0, "own")
            put(SPAN, HALO, COLS, 0, "rim")
            for side in range(2):
                col = COLS if side == parity else -HALO
                put(BAND + side * CORNER, HALO, HALO, col, "lat")
                put(PAD_SIDE + TOKENS + side * SIDE, ROWS, HALO, col, "own")
                put(SPAN + BAND + side * CORNER, HALO, HALO, col, "rim")
    return table


def head_mask(h, dtype):
    lane = lax.broadcasted_iota(jnp.int32, (1, QUAD), 1)
    return jnp.where(lane // HEAD_DIM == h, 1.0, 0.0).astype(dtype)


def head_mean(values):
    a = lax.broadcasted_iota(jnp.int32, (QUAD, QUAD), 0) // HEAD_DIM
    b = lax.broadcasted_iota(jnp.int32, (QUAD, QUAD), 1) // HEAD_DIM
    block = jnp.where(a == b, 1.0 / HEAD_DIM, 0.0).astype(BF)
    return dot(values.astype(BF), block)


def unit(raw):
    return raw * lax.rsqrt(head_mean(raw * raw) + 1e-06)


def unit_back(raw, grad):
    inverse = lax.rsqrt(head_mean(raw * raw) + 1e-06)
    value = raw * inverse
    return inverse * (grad - value * head_mean(value * grad))


def normed(tokens, gain):
    tokens = tokens.astype(F32)
    return tokens * lax.rsqrt(jnp.mean(tokens * tokens, axis=-1, keepdims=True) + 1e-05) * gain


def multiplier(sharp_ref, j):
    out = jnp.zeros((1, QUAD), F32)
    for h in range(QUAD_HEADS):
        out = out + head_mask(h, F32) * (sharp_ref[j * QUAD_HEADS + h] / HEAD_DIM)
    return out


def stacked(block):
    return jnp.concatenate([block * head_mask(h, BF) for h in range(QUAD_HEADS)], axis=0)


def unstacked(stack):
    out = stack[:HALF] * head_mask(0, F32)
    for h in range(1, QUAD_HEADS):
        out = out + stack[h * HALF : (h + 1) * HALF] * head_mask(h, F32)
    return out


def repeated(block):
    return jnp.concatenate([block] * QUAD_HEADS, axis=0)


def head_lanes(first, pick_one):
    a = lax.broadcasted_iota(jnp.int32, (QUAD, STATS), 0)
    b = lax.broadcasted_iota(jnp.int32, (QUAD, STATS), 1)
    hit = b == a // HEAD_DIM + first
    if pick_one:
        hit = hit & (a % HEAD_DIM == 0)
    return jnp.where(hit, 1.0, 0.0).astype(BF)


def halves(values):
    high = values.astype(BF)
    return high, (values - high.astype(F32)).astype(BF)


def spread(stat, j):
    a = lax.broadcasted_iota(jnp.int32, (STATS, QUAD), 0)
    b = lax.broadcasted_iota(jnp.int32, (STATS, QUAD), 1)
    picks = jnp.where(a == b // HEAD_DIM + j * QUAD_HEADS, 1.0, 0.0).astype(BF)
    high, low = halves(stat)
    return dot(high, picks) + dot(low, picks)


def half_start(lat, half):
    return pl.multiple_of(HALF * ((1 - lat) if half == 0 else lat), 16)


def near_mask(mask_ref, tab_ref, flag_ref, lat):
    rows, cols, place = tab_ref[0, 0:1], tab_ref[0, 1:2], tab_ref[0, 2:3]
    keep = jnp.where(place < 0, 1.0, 0.0)
    for i in range(HALO):
        keep = keep + jnp.where(place == i, flag_ref[lat, i].astype(F32), 0.0)
    for half in range(2):
        at = half * PAD_SIDE
        token = lax.broadcasted_iota(jnp.int32, (HALF, SPAN), 0) + half_start(lat, half)
        near = (jnp.abs(rows[:, at : at + SPAN] - token // COLS) <= HALO) & (
            jnp.abs(cols[:, at : at + SPAN] - token % COLS) <= HALO
        )
        mask_ref[half] = jnp.where(near, keep[:, at : at + SPAN], 0.0)


def lay_keys(ref, own, halo):
    ref[:PAD_SIDE] = halo[:PAD_SIDE]
    ref[PAD_SIDE : PAD_SIDE + TOKENS] = own[:TOKENS]
    ref[PAD_SIDE + TOKENS : SPAN] = halo[PAD_SIDE:HALO_QUERIES]
    ref[SPAN : SPAN + BAND] = own[TOKENS:]
    ref[SPAN + BAND :] = halo[HALO_QUERIES:]


class Copies:
    def __init__(self, sems):
        self.sems, self.used = sems, 0

    def start(self, source, target):
        copy = pltpu.make_async_copy(source, target, self.sems.at[self.used])
        self.used += 1
        copy.start()
        return copy

    def by_step(self, pairs):
        base, width = self.used, len(pairs(0))
        self.used += STEPS * width

        def copies(j):
            return [pltpu.make_async_copy(a, b, self.sems.at[base + j * width + k]) for k, (a, b) in enumerate(pairs(j))]

        def start(j):
            for copy in copies(j):
                copy.start()

        def wait(j):
            for copy in copies(j):
                copy.wait()

        return start, wait


def wait_all(copies):
    for copy in copies:
        copy.wait()


def lane_block(at, j):
    return pl.ds(pl.multiple_of((at + j) * QUAD, QUAD), QUAD)


def rows_at(j):
    return pl.ds(j * QUAD, QUAD)


def pack_kernel(
    place_ref, x_hbm, up_hbm, rim_hbm, sel_hbm, edge_a_ref, edge_b_ref, band_ref, corner_a_ref, corner_b_ref,
    x_ref, up_ref, rim_ref, sel_ref, sems,
):
    lat = place_ref[0]
    copies = Copies(sems)
    loads = [
        copies.start(x_hbm, x_ref),
        copies.start(sel_hbm.at[2 * lat + place_ref[1]], sel_ref),
        copies.start(rim_hbm.at[lat], rim_ref),
        copies.start(up_hbm, up_ref),
    ]
    wait_all(loads)
    band_ref[...] = x_ref[pl.ds(half_start(lat, 0), BAND), :]
    picks = sel_ref[...]
    features = dot(picks, jnp.concatenate([x_ref[...], rim_ref[...]], axis=0))
    grads = dot(picks[: 2 * EDGE, :TOKENS], up_ref[...])
    for side, (ref, corner_ref) in enumerate(((edge_a_ref, corner_a_ref), (edge_b_ref, corner_b_ref))):
        at = side * EDGE
        ref[...] = jnp.concatenate([features[at : at + EDGE], grads[at : at + SIDE]], axis=0).astype(BF)
        at = 2 * EDGE + side * CORNER
        corner_ref[...] = features[at : at + CORNER].astype(BF)


def own_kernel(
    place_ref, sharp_ref, x_hbm, rim_hbm, up_hbm, gain_hbm, w3_hbm, wo_hbm,
    qhat_ref, dout_ref, wo_ref, x_ref, gain_ref, qhat_hbm, rawq_hbm, rawk_hbm, kv_hbm,
    kv_ref, w3_ref, rim_ref, up_ref, rawq_ref, rawk_ref, xn_ref, sems,
):
    copies = Copies(sems)
    loads = [copies.start(x_hbm, x_ref), copies.start(rim_hbm.at[place_ref[0]], rim_ref), copies.start(gain_hbm, gain_ref)]
    start, wait = copies.by_step(
        lambda j: [(w3_hbm.at[:, lane_block(k * STEPS, j)], w3_ref.at[j, :, pl.ds(k * QUAD, QUAD)]) for k in range(3)]
        + [(wo_hbm.at[rows_at(j)], wo_ref.at[rows_at(j)])]
    )
    start(0)
    up_load = copies.start(up_hbm, up_ref)
    for j in range(1, STEPS):
        start(j)
    outputs = [(qhat_ref, qhat_hbm), (rawq_ref, rawq_hbm), (rawk_ref, rawk_hbm), (kv_ref, kv_hbm)]
    store, stored = copies.by_step(lambda j: [(ref.at[j], hbm.at[j]) for ref, hbm in outputs])
    wait_all(loads)
    xn_ref[:TOKENS] = normed(x_ref[...], gain_ref[...]).astype(BF)
    xn_ref[TOKENS:] = normed(rim_ref[...], gain_ref[...]).astype(BF)
    for j in range(STEPS):
        wait(j)
        raw = dot(xn_ref[...], w3_ref[j])
        raw_q, raw_k = raw[:TOKENS, :QUAD], raw[:, QUAD : 2 * QUAD]
        units = unit(jnp.concatenate([raw_q, raw_k], axis=0))
        rawq_ref[j] = raw_q
        rawk_ref[j] = raw_k[:TOKENS]
        qhat_ref[j] = (units[:TOKENS] * multiplier(sharp_ref, j)).astype(BF)
        kv_ref[j, 0] = units[TOKENS:].astype(BF)
        kv_ref[j, 1] = raw[:, 2 * QUAD :].astype(BF)
        store(j)
        if j == 0:
            up_load.wait()
        dout_ref[j] = dot_nt(up_ref[...], wo_ref[rows_at(j)]).astype(BF)
    for j in range(STEPS):
        stored(j)


def forward_kernel(
    place_ref, flag_ref, tab_hbm, sel_hbm, w3_hbm, kv_hbm, band_ref, edge_a_ref, edge_b_ref, corner_a_ref, corner_b_ref, gain_ref,
    qhat_ref, dout_ref,
    mixed_ref, stat_a_ref, stat_b_ref, halo_hbm, stat_hbm, xn_hbm, upn_hbm, weight_hbm, dprime_hbm,
    tab_ref, sel_ref, wkv_ref, kv_ref, halo_ref, stat_ref, xn_ref, upn_ref, weight_ref, dprime_ref, mask_ref, key_ref, value_ref, linv_ref, sems,
):
    lat = place_ref[0]
    spot = 2 * lat + place_ref[1]
    copies = Copies(sems)
    loads = [copies.start(tab_hbm.at[spot], tab_ref.at[0])]
    start, wait = copies.by_step(
        lambda j: [(w3_hbm.at[:, lane_block(k * STEPS, j)], wkv_ref.at[j, :, pl.ds((k - 1) * QUAD, QUAD)]) for k in (1, 2)]
        + [(kv_hbm.at[j], kv_ref.at[j])]
    )
    for j in range(STEPS):
        start(j)
    loads.append(copies.start(sel_hbm.at[spot], sel_ref))
    store, stored = copies.by_step(
        lambda j: [(halo_ref.at[j], halo_hbm.at[j]), (weight_ref.at[j], weight_hbm.at[j]), (dprime_ref.at[j], dprime_hbm.at[j])]
    )
    gain = gain_ref[...]
    edge_a, edge_b = edge_a_ref[...].astype(F32), edge_b_ref[...].astype(F32)
    pieces = [ref[...].astype(F32) for ref in (band_ref, corner_a_ref, corner_b_ref)]
    pieces += [edge_a[:SIDE], edge_b[:SIDE], edge_a[SIDE:EDGE], edge_b[SIDE:EDGE]]
    xn_ref[...] = normed(jnp.concatenate(pieces, axis=0), gain).astype(BF)
    upn_ref[...] = jnp.concatenate([edge_a[EDGE:], edge_b[EDGE:]], axis=0).astype(BF)
    stores = [copies.start(xn_ref.at[pl.ds(0, HALO_QUERIES)], xn_hbm), copies.start(upn_ref, upn_hbm)]
    loads[0].wait()
    near_mask(mask_ref, tab_ref, flag_ref, lat)
    stat = jnp.zeros((TOKENS, STATS), F32)
    for j in range(STEPS):
        wait(j)
        raw = dot(xn_ref[...], wkv_ref[j])
        halo_k = unit(raw[:, :QUAD]).astype(BF)
        halo_v = raw[:, QUAD:].astype(BF)
        halo_ref[j, 0] = halo_k
        halo_ref[j, 1] = halo_v
        lay_keys(key_ref.at[j % 2], kv_ref[j, 0], halo_k)
        lay_keys(value_ref.at[j % 2], kv_ref[j, 1], halo_v)
        for half in range(2):
            at, piece = half * PAD_SIDE, pl.ds(half_start(lat, half), HALF)
            scores = dot_nt(stacked(qhat_ref[j, piece, :]), key_ref[j % 2, at : at + SPAN])
            weights = jnp.exp(scores) * repeated(mask_ref[half])
            inverse = jnp.broadcast_to(1.0 / jnp.sum(weights, axis=-1, keepdims=True), (STACK, QUAD))
            weights = weights.astype(BF)
            weight_ref[j, half] = weights
            mixed = unstacked(dot(weights, value_ref[j % 2, at : at + SPAN]) * inverse)
            mixed_ref[piece, rows_at(j)] = mixed.astype(BF)
            linv_ref[j, piece, :] = unstacked(inverse)
        dprime = (dout_ref[j].astype(F32) * linv_ref[j]).astype(BF)
        dprime_ref[j] = dprime
        inner = dprime.astype(F32) * mixed_ref[:, rows_at(j)].astype(F32)
        high, low = halves(linv_ref[j])
        picks = head_lanes(j * QUAD_HEADS, True)
        stat = stat + dot(high, picks) + dot(low, picks) + dot(inner.astype(BF), head_lanes(HEADS + j * QUAD_HEADS, False))
        store(j)
    stat_ref[...] = stat
    stores.append(copies.start(stat_ref, stat_hbm))
    loads[1].wait()
    high, low = halves(stat)
    picks = sel_ref[: 2 * EDGE, :TOKENS]
    picked = dot(picks, high) + dot(picks, low)
    stat_a_ref[...] = picked[:SIDE]
    stat_b_ref[...] = picked[EDGE : EDGE + SIDE]
    for j in range(STEPS):
        stored(j)
    wait_all(stores)


def output_kernel(place_ref, owner_ref, x_ref, mixed_ref, wo_ref, going_hbm, acc_ref, going_ref, count_ref, sems):
    acc_ref[...] = x_ref[...].astype(F32) + dot(mixed_ref[...], wo_ref[...])
    going_ref[...] = jnp.zeros_like(going_ref)
    for o in range(going_ref.shape[0]):
        count_ref[o] = 0
    for s in range(TOKENS // SEG):
        owner = owner_ref[s // (COLS // SEG), s % (COLS // SEG)]
        slot = count_ref[owner]
        count_ref[owner] = slot + 1
        going_ref[owner, slot] = acc_ref[s * SEG : (s + 1) * SEG, :].astype(BF)
    Copies(sems).start(going_ref, going_hbm).wait()


def message_kernel(
    place_ref, up_hbm, upn_hbm, stat_hbm, stat_a_hbm, stat_b_hbm, out_ref, up_ref, upn_ref, stat_ref, stat_a_ref, stat_b_ref, sems
):
    lat = place_ref[0]
    piece = pl.ds(half_start(lat, 0), BAND)
    copies = Copies(sems)
    wait_all(
        [
            copies.start(hbm, ref)
            for hbm, ref in (
                (up_hbm.at[piece], up_ref), (upn_hbm, upn_ref), (stat_hbm.at[piece], stat_ref), (stat_a_hbm, stat_a_ref),
                (stat_b_hbm, stat_b_ref),
            )
        ]
    )
    a = lax.broadcasted_iota(jnp.int32, (2 * CORNER, 2 * SIDE), 0)
    b = lax.broadcasted_iota(jnp.int32, (2 * CORNER, 2 * SIDE), 1)
    side, inside = a // CORNER, HALO * HALO
    row = a - side * CORNER
    picks = jnp.where((b == row + inside * (1 - lat) + side * SIDE) & (row < inside), 1.0, 0.0).astype(BF)
    out_ref[:BAND, :D] = up_ref[...]
    out_ref[BAND:, :D] = dot(picks, upn_ref[...]).astype(BF)
    high, low = halves(jnp.concatenate([stat_a_ref[...], stat_b_ref[...]], axis=0))
    stats = jnp.concatenate([stat_ref[...], dot(picks, high) + dot(picks, low)], axis=0)
    high, low = halves(stats)
    out_ref[:, D : D + STATS] = high
    out_ref[:, D + STATS :] = low


def inner_rows(row_ref, j):
    row = HEADS + j * QUAD_HEADS
    width = row_ref.shape[1]
    parts = [jnp.broadcast_to(row_ref[row + h : row + h + 1, :], (HALF, width)) for h in range(QUAD_HEADS)]
    return jnp.concatenate(parts, axis=0)


def key_pass(keys, values, queries, grads, mask, inner):
    weights = jnp.exp(dot_nt(stacked(keys), queries)) * repeated(mask)
    grad_scores = weights * (dot_nt(stacked(values), grads) - inner)
    return unstacked(dot(grad_scores.astype(BF), queries)), unstacked(dot(weights.astype(BF), grads))


def query_kernel(
    place_ref, sharp_ref, flag_ref, xn_hbm, upn_hbm, tab_hbm, w3_hbm, wo_hbm, qhat_hbm, kv_hbm, halo_hbm, weight_hbm, dprime_hbm,
    rawq_hbm, rawk_hbm, stat_hbm, stat_a_hbm, stat_b_hbm,
    gqn_ref, query_ref, grad_ref, far_ref, mask_ref, wkv_ref, wo_ref, kv_ref, rawk_ref, row_ref,
    xn_ref, upn_ref, tab_ref, wq_ref, qhat_ref, halo_ref, weight_ref, dprime_ref, rawq_ref, stat_ref, stat_a_ref, stat_b_ref,
    key_ref, value_ref, dq_ref, sems,
):
    lat = place_ref[0]
    copies = Copies(sems)
    loads = [
        copies.start(hbm, ref)
        for hbm, ref in (
            (xn_hbm, xn_ref), (upn_hbm, upn_ref), (stat_hbm, stat_ref), (stat_a_hbm, stat_a_ref), (stat_b_hbm, stat_b_ref),
            (tab_hbm.at[2 * lat + place_ref[1]], tab_ref.at[0]),
        )
    ]
    start, wait = copies.by_step(
        lambda j: [
            (w3_hbm.at[:, lane_block(0, j)], wq_ref.at[j]),
            (wo_hbm.at[rows_at(j)], wo_ref.at[rows_at(j)]),
            (qhat_hbm.at[j], qhat_ref.at[j]),
            (kv_hbm.at[j], kv_ref.at[j]),
            (halo_hbm.at[j], halo_ref.at[j]),
            (dprime_hbm.at[j], dprime_ref.at[j]),
            (weight_hbm.at[j], weight_ref.at[j]),
            (rawq_hbm.at[j], rawq_ref.at[j]),
        ]
    )
    start_later, wait_later = copies.by_step(
        lambda j: [
            (rawk_hbm.at[j], rawk_ref.at[j]),
            (w3_hbm.at[:, lane_block(STEPS, j)], wkv_ref.at[j, 0]),
            (w3_hbm.at[:, lane_block(2 * STEPS, j)], wkv_ref.at[j, 1]),
        ]
    )
    for j in range(STEPS):
        start(j)
    for j in range(STEPS):
        start_later(j)
    wait_all(loads)
    near_mask(mask_ref, tab_ref, flag_ref, lat)
    edges = jnp.concatenate([stat_a_ref[...], stat_b_ref[...]], axis=0)
    row_ref[...] = jnp.concatenate([stat_ref[...], edges], axis=0).T
    gqn_ref[...] = jnp.zeros_like(gqn_ref)
    for j in range(STEPS):
        wait(j)
        lay_keys(key_ref.at[j % 2], kv_ref[j, 0], halo_ref[j, 0])
        lay_keys(value_ref.at[j % 2], kv_ref[j, 1], halo_ref[j, 1])
        halo_q = (unit(dot(xn_ref[...], wq_ref[j])) * multiplier(sharp_ref, j)).astype(BF)
        query_ref[j, :PAD_SIDE] = halo_q[:PAD_SIDE]
        query_ref[j, PAD_SIDE : PAD_SIDE + TOKENS] = qhat_ref[j]
        query_ref[j, PAD_SIDE + TOKENS :] = halo_q[PAD_SIDE:]
        grad_ref[j, :TOKENS] = dprime_ref[j]
        grad_ref[j, TOKENS:] = (dot_nt(upn_ref[...], wo_ref[rows_at(j)]) * spread(edges, j)).astype(BF)
        for half in range(2):
            at, piece = half * PAD_SIDE, pl.ds(half_start(lat, half), HALF)
            stat = stat_ref[piece, :]
            lane = HEADS + j * QUAD_HEADS
            inner = jnp.concatenate([stat[:, lane + h : lane + h + 1] for h in range(QUAD_HEADS)], axis=0)
            grad_probs = dot_nt(stacked(dprime_ref[j, piece, :]), value_ref[j % 2, at : at + SPAN])
            grad_scores = weight_ref[j, half].astype(F32) * (grad_probs - inner)
            dq_ref[j % 2, piece, :] = unstacked(dot(grad_scores.astype(BF), key_ref[j % 2, at : at + SPAN]))
        piece = pl.ds(half_start(lat, 1), HALF)
        far_ref[j, 0], far_ref[j, 1] = key_pass(
            kv_ref[j, 0, piece, :], kv_ref[j, 1, piece, :], query_ref[j, PAD_SIDE:], grad_ref[j], mask_ref[1, :, :MIDDLE],
            inner_rows(row_ref, j),
        )
        grad_q = unit_back(rawq_ref[j], dq_ref[j % 2] * multiplier(sharp_ref, j)).astype(BF)
        gqn_ref[...] += dot_nt(grad_q, wq_ref[j])
    for j in range(STEPS):
        wait_later(j)


def key_kernel(
    place_ref, x_hbm, up_hbm, gain_hbm, gqn_ref, query_ref, grad_ref, far_ref, mask_ref, wkv_ref, wo_ref, kv_ref, rawk_ref, row_ref,
    message_ref,
    out_hbm,
    x_ref, up_ref, gain_ref, out_ref, all_row_ref, all_ref, dk_ref, dv_ref, acc_ref, sems,
):
    lat = place_ref[0]
    copies = Copies(sems)
    loads = [copies.start(x_hbm, x_ref), copies.start(up_hbm, up_ref), copies.start(gain_hbm, gain_ref)]
    message = message_ref[:, D : D + STATS].astype(F32) + message_ref[:, D + STATS :].astype(F32)
    all_row_ref[...] = jnp.concatenate([message.T, row_ref[...]], axis=1)
    acc_ref[...] = gqn_ref[...]
    for j in range(STEPS):
        slot = j % 2
        all_ref[slot, :PAD_SIDE] = (dot_nt(message_ref[:, :D], wo_ref[rows_at(j)]) * spread(message, j)).astype(BF)
        all_ref[slot, PAD_SIDE:] = grad_ref[j]
        near, far = pl.ds(half_start(lat, 0), HALF), pl.ds(half_start(lat, 1), HALF)
        dk_ref[slot, near, :], dv_ref[slot, near, :] = key_pass(
            kv_ref[j, 0, near, :], kv_ref[j, 1, near, :], query_ref[j], all_ref[slot], mask_ref[0], inner_rows(all_row_ref, j)
        )
        dk_ref[slot, far, :], dv_ref[slot, far, :] = far_ref[j, 0], far_ref[j, 1]
        grad_k = unit_back(rawk_ref[j], dk_ref[slot]).astype(BF)
        acc_ref[...] += dot_nt(grad_k, wkv_ref[j, 0]) + dot_nt(dv_ref[slot].astype(BF), wkv_ref[j, 1])
    wait_all(loads)
    tokens = x_ref[...].astype(F32)
    inverse = lax.rsqrt(jnp.mean(tokens * tokens, axis=-1, keepdims=True) + 1e-05)
    grad = acc_ref[...] * gain_ref[...]
    value = tokens * inverse
    back = inverse * (grad - value * jnp.mean(value * grad, axis=-1, keepdims=True))
    out_ref[...] = (up_ref[...].astype(F32) + back).astype(BF)
    copies.start(out_ref, out_hbm).wait()


def call(kernel, inputs, outputs, scratch=(), limit=32, flops=0, name=None):
    def specs(pairs):
        return [pl.BlockSpec(memory_space=space) for space, _ in pairs]

    def placed(space, array):
        return array if space == pltpu.SMEM else pltpu.with_memory_space_constraint(array, space)

    return pl.pallas_call(
        kernel,
        in_specs=specs(inputs),
        out_specs=specs(outputs),
        out_shape=[space(shape.shape, shape.dtype) for space, shape in outputs],
        scratch_shapes=list(scratch),
        compiler_params=pltpu.CompilerParams(vmem_limit_bytes=limit * MIB),
        cost_estimate=pl.CostEstimate(flops=flops, bytes_accessed=8 << 20, transcendentals=0),
        name=name,
    )(*[placed(space, array) for space, array in inputs])


def hbm(*arrays):
    return [(pltpu.HBM, array) for array in arrays]


def near(*arrays):
    return [(pltpu.VMEM, array) for array in arrays]


def scalars(*arrays):
    return [(pltpu.SMEM, array) for array in arrays]


def like(*shape, dtype=BF):
    return jax.ShapeDtypeStruct(shape, dtype)


def partners(count):
    return (
        [(i, i + 1 - 2 * (i % 2)) for i in range(count)],
        [(i, (i - 1 + 2 * (i % 2)) % count) for i in range(count)],
    )


def across(pairs):
    return [(2 * a + lat, 2 * b + 1 - lat) for a, b in pairs for lat in range(2)]


def per_device(
    slab_features, upstream_gradient, rim_feature_rows, rim_presence_flags, feature_rescaling_coefficients,
    triple_projection_matrix, final_projection_matrix, score_sharpness, column_group_decoder_longitude,
):
    count = lax.axis_size("lon")
    cap = max(2, (2 * (TOKENS // SEG) + count - 1) // count)
    place = jnp.stack([lax.axis_index("lat"), lax.axis_index("lon") % 2]).astype(jnp.int32)
    x = slab_features.reshape(TOKENS, D)
    up = upstream_gradient.reshape(TOKENS, D)
    rim = rim_feature_rows.reshape(2, BAND, D)
    gain = feature_rescaling_coefficients.reshape(1, D)
    w3, wo = triple_projection_matrix, final_projection_matrix
    table = selection_table()
    selection = jnp.asarray(table, BF)
    keys = jnp.asarray(key_table())
    flags = rim_presence_flags

    side_a, side_b = partners(count)

    def vmem(*shape, dtype=BF):
        return pltpu.VMEM(shape, dtype)

    def sems(n):
        return pltpu.SemaphoreType.DMA((n,))

    picks_shape = table.shape[1:]
    edge_a, edge_b, band, corner_a, corner_b = call(
        pack_kernel,
        scalars(place) + hbm(x, up, rim, selection),
        near(like(EDGE + SIDE, D), like(EDGE + SIDE, D), like(BAND, D), like(CORNER, D), like(CORNER, D)),
        [vmem(TOKENS, D), vmem(TOKENS, D), vmem(BAND, D), vmem(*picks_shape), sems(4)],
        limit=24, name="edge_tokens",
    )
    band = lax.ppermute(band, "lat", [(0, 1), (1, 0)])
    corner_a = lax.ppermute(corner_a, ("lon", "lat"), across(side_a))
    corner_b = lax.ppermute(corner_b, ("lon", "lat"), across(side_b))
    edge_b = lax.ppermute(edge_b, "lon", side_b)
    edge_a = lax.ppermute(edge_a, "lon", side_a)

    quads, quads32 = like(STEPS, TOKENS, QUAD), like(STEPS, TOKENS, QUAD, dtype=F32)
    kv_like = like(STEPS, 2, TOKENS + BAND, QUAD)
    qhat_near, dout, wo_near, x_near, gain_near, qhat, rawq, rawk, kv = call(
        own_kernel,
        scalars(place, score_sharpness) + hbm(x, rim, up, gain, w3, wo),
        near(quads, quads, like(D, D), like(TOKENS, D), like(1, D, dtype=F32))
        + hbm(quads, quads32, quads32, kv_like),
        [vmem(STEPS, 2, TOKENS + BAND, QUAD), vmem(STEPS, D, 3 * QUAD), vmem(BAND, D), vmem(TOKENS, D),
         vmem(STEPS, TOKENS, QUAD, dtype=F32), vmem(STEPS, TOKENS, QUAD, dtype=F32), vmem(TOKENS + BAND, D), sems(4 + 4 * STEPS + 4 * STEPS)],
        limit=24, flops=2 * 1024 * 1024 * (192 * 2 + 288 * 2), name="own_projections",
    )

    kv_scratch = vmem(STEPS, 2, TOKENS + BAND, QUAD)
    stat_like, side_like = like(TOKENS, STATS, dtype=F32), like(SIDE, STATS, dtype=F32)
    mixed, stat_a, stat_b, halo_kv, stat, xn_halo, up_halo, weights, dprime = call(
        forward_kernel,
        scalars(place, flags) + hbm(keys, selection, w3, kv)
        + near(band, edge_a, edge_b, corner_a, corner_b, gain_near, qhat_near, dout),
        near(like(TOKENS, D), side_like, side_like)
        + hbm(like(STEPS, 2, HALO_ROWS, QUAD), stat_like, like(HALO_QUERIES, D), like(2 * SIDE, D),
              like(STEPS, 2, STACK, SPAN), quads),
        [vmem(1, 8, KEYS, dtype=jnp.int32), vmem(*picks_shape), vmem(STEPS, D, 2 * QUAD), kv_scratch, vmem(STEPS, 2, HALO_ROWS, QUAD),
         vmem(TOKENS, STATS, dtype=F32),
         vmem(HALO_ROWS, D), vmem(2 * SIDE, D), vmem(STEPS, 2, STACK, SPAN), vmem(STEPS, TOKENS, QUAD),
         vmem(2, HALF, SPAN, dtype=F32), vmem(2, KEYS, QUAD), vmem(2, KEYS, QUAD), vmem(STEPS, TOKENS, QUAD, dtype=F32),
         sems(2 + 3 * STEPS + 3 * STEPS + 3)],
        limit=24, flops=2 * 1024 * 1024 * 2000, name="attention_forward",
    )
    stat_b = lax.ppermute(stat_b, "lon", side_b)
    stat_a = lax.ppermute(stat_a, "lon", side_a)

    (going,) = call(
        output_kernel,
        scalars(place, column_group_decoder_longitude) + near(x_near, mixed, wo_near),
        hbm(like(count, cap, SEG, D)),
        [vmem(TOKENS, D, dtype=F32), vmem(count, cap, SEG, D), pltpu.SMEM((count,), jnp.int32), sems(1)],
        limit=24, flops=2 * 1024 * 1024 * 200, name="output_segments",
    )
    going, stat_a, stat_b = lax.optimization_barrier((going, stat_a, stat_b))
    arrived = lax.all_to_all(going, "lon", split_axis=0, concat_axis=0, tiled=True)

    (message,) = call(
        message_kernel,
        scalars(place) + hbm(up, up_halo, stat, stat_a, stat_b),
        near(like(PAD_SIDE, MESSAGE)),
        [vmem(BAND, D), vmem(2 * SIDE, D), vmem(BAND, STATS, dtype=F32), vmem(SIDE, STATS, dtype=F32), vmem(SIDE, STATS, dtype=F32),
         sems(5)],
        limit=24, flops=1024, name="boundary_message",
    )
    message = lax.ppermute(message, "lat", [(0, 1), (1, 0)])

    handed = call(
        query_kernel,
        scalars(place, score_sharpness, flags)
        + hbm(xn_halo, up_halo, keys, w3, wo, qhat, kv, halo_kv, weights, dprime, rawq, rawk, stat, stat_a, stat_b),
        near(like(TOKENS, D, dtype=F32), like(STEPS, SPAN, QUAD), like(STEPS, MIDDLE, QUAD), like(STEPS, 2, HALF, QUAD, dtype=F32),
             like(2, HALF, SPAN, dtype=F32), like(STEPS, 2, D, QUAD), like(D, D), kv_like, quads32, like(STATS, MIDDLE, dtype=F32)),
        [vmem(HALO_QUERIES, D), vmem(2 * SIDE, D), vmem(1, 8, KEYS, dtype=jnp.int32), vmem(STEPS, D, QUAD),
         vmem(STEPS, TOKENS, QUAD), vmem(STEPS, 2, HALO_ROWS, QUAD), vmem(STEPS, 2, STACK, SPAN), vmem(STEPS, TOKENS, QUAD),
         vmem(STEPS, TOKENS, QUAD, dtype=F32), vmem(TOKENS, STATS, dtype=F32), vmem(SIDE, STATS, dtype=F32),
         vmem(SIDE, STATS, dtype=F32), vmem(2, KEYS, QUAD), vmem(2, KEYS, QUAD), vmem(2, TOKENS, QUAD, dtype=F32),
         sems(6 + 8 * STEPS + 3 * STEPS)],
        limit=24, flops=2 * 1024 * 1024 * 4000, name="query_gradient",
    )

    (input_grad,) = call(
        key_kernel,
        scalars(place) + hbm(x, up, gain) + near(*handed, message),
        hbm(like(TOKENS, D)),
        [vmem(TOKENS, D), vmem(TOKENS, D), vmem(1, D, dtype=F32), vmem(TOKENS, D), vmem(STATS, SPAN, dtype=F32),
         vmem(2, SPAN, QUAD), vmem(2, TOKENS, QUAD, dtype=F32), vmem(2, TOKENS, QUAD, dtype=F32), vmem(TOKENS, D, dtype=F32), sems(4)],
        limit=24, flops=2 * 1024 * 1024 * 2000, name="key_gradient",
    )
    return (
        arrived.reshape(1, 1, count, cap, SEG, D),
        input_grad.reshape(ROWS, COLS, D),
    )


def solution(mesh):
    return jax.shard_map(
        per_device,
        mesh=mesh,
        in_specs=(
            P("lat", "lon", None),
            P("lat", "lon", None),
            P(None, None, "lon", None),
            P(),
            P(),
            P(),
            P(),
            P(),
            P("lat", "lon"),
        ),
        out_specs=(P("lat", "lon", None, None, None, None), P("lat", "lon", None)),
        check_vma=False,
    )
```

time: 76.3 us -> 64.7 us (0.85)
  Pallas kernels: 48.2 us -> 43.3 us
  starting transfers between devices: 21.6 us -> 18.1 us
  local copies, waits for them, and re-layouts: 2.65 us -> 1 us
    pallas_call x5 -> x7, Pallas kernels: 48.2 us -> 43.3 us  [call(): pl.pallas_call(kernel, in_specs=specs(inputs), out_specs=specs(outputs),...]
    ppermute x10 -> x8, starting transfers between devices: 17.9 us -> 13.8 us  [the longest x1 5.66 us: per_device(): edge_b = lax.ppermute(edge_b, 'lon', side_b)]
    unnamed x24 -> x12, local copies, waits for them, and re-layouts: 2.65 us -> 1 us
    ppermute x10 -> x8, waiting for transfers between devices: 1.88 us -> 1.13 us  [the longest x1 1.11 us: per_device(): stat_b = lax.ppermute(stat_b, 'lon', side_b)]
  transfers between devices with their start and end apart: 11 -> 9, of which waited for: 1 -> 1; matrix products, arithmetic and copies ran while one was open for 1% -> 0% of each run, Pallas kernels for 43% -> 46%
where the time goes in v2:
time: 64.7 us; the launch traced here: 64.4 us
  Pallas kernels  43.3 us (67%)
  starting transfers between devices  18.1 us (28%)
  waiting for transfers between devices  1.13 us (2%)
  local copies, waits for them, and re-layouts  1 us (2%)
  between operations  0.81 us (1%)
    pallas_call x7, Pallas kernels, call(): pl.pallas_call(kernel, in_specs=specs(inputs), out_specs=specs(outputs),...  43.3 us
    ppermute x1, starting transfers between devices, per_device(): edge_b = lax.ppermute(edge_b, 'lon', side_b)  5.66 us
    all_to_all x1, starting transfers between devices, per_device(): lax.all_to_all(going, 'lon', split_axis=0, concat_axis=0, tiled=True)  4.28 us
    ppermute x1, starting transfers between devices, per_device(): stat_b = lax.ppermute(stat_b, 'lon', side_b)  2.79 us
    ppermute x1, starting transfers between devices, per_device(): corner_b = lax.ppermute(corner_b, ('lon', 'lat'), across(side_b))  1.68 us
    ppermute x1, starting transfers between devices, per_device(): message = lax.ppermute(message, 'lat', [(0, 1), (1, 0)])  1.56 us
    ppermute x1, starting transfers between devices, per_device(): band = lax.ppermute(band, 'lat', [(0, 1), (1, 0)])  1.5 us
  transfers between devices with their start and end apart: 9, of which 1 were waited for; matrix products, arithmetic and copies ran while one was open for 0% of the time, Pallas kernels for 46%

profile of v2, /device:TPU:0, one launch (start us, length us, event | category | flops | bytes accessed | tf_op | source)
XLA Modules:
  0.0 64.4 jit_solution(11709921600004465076)
XLA Ops:
  0.6 0.0 copy-start
  0.7 0.1 pad_add_fusion.place_ref
  0.7 3.4 %edge_tokens.1 = (bf16[184,1024]{1,0:T(8,128)(2,1)}, bf16[184,1024]{1,0:T(8,128)(2,1)}, bf16[96,1024]{1,0:T(8,128)(2,1)}, bf16[40,1024]{1,0:T(8,128)(2,1)}, bf16[40,1024]{1,0:T(8,128)(2,1)}) custom-call(s32[2]{0:T(128)S(1)} %pad_add_fusion.place_ref, bf16[192,1024]{1,0:T(8,128)(2,1)} %bitcast.15, bf16[192,1024]{1,0:T(8,128)(2,1)} %bitcast.8, ...), custom_call_target="tpu_custom_call" | custom-call | bytes 8388608 | tf_op jit(solution)/shard_map/edge_tokens/pallas_call | solution.py:538
  4.1 0.5 collective-permute-start.1
  4.6 5.7 %collective-permute-start.2 = (bf16[184,1024]{1,0:T(8,128)(2,1)}, bf16[184,1024]{1,0:T(8,128)(2,1)}, u32[]{:S(2)}, u32[]{:S(2)}) collective-permute-start(bf16[184,1024]{1,0:T(8,128)(2,1)} %get-tuple-element.42), channel_id=1, source_target_pairs={{0,30},{2,4},{4,2},{6,8},{8,6},{10,12},{12,10},{14,16},{16,14},{18... | collective-permute-start | bytes 1130504 | tf_op jit(solution)/shard_map/ppermute | solution.py:613
  10.3 1.5 %collective-permute-start = (bf16[96,1024]{1,0:T(8,128)(2,1)}, bf16[96,1024]{1,0:T(8,128)(2,1)S(1)}, u32[]{:S(2)}, u32[]{:S(2)}) collective-permute-start(bf16[96,1024]{1,0:T(8,128)(2,1)} %get-tuple-element.40), channel_id=1, source_target_pairs={{0,1},{1,0},{2,3},{3,2},{4,5},{5,4},{6,7},{7,6},{8,9},{9,8},{10,11... | collective-permute-start | bytes 589832 | tf_op jit(solution)/shard_map/ppermute | solution.py:610
  11.8 0.0 collective-permute-start.3
  11.8 1.7 %collective-permute-start.4 = (bf16[40,1024]{1,0:T(8,128)(2,1)}, bf16[40,1024]{1,0:T(8,128)(2,1)}, u32[]{:S(2)}, u32[]{:S(2)}) collective-permute-start(bf16[40,1024]{1,0:T(8,128)(2,1)} %get-tuple-element.44), channel_id=1, source_target_pairs={{0,31},{1,30},{2,5},{3,4},{4,3},{5,2},{6,9},{7,8},{8,7},{9,6},{10,... | collective-permute-start | bytes 245768 | tf_op jit(solution)/shard_map/ppermute | solution.py:612
  13.5 0.0 copy-done
  13.5 0.0 copy-start.4
  13.5 0.0 copy-start.1
  13.5 7.1 %own_projections.1 = (bf16[4,192,256]{2,1,0:T(8,128)(2,1)S(1)}, bf16[4,192,256]{2,1,0:T(8,128)(2,1)S(1)}, bf16[1024,1024]{1,0:T(8,128)(2,1)S(1)}, bf16[192,1024]...) custom-call(s32[2]{0:T(128)S(1)} %pad_add_fusion.place_ref, ...), custom_call_target="tpu_custom_call" | custom-call | flops 2013265920 | bytes 8388608 | tf_op jit(solution)/shard_map/own_projections/pallas_call | solution.py:538
  20.6 0.0 copy-done.4
  20.6 0.1 copy.13.owner_ref
  20.7 0.0 collective-permute-done.3.corner_a_ref
  20.7 0.0 collective-permute-done.4.corner_b_ref
  20.7 0.0 collective-permute-done.band_ref
  20.8 0.0 collective-permute-done.1.edge_a_ref
  20.8 0.0 collective-permute-done.2.edge_b_ref
  20.8 0.0 copy-done.1
  20.8 10.0 %attention_forward.1 = (bf16[192,1024]{1,0:T(8,128)(2,1)S(1)}, f32[72,128]{1,0:T(8,128)S(1)}, f32[72,128]{1,0:T(8,128)S(1)}, bf16[4,2,400,256]{3,2,1,0:T(8,128)(...) custom-call(s32[2]{0:T(128)S(1)} %pad_add_fusion.place_ref, ...), custom_call_target="tpu_custom_call" | custom-call | flops 4194304000 | bytes 8388608 | tf_op jit(solution)/shard_map/attention_forward/pallas_call | solution.py:538
  30.8 0.1 collective-permute-start.5
  30.9 2.8 %collective-permute-start.6 = (f32[72,128]{1,0:T(8,128)S(1)}, f32[72,128]{1,0:T(8,128)S(1)}, u32[]{:S(2)}, u32[]{:S(2)}) collective-permute-start(f32[72,128]{1,0:T(8,128)S(1)} %get-tuple-element.51), channel_id=1, source_target_pairs={{0,30},{2,4},{4,2},{6,8},{8,6},{10,12},{12,10},{14,16},{16,14},{18... | collective-permute-start | bytes 110600 | tf_op jit(solution)/shard_map/ppermute | solution.py:644
  33.7 2.2 %output_segments.1 = bf16[16,6,4,1024]{3,2,1,0:T(4,128)(2,1)} custom-call(s32[2]{0:T(128)S(1)} %pad_add_fusion.place_ref, s32[12,4]{1,0:T(8,128)S(1)} %copy.13.owner_ref, bf16[192,1024]{1,0:T(8,128)(2,1)S(1)} %get-tuple-element.38.x_ref, bf16[192,1024]{1,0:T(8,128)(2,1)S(1)} %get-tuple-element.48.mixed_ref, bf16[1024,1024]{1,0:T(8,128)(2,1)S(1)} %get-tuple-element.49.wo_ref), custom_call_target="tpu_custom_call" | custom-call | flops 419430400 | bytes 8388608 | tf_op jit(solution)/shard_map/output_segments/pallas_call | solution.py:538
  35.9 0.0 collective-permute-done.5.stat_a_hbm
  35.9 0.0 copy-start.2
  35.9 1.1 %collective-permute-done.6.stat_b_hbm = f32[72,128]{1,0:T(8,128)S(1)} collective-permute-done((f32[72,128]{1,0:T(8,128)S(1)}, f32[72,128]{1,0:T(8,128)S(1)}, u32[]{:S(2)}, u32[]{:S(2)}) %collective-permute-start.6) | collective-permute-done | bytes 36896 | tf_op jit(solution)/shard_map/ppermute | solution.py:644
  37.0 0.0 copy-start.3
  37.0 4.3 %all-to-all-start = ((bf16[16,6,4,1024]{3,2,1,0:T(4,128)(2,1)}), bf16[16,6,4,1024]{3,2,1,0:T(4,128)(2,1)S(1)}, u32[]{:S(2)}, u32[]{:S(2)}) async-start(bf16[16,6,4,1024]{3,2,1,0:T(4,128)(2,1)} %output_segments.1), calls=%async_computation | async-start | bytes 1572864 | tf_op jit(solution)/shard_map/all_to_all | solution.py:655
  41.3 0.0 copy-done.2
  41.3 0.0 copy-done.3
  41.4 1.9 %boundary_message.1 = bf16[176,1280]{1,0:T(8,128)(2,1)S(1)} custom-call(s32[2]{0:T(128)S(1)} %pad_add_fusion.place_ref, bf16[192,1024]{1,0:T(8,128)(2,1)} %bitcast.10, bf16[144,1024]{1,0:T(8,128)(2,1)} %get-tuple-element.54.upn_hbm, f32[192,128]{1,0:T(8,128)} %get-tuple-element.61.stat_hbm, f32[72,128]{1,0:T(8,128)} %copy-done.2, f32[72,128]{1,0:T(8,128)} %copy-done.3), custom_call_target="tpu_custom_call" | custom-call | flops 1024 | bytes 8388608 | tf_op jit(solution)/shard_map/boundary_message/pallas_call | solution.py:538
  43.3 1.6 %collective-permute-start.7 = (bf16[176,1280]{1,0:T(8,128)(2,1)S(1)}, bf16[176,1280]{1,0:T(8,128)(2,1)S(1)}, u32[]{:S(2)}, u32[]{:S(2)}) collective-permute-start(bf16[176,1280]{1,0:T(8,128)(2,1)S(1)} %boundary_message.1), channel_id=1, source_target_pairs={{0,1},{1,0},{2,3},{3,2},{4,5},{5,4},{6,7},{7,6},{8,9},{9,8},{10,11... | collective-permute-start | bytes 1351688 | tf_op jit(solution)/shard_map/ppermute | solution.py:665
  44.8 11.5 %query_gradient.1 = (f32[192,1024]{1,0:T(8,128)S(1)}, bf16[4,512,256]{2,1,0:T(8,128)(2,1)S(1)}, bf16[4,336,256]{2,1,0:T(8,128)(2,1)S(1)}, f32[4,2,96,256]{3,2,1,...) custom-call(s32[2]{0:T(128)S(1)} %pad_add_fusion.place_ref, ...), custom_call_target="tpu_custom_call" | custom-call | flops 8388608000 | bytes 8388608 | tf_op jit(solution)/shard_map/query_gradient/pallas_call | solution.py:538
  56.3 0.0 collective-permute-done.7.message_ref
  56.3 7.2 %key_gradient.1 = bf16[192,1024]{1,0:T(8,128)(2,1)} custom-call(s32[2]{0:T(128)S(1)} %pad_add_fusion.place_ref, bf16[192,1024]{1,0:T(8,128)(2,1)} %bitcast.17, bf16[192,1024]{1,0:T(8,128)(2,1)} %bitcast.11, f32[1,1024]{1,0:T(1,128)} %bitcast.19, f32[192,1024]{1,0:T(8,128)S(1)} %get-tuple-element.64.gqn_ref, ...), custom_call_target="tpu_custom_call" | custom-call | flops 4194304000 | bytes 8388608 | tf_op jit(solution)/shard_map/key_gradient/pallas_call | solution.py:538
  63.5 0.0 all-to-all-done
  63.5 0.9 %copy.15 = bf16[1,1,16,6,4,1024]{5,4,3,2,1,0:T(4,128)(2,1)} copy(bf16[1,1,16,6,4,1024]{5,4,3,2,1,0:T(4,128)(2,1)S(1)} %bitcast.12) | data formatting | bytes 1572864
Async XLA Ops:
  0.6 12.8 %copy-start = (f32[16]{0:T(128)S(1)}, f32[16]{0:T(128)}, u32[]{:S(2)}) copy-start(f32[16]{0:T(128)} %sharp_ref.3) | copy-start | bytes 196
  4.1 16.6 %collective-permute-start.1 = (bf16[184,1024]{1,0:T(8,128)(2,1)}, bf16[184,1024]{1,0:T(8,128)(2,1)}, u32[]{:S(2)}, u32[]{:S(2)}) collective-permute-start(bf16[184,1024]{1,0:T(8,128)(2,1)} %get-tuple-element.41), channel_id=1, source_target_pairs={{0,2},{2,0},{4,6},{6,4},{8,10},{10,8},{12,14},{14,12},{16,18},{18,... | collective-permute-start | bytes 1130504 | tf_op jit(solution)/shard_map/ppermute | solution.py:614
  4.6 16.1 %collective-permute-start.2 = (bf16[184,1024]{1,0:T(8,128)(2,1)}, bf16[184,1024]{1,0:T(8,128)(2,1)}, u32[]{:S(2)}, u32[]{:S(2)}) collective-permute-start(bf16[184,1024]{1,0:T(8,128)(2,1)} %get-tuple-element.42), channel_id=1, source_target_pairs={{0,30},{2,4},{4,2},{6,8},{8,6},{10,12},{12,10},{14,16},{16,14},{18... | collective-permute-start | bytes 1130504 | tf_op jit(solution)/shard_map/ppermute | solution.py:613
  10.3 10.5 %collective-permute-start = (bf16[96,1024]{1,0:T(8,128)(2,1)}, bf16[96,1024]{1,0:T(8,128)(2,1)S(1)}, u32[]{:S(2)}, u32[]{:S(2)}) collective-permute-start(bf16[96,1024]{1,0:T(8,128)(2,1)} %get-tuple-element.40), channel_id=1, source_target_pairs={{0,1},{1,0},{2,3},{3,2},{4,5},{5,4},{6,7},{7,6},{8,9},{9,8},{10,11... | collective-permute-start | bytes 589832 | tf_op jit(solution)/shard_map/ppermute | solution.py:610
  11.8 9.0 %collective-permute-start.3 = (bf16[40,1024]{1,0:T(8,128)(2,1)}, bf16[40,1024]{1,0:T(8,128)(2,1)}, u32[]{:S(2)}, u32[]{:S(2)}) collective-permute-start(bf16[40,1024]{1,0:T(8,128)(2,1)} %get-tuple-element.43), channel_id=1, source_target_pairs={{0,3},{1,2},{2,1},{3,0},{4,7},{5,6},{6,5},{7,4},{8,11},{9,10},{10,... | collective-permute-start | bytes 245768 | tf_op jit(solution)/shard_map/ppermute | solution.py:611
  11.8 9.0 %collective-permute-start.4 = (bf16[40,1024]{1,0:T(8,128)(2,1)}, bf16[40,1024]{1,0:T(8,128)(2,1)}, u32[]{:S(2)}, u32[]{:S(2)}) collective-permute-start(bf16[40,1024]{1,0:T(8,128)(2,1)} %get-tuple-element.44), channel_id=1, source_target_pairs={{0,31},{1,30},{2,5},{3,4},{4,3},{5,2},{6,9},{7,8},{8,7},{9,6},{10,... | collective-permute-start | bytes 245768 | tf_op jit(solution)/shard_map/ppermute | solution.py:612
  13.5 7.2 %copy-start.4 = (s32[12,4]{0,1:T(4,128)S(1)}, s32[12,4]{0,1:T(4,128)}, u32[]{:S(2)}) copy-start(s32[12,4]{0,1:T(4,128)} %param.19) | copy-start | bytes 580
  13.5 7.3 %copy-start.1 = (s32[2,6]{1,0:T(2,128)S(1)}, s32[2,6]{1,0:T(2,128)}, u32[]{:S(2)}) copy-start(s32[2,6]{1,0:T(2,128)} %flag_ref.3) | copy-start | bytes 148
  30.8 5.1 %collective-permute-start.5 = (f32[72,128]{1,0:T(8,128)S(1)}, f32[72,128]{1,0:T(8,128)S(1)}, u32[]{:S(2)}, u32[]{:S(2)}) collective-permute-start(f32[72,128]{1,0:T(8,128)S(1)} %get-tuple-element.50), channel_id=1, source_target_pairs={{0,2},{2,0},{4,6},{6,4},{8,10},{10,8},{12,14},{14,12},{16,18},{18,... | collective-permute-start | bytes 110600 | tf_op jit(solution)/shard_map/ppermute | solution.py:645
  30.9 6.1 %collective-permute-start.6 = (f32[72,128]{1,0:T(8,128)S(1)}, f32[72,128]{1,0:T(8,128)S(1)}, u32[]{:S(2)}, u32[]{:S(2)}) collective-permute-start(f32[72,128]{1,0:T(8,128)S(1)} %get-tuple-element.51), channel_id=1, source_target_pairs={{0,30},{2,4},{4,2},{6,8},{8,6},{10,12},{12,10},{14,16},{16,14},{18... | collective-permute-start | bytes 110600 | tf_op jit(solution)/shard_map/ppermute | solution.py:644
  35.9 5.4 %copy-start.2 = (f32[72,128]{1,0:T(8,128)}, f32[72,128]{1,0:T(8,128)S(1)}, u32[]{:S(2)}) copy-start(f32[72,128]{1,0:T(8,128)S(1)} %collective-permute-done.5.stat_a_hbm) | copy-start | bytes 110596
  37.0 4.3 %copy-start.3 = (f32[72,128]{1,0:T(8,128)}, f32[72,128]{1,0:T(8,128)S(1)}, u32[]{:S(2)}) copy-start(f32[72,128]{1,0:T(8,128)S(1)} %collective-permute-done.6.stat_b_hbm) | copy-start | bytes 110596
  37.0 26.5 %all-to-all-start = ((bf16[16,6,4,1024]{3,2,1,0:T(4,128)(2,1)}), bf16[16,6,4,1024]{3,2,1,0:T(4,128)(2,1)S(1)}, u32[]{:S(2)}, u32[]{:S(2)}) async-start(bf16[16,6,4,1024]{3,2,1,0:T(4,128)(2,1)} %output_segments.1), calls=%async_computation | async-start | bytes 1572864 | tf_op jit(solution)/shard_map/all_to_all | solution.py:655
  43.3 13.1 %collective-permute-start.7 = (bf16[176,1280]{1,0:T(8,128)(2,1)S(1)}, bf16[176,1280]{1,0:T(8,128)(2,1)S(1)}, u32[]{:S(2)}, u32[]{:S(2)}) collective-permute-start(bf16[176,1280]{1,0:T(8,128)(2,1)S(1)} %boundary_message.1), channel_id=1, source_target_pairs={{0,1},{1,0},{2,3},{3,2},{4,5},{5,4},{6,7},{7,6},{8,9},{9,8},{10,11... | collective-permute-start | bytes 1351688 | tf_op jit(solution)/shard_map/ppermute | solution.py:665

commit v3 on v2

--- a/solution.py
+++ b/solution.py
@@ -54,6 +54,10 @@
     return COLS - HALO if side == parity else 0
 
 
+def inner_row(lat, row):
+    return (row + HALO * (1 - lat)) % ROWS
+
+
 def selection_table():
     table = np.zeros((4, 2 * EDGE + 2 * CORNER, TOKENS + BAND), np.float32)
     for lat in range(2):
@@ -63,11 +67,11 @@
                 picks = table[2 * lat + parity]
                 for c in range(HALO):
                     for r in range(ROWS):
-                        picks[base + r * HALO + c, r * COLS + first + c] = 1
+                        picks[base + r * HALO + c, inner_row(lat, r) * COLS + first + c] = 1
                     for i in range(HALO):
                         picks[base + SIDE + i * HALO + c, TOKENS + i * COLS + first + c] = 1
                         row = i + HALO * (1 - lat)
-                        picks[2 * EDGE + side * CORNER + i * HALO + c, row * COLS + first + c] = 1
+                        picks[2 * EDGE + side * CORNER + i * HALO + c, inner_row(lat, row) * COLS + first + c] = 1
     return table
 
 
@@ -89,6 +93,7 @@
 
             put(0, HALO, COLS, 0, "lat")
             put(PAD_SIDE, ROWS, COLS, 0, "own")
+            picks[0, PAD_SIDE : PAD_SIDE + TOKENS] = np.repeat([r for _, r in sorted((inner_row(lat, r), r) for r in range(ROWS))], COLS)
             put(SPAN, HALO, COLS, 0, "rim")
             for side in range(2):
                 col = COLS if side == parity else -HALO
@@ -115,6 +120,7 @@
 
 
 def unit_back(raw, grad):
+    raw = raw.astype(F32)
     inverse = lax.rsqrt(head_mean(raw * raw) + 1e-06)
     value = raw * inverse
     return inverse * (grad - value * head_mean(value * grad))
@@ -167,6 +173,11 @@
     picks = jnp.where(a == b // HEAD_DIM + j * QUAD_HEADS, 1.0, 0.0).astype(BF)
     high, low = halves(stat)
     return dot(high, picks) + dot(low, picks)
+
+
+def where():
+    lat = lax.axis_index("lat")
+    return lat, 2 * lat + lax.axis_index("lon") % 2
 
 
 def half_start(lat, half):
@@ -205,6 +216,12 @@
         copy.start()
         return copy
 
+    def load_tokens(self, hbm, ref, lat):
+        return [self.start(hbm.at[pl.ds(half_start(lat, k), HALF)], ref.at[pl.ds(k * HALF, HALF)]) for k in range(2)]
+
+    def store_tokens(self, ref, hbm, lat):
+        return [self.start(ref.at[pl.ds(k * HALF, HALF)], hbm.at[pl.ds(half_start(lat, k), HALF)]) for k in range(2)]
+
     def by_step(self, pairs):
         base, width = self.used, len(pairs(0))
         self.used += STEPS * width
@@ -237,19 +254,16 @@
 
 
 def pack_kernel(
-    place_ref, x_hbm, up_hbm, rim_hbm, sel_hbm, edge_a_ref, edge_b_ref, band_ref, corner_a_ref, corner_b_ref,
+    x_hbm, up_hbm, rim_hbm, sel_hbm, edge_a_ref, edge_b_ref, band_ref, corner_a_ref, corner_b_ref,
     x_ref, up_ref, rim_ref, sel_ref, sems,
 ):
-    lat = place_ref[0]
+    lat, spot = where()
     copies = Copies(sems)
-    loads = [
-        copies.start(x_hbm, x_ref),
-        copies.start(sel_hbm.at[2 * lat + place_ref[1]], sel_ref),
-        copies.start(rim_hbm.at[lat], rim_ref),
-        copies.start(up_hbm, up_ref),
-    ]
+    loads = copies.load_tokens(x_hbm, x_ref, lat)
+    loads += [copies.start(sel_hbm.at[spot], sel_ref), copies.start(rim_hbm.at[lat], rim_ref)]
+    loads += copies.load_tokens(up_hbm, up_ref, lat)
     wait_all(loads)
-    band_ref[...] = x_ref[pl.ds(half_start(lat, 0), BAND), :]
+    band_ref[...] = x_ref[:BAND]
     picks = sel_ref[...]
     features = dot(picks, jnp.concatenate([x_ref[...], rim_ref[...]], axis=0))
     grads = dot(picks[: 2 * EDGE, :TOKENS], up_ref[...])
@@ -261,63 +275,64 @@
 
 
 def own_kernel(
-    place_ref, sharp_ref, x_hbm, rim_hbm, up_hbm, gain_hbm, w3_hbm, wo_hbm,
+    sharp_ref, x_hbm, rim_hbm, up_hbm, gain_hbm, w3_hbm, wo_hbm,
     qhat_ref, dout_ref, wo_ref, x_ref, gain_ref, qhat_hbm, rawq_hbm, rawk_hbm, kv_hbm,
     kv_ref, w3_ref, rim_ref, up_ref, rawq_ref, rawk_ref, xn_ref, sems,
 ):
     copies = Copies(sems)
-    loads = [copies.start(x_hbm, x_ref), copies.start(rim_hbm.at[place_ref[0]], rim_ref), copies.start(gain_hbm, gain_ref)]
+    lat, spot = where()
+    loads = copies.load_tokens(x_hbm, x_ref, lat) + [copies.start(rim_hbm.at[lat], rim_ref), copies.start(gain_hbm, gain_ref)]
     start, wait = copies.by_step(
         lambda j: [(w3_hbm.at[:, lane_block(k * STEPS, j)], w3_ref.at[j, :, pl.ds(k * QUAD, QUAD)]) for k in range(3)]
-        + [(wo_hbm.at[rows_at(j)], wo_ref.at[rows_at(j)])]
-    )
-    start(0)
-    up_load = copies.start(up_hbm, up_ref)
-    for j in range(1, STEPS):
+    )
+    grad_loads = copies.load_tokens(up_hbm, up_ref, lat) + [copies.start(wo_hbm, wo_ref)]
+    for j in range(STEPS):
         start(j)
     outputs = [(qhat_ref, qhat_hbm), (rawq_ref, rawq_hbm), (rawk_ref, rawk_hbm), (kv_ref, kv_hbm)]
     store, stored = copies.by_step(lambda j: [(ref.at[j], hbm.at[j]) for ref, hbm in outputs])
     wait_all(loads)
     xn_ref[:TOKENS] = normed(x_ref[...], gain_ref[...]).astype(BF)
     xn_ref[TOKENS:] = normed(rim_ref[...], gain_ref[...]).astype(BF)
+    wait_all(grad_loads)
+    dout = dot_nt(up_ref[...], wo_ref[...]).astype(BF)
+    for j in range(STEPS):
+        dout_ref[j] = dout[:, j * QUAD : (j + 1) * QUAD]
     for j in range(STEPS):
         wait(j)
         raw = dot(xn_ref[...], w3_ref[j])
         raw_q, raw_k = raw[:TOKENS, :QUAD], raw[:, QUAD : 2 * QUAD]
         units = unit(jnp.concatenate([raw_q, raw_k], axis=0))
-        rawq_ref[j] = raw_q
-        rawk_ref[j] = raw_k[:TOKENS]
+        rawq_ref[j] = raw_q.astype(BF)
+        rawk_ref[j] = raw_k[:TOKENS].astype(BF)
         qhat_ref[j] = (units[:TOKENS] * multiplier(sharp_ref, j)).astype(BF)
         kv_ref[j, 0] = units[TOKENS:].astype(BF)
         kv_ref[j, 1] = raw[:, 2 * QUAD :].astype(BF)
         store(j)
-        if j == 0:
-            up_load.wait()
-        dout_ref[j] = dot_nt(up_ref[...], wo_ref[rows_at(j)]).astype(BF)
     for j in range(STEPS):
         stored(j)
 
 
 def forward_kernel(
-    place_ref, flag_ref, tab_hbm, sel_hbm, w3_hbm, kv_hbm, band_ref, edge_a_ref, edge_b_ref, corner_a_ref, corner_b_ref, gain_ref,
+    flag_ref, tab_hbm, sel_hbm, w3_hbm, kv_hbm, band_ref, edge_a_ref, edge_b_ref, corner_a_ref, corner_b_ref, gain_ref,
     qhat_ref, dout_ref,
     mixed_ref, stat_a_ref, stat_b_ref, halo_hbm, stat_hbm, xn_hbm, upn_hbm, weight_hbm, dprime_hbm,
     tab_ref, sel_ref, wkv_ref, kv_ref, halo_ref, stat_ref, xn_ref, upn_ref, weight_ref, dprime_ref, mask_ref, key_ref, value_ref, linv_ref, sems,
 ):
-    lat = place_ref[0]
-    spot = 2 * lat + place_ref[1]
+    lat, spot = where()
     copies = Copies(sems)
     loads = [copies.start(tab_hbm.at[spot], tab_ref.at[0])]
     start, wait = copies.by_step(
         lambda j: [(w3_hbm.at[:, lane_block(k * STEPS, j)], wkv_ref.at[j, :, pl.ds((k - 1) * QUAD, QUAD)]) for k in (1, 2)]
-        + [(kv_hbm.at[j], kv_ref.at[j])]
-    )
+    )
+    start_kv, wait_kv = copies.by_step(lambda j: [(kv_hbm.at[j], kv_ref.at[j])])
     for j in range(STEPS):
         start(j)
+        start_kv(j)
     loads.append(copies.start(sel_hbm.at[spot], sel_ref))
     store, stored = copies.by_step(
-        lambda j: [(halo_ref.at[j], halo_hbm.at[j]), (weight_ref.at[j], weight_hbm.at[j]), (dprime_ref.at[j], dprime_hbm.at[j])]
-    )
+        lambda j: [(halo_ref.at[j], halo_hbm.at[j]), (dprime_ref.at[j], dprime_hbm.at[j])]
+    )
+    weight_stores = []
     gain = gain_ref[...]
     edge_a, edge_b = edge_a_ref[...].astype(F32), edge_b_ref[...].astype(F32)
     pieces = [ref[...].astype(F32) for ref in (band_ref, corner_a_ref, corner_b_ref)]
@@ -335,15 +350,17 @@
         halo_v = raw[:, QUAD:].astype(BF)
         halo_ref[j, 0] = halo_k
         halo_ref[j, 1] = halo_v
+        wait_kv(j)
         lay_keys(key_ref.at[j % 2], kv_ref[j, 0], halo_k)
         lay_keys(value_ref.at[j % 2], kv_ref[j, 1], halo_v)
         for half in range(2):
-            at, piece = half * PAD_SIDE, pl.ds(half_start(lat, half), HALF)
+            at, piece = half * PAD_SIDE, slice(half * HALF, (half + 1) * HALF)
             scores = dot_nt(stacked(qhat_ref[j, piece, :]), key_ref[j % 2, at : at + SPAN])
             weights = jnp.exp(scores) * repeated(mask_ref[half])
             inverse = jnp.broadcast_to(1.0 / jnp.sum(weights, axis=-1, keepdims=True), (STACK, QUAD))
             weights = weights.astype(BF)
             weight_ref[j, half] = weights
+            weight_stores.append(copies.start(weight_ref.at[j, half], weight_hbm.at[j, half]))
             mixed = unstacked(dot(weights, value_ref[j % 2, at : at + SPAN]) * inverse)
             mixed_ref[piece, rows_at(j)] = mixed.astype(BF)
             linv_ref[j, piece, :] = unstacked(inverse)
@@ -364,11 +381,14 @@
     stat_b_ref[...] = picked[EDGE : EDGE + SIDE]
     for j in range(STEPS):
         stored(j)
-    wait_all(stores)
-
-
-def output_kernel(place_ref, owner_ref, x_ref, mixed_ref, wo_ref, going_hbm, acc_ref, going_ref, count_ref, sems):
-    acc_ref[...] = x_ref[...].astype(F32) + dot(mixed_ref[...], wo_ref[...])
+    wait_all(stores + weight_stores)
+
+
+def output_kernel(owner_ref, x_ref, mixed_ref, wo_ref, going_hbm, acc_ref, going_ref, count_ref, sems):
+    lat, spot = where()
+    rows = x_ref[...].astype(F32) + dot(mixed_ref[...], wo_ref[...])
+    for half in range(2):
+        acc_ref[pl.ds(half_start(lat, half), HALF), :] = rows[half * HALF : (half + 1) * HALF]
     going_ref[...] = jnp.zeros_like(going_ref)
     for o in range(going_ref.shape[0]):
         count_ref[o] = 0
@@ -381,16 +401,16 @@
 
 
 def message_kernel(
-    place_ref, up_hbm, upn_hbm, stat_hbm, stat_a_hbm, stat_b_hbm, out_ref, up_ref, upn_ref, stat_ref, stat_a_ref, stat_b_ref, sems
+    up_hbm, upn_hbm, stat_hbm, stat_a_hbm, stat_b_hbm, out_ref, up_ref, upn_ref, stat_ref, stat_a_ref, stat_b_ref, sems
 ):
-    lat = place_ref[0]
+    lat, spot = where()
     piece = pl.ds(half_start(lat, 0), BAND)
     copies = Copies(sems)
     wait_all(
         [
             copies.start(hbm, ref)
             for hbm, ref in (
-                (up_hbm.at[piece], up_ref), (upn_hbm, upn_ref), (stat_hbm.at[piece], stat_ref), (stat_a_hbm, stat_a_ref),
+                (up_hbm.at[piece], up_ref), (upn_hbm, upn_ref), (stat_hbm.at[pl.ds(0, BAND)], stat_ref), (stat_a_hbm, stat_a_ref),
                 (stat_b_hbm, stat_b_ref),
             )
         ]
@@ -423,109 +443,110 @@
 
 
 def query_kernel(
-    place_ref, sharp_ref, flag_ref, xn_hbm, upn_hbm, tab_hbm, w3_hbm, wo_hbm, qhat_hbm, kv_hbm, halo_hbm, weight_hbm, dprime_hbm,
+    sharp_ref, flag_ref, xn_hbm, upn_hbm, tab_hbm, w3_hbm, wo_hbm, qhat_hbm, kv_hbm, halo_hbm, weight_hbm, dprime_hbm,
     rawq_hbm, rawk_hbm, stat_hbm, stat_a_hbm, stat_b_hbm,
-    gqn_ref, query_ref, grad_ref, far_ref, mask_ref, wkv_ref, wo_ref, kv_ref, rawk_ref, row_ref,
+    gqn_ref, query_ref, grad_ref, far_ref, mask_ref, wk_ref, wv_ref, wo_ref, kv_ref, rawk_ref, row_ref,
     xn_ref, upn_ref, tab_ref, wq_ref, qhat_ref, halo_ref, weight_ref, dprime_ref, rawq_ref, stat_ref, stat_a_ref, stat_b_ref,
-    key_ref, value_ref, dq_ref, sems,
+    key_ref, value_ref, dq_ref, raw_ref, dout_ref, grad_q_ref, sems,
 ):
-    lat = place_ref[0]
+    lat, spot = where()
     copies = Copies(sems)
-    loads = [
-        copies.start(hbm, ref)
-        for hbm, ref in (
-            (xn_hbm, xn_ref), (upn_hbm, upn_ref), (stat_hbm, stat_ref), (stat_a_hbm, stat_a_ref), (stat_b_hbm, stat_b_ref),
-            (tab_hbm.at[2 * lat + place_ref[1]], tab_ref.at[0]),
-        )
-    ]
+    first = [copies.start(xn_hbm, xn_ref), copies.start(w3_hbm.at[:, pl.ds(0, D)], wq_ref)]
+    second = [copies.start(upn_hbm, upn_ref), copies.start(wo_hbm, wo_ref)]
     start, wait = copies.by_step(
         lambda j: [
-            (w3_hbm.at[:, lane_block(0, j)], wq_ref.at[j]),
-            (wo_hbm.at[rows_at(j)], wo_ref.at[rows_at(j)]),
             (qhat_hbm.at[j], qhat_ref.at[j]),
+            (dprime_hbm.at[j], dprime_ref.at[j]),
             (kv_hbm.at[j], kv_ref.at[j]),
             (halo_hbm.at[j], halo_ref.at[j]),
-            (dprime_hbm.at[j], dprime_ref.at[j]),
             (weight_hbm.at[j], weight_ref.at[j]),
             (rawq_hbm.at[j], rawq_ref.at[j]),
         ]
     )
-    start_later, wait_later = copies.by_step(
-        lambda j: [
-            (rawk_hbm.at[j], rawk_ref.at[j]),
-            (w3_hbm.at[:, lane_block(STEPS, j)], wkv_ref.at[j, 0]),
-            (w3_hbm.at[:, lane_block(2 * STEPS, j)], wkv_ref.at[j, 1]),
-        ]
-    )
-    for j in range(STEPS):
+    start(0)
+    third = [
+        copies.start(hbm, ref)
+        for hbm, ref in (
+            (stat_hbm, stat_ref), (stat_a_hbm, stat_a_ref), (stat_b_hbm, stat_b_ref), (tab_hbm.at[spot], tab_ref.at[0]),
+        )
+    ]
+    for j in range(1, STEPS):
         start(j)
-    for j in range(STEPS):
-        start_later(j)
-    wait_all(loads)
+    later = [
+        copies.start(rawk_hbm, rawk_ref),
+        copies.start(w3_hbm.at[:, pl.ds(D, D)], wk_ref),
+        copies.start(w3_hbm.at[:, pl.ds(2 * D, D)], wv_ref),
+    ]
+    wait_all(first)
+    raw_ref[...] = dot(xn_ref[...], wq_ref[...])
+    wait_all(second)
+    dout_ref[...] = dot_nt(upn_ref[...], wo_ref[...]).astype(BF)
+    wait_all(third)
     near_mask(mask_ref, tab_ref, flag_ref, lat)
     edges = jnp.concatenate([stat_a_ref[...], stat_b_ref[...]], axis=0)
     row_ref[...] = jnp.concatenate([stat_ref[...], edges], axis=0).T
-    gqn_ref[...] = jnp.zeros_like(gqn_ref)
-    for j in range(STEPS):
+    for j in range(STEPS):
+        halo_q = (unit(raw_ref[:, rows_at(j)]) * multiplier(sharp_ref, j)).astype(BF)
+        query_ref[j, :PAD_SIDE] = halo_q[:PAD_SIDE]
+        query_ref[j, PAD_SIDE + TOKENS :] = halo_q[PAD_SIDE:]
+        grad_ref[j, TOKENS:] = (dout_ref[:, rows_at(j)].astype(F32) * spread(edges, j)).astype(BF)
         wait(j)
+        query_ref[j, PAD_SIDE : PAD_SIDE + TOKENS] = qhat_ref[j]
+        grad_ref[j, :TOKENS] = dprime_ref[j]
         lay_keys(key_ref.at[j % 2], kv_ref[j, 0], halo_ref[j, 0])
         lay_keys(value_ref.at[j % 2], kv_ref[j, 1], halo_ref[j, 1])
-        halo_q = (unit(dot(xn_ref[...], wq_ref[j])) * multiplier(sharp_ref, j)).astype(BF)
-        query_ref[j, :PAD_SIDE] = halo_q[:PAD_SIDE]
-        query_ref[j, PAD_SIDE : PAD_SIDE + TOKENS] = qhat_ref[j]
-        query_ref[j, PAD_SIDE + TOKENS :] = halo_q[PAD_SIDE:]
-        grad_ref[j, :TOKENS] = dprime_ref[j]
-        grad_ref[j, TOKENS:] = (dot_nt(upn_ref[...], wo_ref[rows_at(j)]) * spread(edges, j)).astype(BF)
         for half in range(2):
-            at, piece = half * PAD_SIDE, pl.ds(half_start(lat, half), HALF)
+            at, piece = half * PAD_SIDE, slice(half * HALF, (half + 1) * HALF)
             stat = stat_ref[piece, :]
             lane = HEADS + j * QUAD_HEADS
             inner = jnp.concatenate([stat[:, lane + h : lane + h + 1] for h in range(QUAD_HEADS)], axis=0)
             grad_probs = dot_nt(stacked(dprime_ref[j, piece, :]), value_ref[j % 2, at : at + SPAN])
             grad_scores = weight_ref[j, half].astype(F32) * (grad_probs - inner)
             dq_ref[j % 2, piece, :] = unstacked(dot(grad_scores.astype(BF), key_ref[j % 2, at : at + SPAN]))
-        piece = pl.ds(half_start(lat, 1), HALF)
+        piece = slice(HALF, TOKENS)
         far_ref[j, 0], far_ref[j, 1] = key_pass(
             kv_ref[j, 0, piece, :], kv_ref[j, 1, piece, :], query_ref[j, PAD_SIDE:], grad_ref[j], mask_ref[1, :, :MIDDLE],
             inner_rows(row_ref, j),
         )
-        grad_q = unit_back(rawq_ref[j], dq_ref[j % 2] * multiplier(sharp_ref, j)).astype(BF)
-        gqn_ref[...] += dot_nt(grad_q, wq_ref[j])
-    for j in range(STEPS):
-        wait_later(j)
+        grad_q = unit_back(rawq_ref[j], dq_ref[j % 2] * multiplier(sharp_ref, j))
+        grad_q_ref[:, rows_at(j)] = grad_q.astype(BF)
+    gqn_ref[...] = dot_nt(grad_q_ref[...], wq_ref[...])
+    wait_all(later)
 
 
 def key_kernel(
-    place_ref, x_hbm, up_hbm, gain_hbm, gqn_ref, query_ref, grad_ref, far_ref, mask_ref, wkv_ref, wo_ref, kv_ref, rawk_ref, row_ref,
+    x_hbm, up_hbm, gain_hbm, gqn_ref, query_ref, grad_ref, far_ref, mask_ref, wk_ref, wv_ref, wo_ref, kv_ref, rawk_ref, row_ref,
     message_ref,
     out_hbm,
-    x_ref, up_ref, gain_ref, out_ref, all_row_ref, all_ref, dk_ref, dv_ref, acc_ref, sems,
+    x_ref, up_ref, gain_ref, out_ref, all_row_ref, all_ref, dk_ref, dout_ref, grad_k_ref, grad_v_ref, sems,
 ):
-    lat = place_ref[0]
+    lat, spot = where()
     copies = Copies(sems)
-    loads = [copies.start(x_hbm, x_ref), copies.start(up_hbm, up_ref), copies.start(gain_hbm, gain_ref)]
+    loads = copies.load_tokens(x_hbm, x_ref, lat) + copies.load_tokens(up_hbm, up_ref, lat)
+    loads.append(copies.start(gain_hbm, gain_ref))
     message = message_ref[:, D : D + STATS].astype(F32) + message_ref[:, D + STATS :].astype(F32)
     all_row_ref[...] = jnp.concatenate([message.T, row_ref[...]], axis=1)
-    acc_ref[...] = gqn_ref[...]
+    dout_ref[...] = dot_nt(message_ref[:, :D], wo_ref[...]).astype(BF)
     for j in range(STEPS):
         slot = j % 2
-        all_ref[slot, :PAD_SIDE] = (dot_nt(message_ref[:, :D], wo_ref[rows_at(j)]) * spread(message, j)).astype(BF)
+        all_ref[slot, :PAD_SIDE] = (dout_ref[:, rows_at(j)].astype(F32) * spread(message, j)).astype(BF)
         all_ref[slot, PAD_SIDE:] = grad_ref[j]
-        near, far = pl.ds(half_start(lat, 0), HALF), pl.ds(half_start(lat, 1), HALF)
-        dk_ref[slot, near, :], dv_ref[slot, near, :] = key_pass(
-            kv_ref[j, 0, near, :], kv_ref[j, 1, near, :], query_ref[j], all_ref[slot], mask_ref[0], inner_rows(all_row_ref, j)
+        dk_ref[slot, :HALF, :], near_dv = key_pass(
+            kv_ref[j, 0, :HALF, :], kv_ref[j, 1, :HALF, :], query_ref[j], all_ref[slot], mask_ref[0], inner_rows(all_row_ref, j)
         )
-        dk_ref[slot, far, :], dv_ref[slot, far, :] = far_ref[j, 0], far_ref[j, 1]
-        grad_k = unit_back(rawk_ref[j], dk_ref[slot]).astype(BF)
-        acc_ref[...] += dot_nt(grad_k, wkv_ref[j, 0]) + dot_nt(dv_ref[slot].astype(BF), wkv_ref[j, 1])
+        dk_ref[slot, HALF:, :] = far_ref[j, 0]
+        grad_k_ref[:, rows_at(j)] = unit_back(rawk_ref[j], dk_ref[slot]).astype(BF)
+        grad_v_ref[:HALF, rows_at(j)] = near_dv.astype(BF)
+        grad_v_ref[HALF:, rows_at(j)] = far_ref[j, 1].astype(BF)
+    total = gqn_ref[...] + dot_nt(grad_k_ref[...], wk_ref[...]) + dot_nt(grad_v_ref[...], wv_ref[...])
     wait_all(loads)
     tokens = x_ref[...].astype(F32)
     inverse = lax.rsqrt(jnp.mean(tokens * tokens, axis=-1, keepdims=True) + 1e-05)
-    grad = acc_ref[...] * gain_ref[...]
+    grad = total * gain_ref[...]
     value = tokens * inverse
     back = inverse * (grad - value * jnp.mean(value * grad, axis=-1, keepdims=True))
     out_ref[...] = (up_ref[...].astype(F32) + back).astype(BF)
-    copies.start(out_ref, out_hbm).wait()
+    wait_all(copies.store_tokens(out_ref, out_hbm, lat))
 
 
 def call(kernel, inputs, outputs, scratch=(), limit=32, flops=0, name=None):
@@ -580,7 +601,6 @@
 ):
     count = lax.axis_size("lon")
     cap = max(2, (2 * (TOKENS // SEG) + count - 1) // count)
-    place = jnp.stack([lax.axis_index("lat"), lax.axis_index("lon") % 2]).astype(jnp.int32)
     x = slab_features.reshape(TOKENS, D)
     up = upstream_gradient.reshape(TOKENS, D)
     rim = rim_feature_rows.reshape(2, BAND, D)
@@ -602,9 +622,9 @@
     picks_shape = table.shape[1:]
     edge_a, edge_b, band, corner_a, corner_b = call(
         pack_kernel,
-        scalars(place) + hbm(x, up, rim, selection),
+        hbm(x, up, rim, selection),
         near(like(EDGE + SIDE, D), like(EDGE + SIDE, D), like(BAND, D), like(CORNER, D), like(CORNER, D)),
-        [vmem(TOKENS, D), vmem(TOKENS, D), vmem(BAND, D), vmem(*picks_shape), sems(4)],
+        [vmem(TOKENS, D), vmem(TOKENS, D), vmem(BAND, D), vmem(*picks_shape), sems(6)],
         limit=24, name="edge_tokens",
     )
     band = lax.ppermute(band, "lat", [(0, 1), (1, 0)])
@@ -613,15 +633,15 @@
     edge_b = lax.ppermute(edge_b, "lon", side_b)
     edge_a = lax.ppermute(edge_a, "lon", side_a)
 
-    quads, quads32 = like(STEPS, TOKENS, QUAD), like(STEPS, TOKENS, QUAD, dtype=F32)
+    quads = like(STEPS, TOKENS, QUAD)
     kv_like = like(STEPS, 2, TOKENS + BAND, QUAD)
     qhat_near, dout, wo_near, x_near, gain_near, qhat, rawq, rawk, kv = call(
         own_kernel,
-        scalars(place, score_sharpness) + hbm(x, rim, up, gain, w3, wo),
+        scalars(score_sharpness) + hbm(x, rim, up, gain, w3, wo),
         near(quads, quads, like(D, D), like(TOKENS, D), like(1, D, dtype=F32))
-        + hbm(quads, quads32, quads32, kv_like),
+        + hbm(quads, quads, quads, kv_like),
         [vmem(STEPS, 2, TOKENS + BAND, QUAD), vmem(STEPS, D, 3 * QUAD), vmem(BAND, D), vmem(TOKENS, D),
-         vmem(STEPS, TOKENS, QUAD, dtype=F32), vmem(STEPS, TOKENS, QUAD, dtype=F32), vmem(TOKENS + BAND, D), sems(4 + 4 * STEPS + 4 * STEPS)],
+         vmem(STEPS, TOKENS, QUAD), vmem(STEPS, TOKENS, QUAD), vmem(TOKENS + BAND, D), sems(6 + 4 * STEPS + 4 * STEPS)],
         limit=24, flops=2 * 1024 * 1024 * (192 * 2 + 288 * 2), name="own_projections",
     )
 
@@ -629,7 +649,7 @@
     stat_like, side_like = like(TOKENS, STATS, dtype=F32), like(SIDE, STATS, dtype=F32)
     mixed, stat_a, stat_b, halo_kv, stat, xn_halo, up_halo, weights, dprime = call(
         forward_kernel,
-        scalars(place, flags) + hbm(keys, selection, w3, kv)
+        scalars(flags) + hbm(keys, selection, w3, kv)
         + near(band, edge_a, edge_b, corner_a, corner_b, gain_near, qhat_near, dout),
         near(like(TOKENS, D), side_like, side_like)
         + hbm(like(STEPS, 2, HALO_ROWS, QUAD), stat_like, like(HALO_QUERIES, D), like(2 * SIDE, D),
@@ -638,7 +658,7 @@
          vmem(TOKENS, STATS, dtype=F32),
          vmem(HALO_ROWS, D), vmem(2 * SIDE, D), vmem(STEPS, 2, STACK, SPAN), vmem(STEPS, TOKENS, QUAD),
          vmem(2, HALF, SPAN, dtype=F32), vmem(2, KEYS, QUAD), vmem(2, KEYS, QUAD), vmem(STEPS, TOKENS, QUAD, dtype=F32),
-         sems(2 + 3 * STEPS + 3 * STEPS + 3)],
+         sems(2 + 3 * STEPS + 4 * STEPS + 3)],
         limit=24, flops=2 * 1024 * 1024 * 2000, name="attention_forward",
     )
     stat_b = lax.ppermute(stat_b, "lon", side_b)
@@ -646,7 +666,7 @@
 
     (going,) = call(
         output_kernel,
-        scalars(place, column_group_decoder_longitude) + near(x_near, mixed, wo_near),
+        scalars(column_group_decoder_longitude) + near(x_near, mixed, wo_near),
         hbm(like(count, cap, SEG, D)),
         [vmem(TOKENS, D, dtype=F32), vmem(count, cap, SEG, D), pltpu.SMEM((count,), jnp.int32), sems(1)],
         limit=24, flops=2 * 1024 * 1024 * 200, name="output_segments",
@@ -656,7 +676,7 @@
 
     (message,) = call(
         message_kernel,
-        scalars(place) + hbm(up, up_halo, stat, stat_a, stat_b),
+        hbm(up, up_halo, stat, stat_a, stat_b),
         near(like(PAD_SIDE, MESSAGE)),
         [vmem(BAND, D), vmem(2 * SIDE, D), vmem(BAND, STATS, dtype=F32), vmem(SIDE, STATS, dtype=F32), vmem(SIDE, STATS, dtype=F32),
          sems(5)],
@@ -666,24 +686,24 @@
 
     handed = call(
         query_kernel,
-        scalars(place, score_sharpness, flags)
+        scalars(score_sharpness, flags)
         + hbm(xn_halo, up_halo, keys, w3, wo, qhat, kv, halo_kv, weights, dprime, rawq, rawk, stat, stat_a, stat_b),
         near(like(TOKENS, D, dtype=F32), like(STEPS, SPAN, QUAD), like(STEPS, MIDDLE, QUAD), like(STEPS, 2, HALF, QUAD, dtype=F32),
-             like(2, HALF, SPAN, dtype=F32), like(STEPS, 2, D, QUAD), like(D, D), kv_like, quads32, like(STATS, MIDDLE, dtype=F32)),
-        [vmem(HALO_QUERIES, D), vmem(2 * SIDE, D), vmem(1, 8, KEYS, dtype=jnp.int32), vmem(STEPS, D, QUAD),
+             like(2, HALF, SPAN, dtype=F32), like(D, D), like(D, D), like(D, D), kv_like, quads, like(STATS, MIDDLE, dtype=F32)),
+        [vmem(HALO_QUERIES, D), vmem(2 * SIDE, D), vmem(1, 8, KEYS, dtype=jnp.int32), vmem(D, D),
          vmem(STEPS, TOKENS, QUAD), vmem(STEPS, 2, HALO_ROWS, QUAD), vmem(STEPS, 2, STACK, SPAN), vmem(STEPS, TOKENS, QUAD),
-         vmem(STEPS, TOKENS, QUAD, dtype=F32), vmem(TOKENS, STATS, dtype=F32), vmem(SIDE, STATS, dtype=F32),
+         vmem(STEPS, TOKENS, QUAD), vmem(TOKENS, STATS, dtype=F32), vmem(SIDE, STATS, dtype=F32),
          vmem(SIDE, STATS, dtype=F32), vmem(2, KEYS, QUAD), vmem(2, KEYS, QUAD), vmem(2, TOKENS, QUAD, dtype=F32),
-         sems(6 + 8 * STEPS + 3 * STEPS)],
+         vmem(HALO_QUERIES, D, dtype=F32), vmem(2 * SIDE, D), vmem(TOKENS, D), sems(4 + 6 * STEPS + 4 + 3)],
         limit=24, flops=2 * 1024 * 1024 * 4000, name="query_gradient",
     )
 
     (input_grad,) = call(
         key_kernel,
-        scalars(place) + hbm(x, up, gain) + near(*handed, message),
+        hbm(x, up, gain) + near(*handed, message),
         hbm(like(TOKENS, D)),
         [vmem(TOKENS, D), vmem(TOKENS, D), vmem(1, D, dtype=F32), vmem(TOKENS, D), vmem(STATS, SPAN, dtype=F32),
-         vmem(2, SPAN, QUAD), vmem(2, TOKENS, QUAD, dtype=F32), vmem(2, TOKENS, QUAD, dtype=F32), vmem(TOKENS, D, dtype=F32), sems(4)],
+         vmem(2, SPAN, QUAD), vmem(2, TOKENS, QUAD, dtype=F32), vmem(PAD_SIDE, D), vmem(TOKENS, D), vmem(TOKENS, D), sems(7)],
         limit=24, flops=2 * 1024 * 1024 * 2000, name="key_gradient",
     )
     return (

time: 64.7 us -> 63.8 us (0.986)
  Pallas kernels: 43.3 us -> 42.4 us
    pallas_call x7, Pallas kernels: 43.3 us -> 42.4 us  [call(): pl.pallas_call(kernel, in_specs=specs(inputs), out_specs=specs(outputs),...]
  transfers between devices with their start and end apart: 9 -> 9, of which waited for: 1 -> 2; matrix products, arithmetic and copies ran while one was open for 0% -> 0% of each run, Pallas kernels for 46% -> 46%
where the time goes in v3:
time: 63.8 us; the launch traced here: 63.5 us
  Pallas kernels  42.4 us (66%)
  starting transfers between devices  17.9 us (28%)
  waiting for transfers between devices  1.43 us (2%)
  local copies, waits for them, and re-layouts  1 us (2%)
  between operations  0.79 us (1%)
    pallas_call x7, Pallas kernels, call(): pl.pallas_call(kernel, in_specs=specs(inputs), out_specs=specs(outputs),...  42.4 us
    ppermute x1, starting transfers between devices, per_device(): edge_b = lax.ppermute(edge_b, 'lon', side_b)  5.67 us
    all_to_all x1, starting transfers between devices, per_device(): lax.all_to_all(going, 'lon', split_axis=0, concat_axis=0, tiled=True)  4.13 us
    ppermute x1, starting transfers between devices, per_device(): stat_b = lax.ppermute(stat_b, 'lon', side_b)  2.8 us
    ppermute x1, starting transfers between devices, per_device(): corner_b = lax.ppermute(corner_b, ('lon', 'lat'), across(side_b))  1.69 us
    ppermute x1, starting transfers between devices, per_device(): message = lax.ppermute(message, 'lat', [(0, 1), (1, 0)])  1.55 us
    ppermute x1, starting transfers between devices, per_device(): band = lax.ppermute(band, 'lat', [(0, 1), (1, 0)])  1.48 us
  transfers between devices with their start and end apart: 9, of which 2 were waited for; matrix products, arithmetic and copies ran while one was open for 0% of the time, Pallas kernels for 46%

profile of v3, /device:TPU:0, one launch (start us, length us, event | category | flops | bytes accessed | tf_op | source)
XLA Modules:
  0.0 63.5 jit_solution(18026349423464715128)
XLA Ops:
  0.6 0.0 copy-start
  0.6 2.9 %edge_tokens.1 = (bf16[184,1024]{1,0:T(8,128)(2,1)}, bf16[184,1024]{1,0:T(8,128)(2,1)}, bf16[96,1024]{1,0:T(8,128)(2,1)}, bf16[40,1024]{1,0:T(8,128)(2,1)}, bf16[40,1024]{1,0:T(8,128)(2,1)}) custom-call(bf16[192,1024]{1,0:T(8,128)(2,1)} %bitcast.13, bf16[192,1024]{1,0:T(8,128)(2,1)} %bitcast.6, bf16[2,96,1024]{2,1,0:T(8,128)(2,1)} %bitcast.11, ...), custom_call_target="tpu_custom_call" | custom-call | bytes 8388608 | tf_op jit(solution)/shard_map/edge_tokens/pallas_call | solution.py:559
  3.6 0.5 collective-permute-start.1
  4.1 5.7 %collective-permute-start.2 = (bf16[184,1024]{1,0:T(8,128)(2,1)}, bf16[184,1024]{1,0:T(8,128)(2,1)}, u32[]{:S(2)}, u32[]{:S(2)}) collective-permute-start(bf16[184,1024]{1,0:T(8,128)(2,1)} %get-tuple-element.43), channel_id=1, source_target_pairs={{0,30},{2,4},{4,2},{6,8},{8,6},{10,12},{12,10},{14,16},{16,14},{18... | collective-permute-start | bytes 1130504 | tf_op jit(solution)/shard_map/ppermute | solution.py:633
  9.7 1.5 %collective-permute-start = (bf16[96,1024]{1,0:T(8,128)(2,1)}, bf16[96,1024]{1,0:T(8,128)(2,1)S(1)}, u32[]{:S(2)}, u32[]{:S(2)}) collective-permute-start(bf16[96,1024]{1,0:T(8,128)(2,1)} %get-tuple-element.41), channel_id=1, source_target_pairs={{0,1},{1,0},{2,3},{3,2},{4,5},{5,4},{6,7},{7,6},{8,9},{9,8},{10,11... | collective-permute-start | bytes 589832 | tf_op jit(solution)/shard_map/ppermute | solution.py:630
  11.2 0.0 collective-permute-start.3
  11.2 1.7 %collective-permute-start.4 = (bf16[40,1024]{1,0:T(8,128)(2,1)}, bf16[40,1024]{1,0:T(8,128)(2,1)}, u32[]{:S(2)}, u32[]{:S(2)}) collective-permute-start(bf16[40,1024]{1,0:T(8,128)(2,1)} %get-tuple-element.45), channel_id=1, source_target_pairs={{0,31},{1,30},{2,5},{3,4},{4,3},{5,2},{6,9},{7,8},{8,7},{9,6},{10,... | collective-permute-start | bytes 245768 | tf_op jit(solution)/shard_map/ppermute | solution.py:632
  12.9 0.0 copy-done
  12.9 0.0 copy-start.4
  12.9 0.0 copy-start.1
  12.9 7.6 %own_projections.1 = (bf16[4,192,256]{2,1,0:T(8,128)(2,1)S(1)}, bf16[4,192,256]{2,1,0:T(8,128)(2,1)S(1)}, bf16[1024,1024]{1,0:T(8,128)(2,1)S(1)}, bf16[192,1024]...) custom-call(f32[16]{0:T(128)S(1)} %copy-done, ...), custom_call_target="tpu_custom_call" | custom-call | flops 2013265920 | bytes 8388608 | tf_op jit(solution)/shard_map/own_projections/pallas_call | solution.py:559
  20.6 0.0 copy-done.4
  20.6 0.1 copy.13.owner_ref
  20.7 0.0 collective-permute-done.3.corner_a_ref
  20.7 0.0 collective-permute-done.4.corner_b_ref
  20.7 0.0 collective-permute-done.band_ref
  20.7 0.0 collective-permute-done.1.edge_a_ref
  20.7 0.0 collective-permute-done.2.edge_b_ref
  20.7 0.0 copy-done.1
  20.7 10.2 %attention_forward.1 = (bf16[192,1024]{1,0:T(8,128)(2,1)S(1)}, f32[72,128]{1,0:T(8,128)S(1)}, f32[72,128]{1,0:T(8,128)S(1)}, bf16[4,2,400,256]{3,2,1,0:T(8,128)(...) custom-call(s32[2,6]{1,0:T(2,128)S(1)} %copy-done.1, ...), custom_call_target="tpu_custom_call" | custom-call | flops 4194304000 | bytes 8388608 | tf_op jit(solution)/shard_map/attention_forward/pallas_call | solution.py:559
  31.0 0.1 collective-permute-start.5
  31.0 2.8 %collective-permute-start.6 = (f32[72,128]{1,0:T(8,128)S(1)}, f32[72,128]{1,0:T(8,128)S(1)}, u32[]{:S(2)}, u32[]{:S(2)}) collective-permute-start(f32[72,128]{1,0:T(8,128)S(1)} %get-tuple-element.52), channel_id=1, source_target_pairs={{0,30},{2,4},{4,2},{6,8},{8,6},{10,12},{12,10},{14,16},{16,14},{18... | collective-permute-start | bytes 110600 | tf_op jit(solution)/shard_map/ppermute | solution.py:664
  33.8 2.3 %output_segments.1 = bf16[16,6,4,1024]{3,2,1,0:T(4,128)(2,1)} custom-call(s32[12,4]{1,0:T(8,128)S(1)} %copy.13.owner_ref, bf16[192,1024]{1,0:T(8,128)(2,1)S(1)} %get-tuple-element.39.x_ref, bf16[192,1024]{1,0:T(8,128)(2,1)S(1)} %get-tuple-element.49.mixed_ref, bf16[1024,1024]{1,0:T(8,128)(2,1)S(1)} %get-tuple-element.50.wo_ref), custom_call_target="tpu_custom_call" | custom-call | flops 419430400 | bytes 8388608 | tf_op jit(solution)/shard_map/output_segments/pallas_call | solution.py:559
  36.2 0.0 collective-permute-done.5.stat_a_hbm
  36.2 0.0 copy-start.2
  36.2 1.0 %collective-permute-done.6.stat_b_hbm = f32[72,128]{1,0:T(8,128)S(1)} collective-permute-done((f32[72,128]{1,0:T(8,128)S(1)}, f32[72,128]{1,0:T(8,128)S(1)}, u32[]{:S(2)}, u32[]{:S(2)}) %collective-permute-start.6) | collective-permute-done | bytes 36896 | tf_op jit(solution)/shard_map/ppermute | solution.py:664
  37.2 0.0 copy-start.3
  37.2 4.1 %all-to-all-start = ((bf16[16,6,4,1024]{3,2,1,0:T(4,128)(2,1)}), bf16[16,6,4,1024]{3,2,1,0:T(4,128)(2,1)S(1)}, u32[]{:S(2)}, u32[]{:S(2)}) async-start(bf16[16,6,4,1024]{3,2,1,0:T(4,128)(2,1)} %output_segments.1), calls=%async_computation | async-start | bytes 1572864 | tf_op jit(solution)/shard_map/all_to_all | solution.py:675
  41.3 0.0 copy-done.2
  41.3 0.0 copy-done.3
  41.3 1.4 %boundary_message.1 = bf16[176,1280]{1,0:T(8,128)(2,1)S(1)} custom-call(bf16[192,1024]{1,0:T(8,128)(2,1)} %bitcast.8, bf16[144,1024]{1,0:T(8,128)(2,1)} %get-tuple-element.55.upn_hbm, f32[192,128]{1,0:T(8,128)} %get-tuple-element.62.stat_hbm, f32[72,128]{1,0:T(8,128)} %copy-done.2, f32[72,128]{1,0:T(8,128)} %copy-done.3), custom_call_target="tpu_custom_call" | custom-call | flops 1024 | bytes 8388608 | tf_op jit(solution)/shard_map/boundary_message/pallas_call | solution.py:559
  42.7 1.5 %collective-permute-start.7 = (bf16[176,1280]{1,0:T(8,128)(2,1)S(1)}, bf16[176,1280]{1,0:T(8,128)(2,1)S(1)}, u32[]{:S(2)}, u32[]{:S(2)}) collective-permute-start(bf16[176,1280]{1,0:T(8,128)(2,1)S(1)} %boundary_message.1), channel_id=1, source_target_pairs={{0,1},{1,0},{2,3},{3,2},{4,5},{5,4},{6,7},{7,6},{8,9},{9,8},{10,11... | collective-permute-start | bytes 1351688 | tf_op jit(solution)/shard_map/ppermute | solution.py:685
  44.3 10.8 %query_gradient.1 = (f32[192,1024]{1,0:T(8,128)S(1)}, bf16[4,512,256]{2,1,0:T(8,128)(2,1)S(1)}, bf16[4,336,256]{2,1,0:T(8,128)(2,1)S(1)}, f32[4,2,96,256]{3,2,1,...) custom-call(f32[16]{0:T(128)S(1)} %copy-done, ...), custom_call_target="tpu_custom_call" | custom-call | flops 8388608000 | bytes 8388608 | tf_op jit(solution)/shard_map/query_gradient/pallas_call | solution.py:559
  55.0 0.4 collective-permute-done.7.message_ref
  55.5 7.1 %key_gradient.1 = bf16[192,1024]{1,0:T(8,128)(2,1)} custom-call(bf16[192,1024]{1,0:T(8,128)(2,1)} %bitcast.15, bf16[192,1024]{1,0:T(8,128)(2,1)} %bitcast.9, f32[1,1024]{1,0:T(1,128)} %bitcast.17, f32[192,1024]{1,0:T(8,128)S(1)} %get-tuple-element.65.gqn_ref, bf16[4,512,256]{2,1,0:T(8,128)(2,1)S(1)} %get-tuple-element.66.query_ref, ...), custom_call_target="tpu_custom_call" | custom-call | flops 4194304000 | bytes 8388608 | tf_op jit(solution)/shard_map/key_gradient/pallas_call | solution.py:559
  62.6 0.0 all-to-all-done
  62.6 0.9 %copy.15 = bf16[1,1,16,6,4,1024]{5,4,3,2,1,0:T(4,128)(2,1)} copy(bf16[1,1,16,6,4,1024]{5,4,3,2,1,0:T(4,128)(2,1)S(1)} %bitcast.10) | data formatting | bytes 1572864
Async XLA Ops:
  0.6 12.3 %copy-start = (f32[16]{0:T(128)S(1)}, f32[16]{0:T(128)}, u32[]{:S(2)}) copy-start(f32[16]{0:T(128)} %sharp_ref.3) | copy-start | bytes 196
  3.6 17.2 %collective-permute-start.1 = (bf16[184,1024]{1,0:T(8,128)(2,1)}, bf16[184,1024]{1,0:T(8,128)(2,1)}, u32[]{:S(2)}, u32[]{:S(2)}) collective-permute-start(bf16[184,1024]{1,0:T(8,128)(2,1)} %get-tuple-element.42), channel_id=1, source_target_pairs={{0,2},{2,0},{4,6},{6,4},{8,10},{10,8},{12,14},{14,12},{16,18},{18,... | collective-permute-start | bytes 1130504 | tf_op jit(solution)/shard_map/ppermute | solution.py:634
  4.1 16.6 %collective-permute-start.2 = (bf16[184,1024]{1,0:T(8,128)(2,1)}, bf16[184,1024]{1,0:T(8,128)(2,1)}, u32[]{:S(2)}, u32[]{:S(2)}) collective-permute-start(bf16[184,1024]{1,0:T(8,128)(2,1)} %get-tuple-element.43), channel_id=1, source_target_pairs={{0,30},{2,4},{4,2},{6,8},{8,6},{10,12},{12,10},{14,16},{16,14},{18... | collective-permute-start | bytes 1130504 | tf_op jit(solution)/shard_map/ppermute | solution.py:633
  9.7 11.0 %collective-permute-start = (bf16[96,1024]{1,0:T(8,128)(2,1)}, bf16[96,1024]{1,0:T(8,128)(2,1)S(1)}, u32[]{:S(2)}, u32[]{:S(2)}) collective-permute-start(bf16[96,1024]{1,0:T(8,128)(2,1)} %get-tuple-element.41), channel_id=1, source_target_pairs={{0,1},{1,0},{2,3},{3,2},{4,5},{5,4},{6,7},{7,6},{8,9},{9,8},{10,11... | collective-permute-start | bytes 589832 | tf_op jit(solution)/shard_map/ppermute | solution.py:630
  11.2 9.5 %collective-permute-start.3 = (bf16[40,1024]{1,0:T(8,128)(2,1)}, bf16[40,1024]{1,0:T(8,128)(2,1)}, u32[]{:S(2)}, u32[]{:S(2)}) collective-permute-start(bf16[40,1024]{1,0:T(8,128)(2,1)} %get-tuple-element.44), channel_id=1, source_target_pairs={{0,3},{1,2},{2,1},{3,0},{4,7},{5,6},{6,5},{7,4},{8,11},{9,10},{10,... | collective-permute-start | bytes 245768 | tf_op jit(solution)/shard_map/ppermute | solution.py:631
  11.2 9.5 %collective-permute-start.4 = (bf16[40,1024]{1,0:T(8,128)(2,1)}, bf16[40,1024]{1,0:T(8,128)(2,1)}, u32[]{:S(2)}, u32[]{:S(2)}) collective-permute-start(bf16[40,1024]{1,0:T(8,128)(2,1)} %get-tuple-element.45), channel_id=1, source_target_pairs={{0,31},{1,30},{2,5},{3,4},{4,3},{5,2},{6,9},{7,8},{8,7},{9,6},{10,... | collective-permute-start | bytes 245768 | tf_op jit(solution)/shard_map/ppermute | solution.py:632
  12.9 7.7 %copy-start.4 = (s32[12,4]{0,1:T(4,128)S(1)}, s32[12,4]{0,1:T(4,128)}, u32[]{:S(2)}) copy-start(s32[12,4]{0,1:T(4,128)} %param.19) | copy-start | bytes 580
  12.9 7.8 %copy-start.1 = (s32[2,6]{1,0:T(2,128)S(1)}, s32[2,6]{1,0:T(2,128)}, u32[]{:S(2)}) copy-start(s32[2,6]{1,0:T(2,128)} %flag_ref.3) | copy-start | bytes 148
  31.0 5.2 %collective-permute-start.5 = (f32[72,128]{1,0:T(8,128)S(1)}, f32[72,128]{1,0:T(8,128)S(1)}, u32[]{:S(2)}, u32[]{:S(2)}) collective-permute-start(f32[72,128]{1,0:T(8,128)S(1)} %get-tuple-element.51), channel_id=1, source_target_pairs={{0,2},{2,0},{4,6},{6,4},{8,10},{10,8},{12,14},{14,12},{16,18},{18,... | collective-permute-start | bytes 110600 | tf_op jit(solution)/shard_map/ppermute | solution.py:665
  31.0 6.1 %collective-permute-start.6 = (f32[72,128]{1,0:T(8,128)S(1)}, f32[72,128]{1,0:T(8,128)S(1)}, u32[]{:S(2)}, u32[]{:S(2)}) collective-permute-start(f32[72,128]{1,0:T(8,128)S(1)} %get-tuple-element.52), channel_id=1, source_target_pairs={{0,30},{2,4},{4,2},{6,8},{8,6},{10,12},{12,10},{14,16},{16,14},{18... | collective-permute-start | bytes 110600 | tf_op jit(solution)/shard_map/ppermute | solution.py:664
  36.2 5.1 %copy-start.2 = (f32[72,128]{1,0:T(8,128)}, f32[72,128]{1,0:T(8,128)S(1)}, u32[]{:S(2)}) copy-start(f32[72,128]{1,0:T(8,128)S(1)} %collective-permute-done.5.stat_a_hbm) | copy-start | bytes 110596
  37.2 4.1 %copy-start.3 = (f32[72,128]{1,0:T(8,128)}, f32[72,128]{1,0:T(8,128)S(1)}, u32[]{:S(2)}) copy-start(f32[72,128]{1,0:T(8,128)S(1)} %collective-permute-done.6.stat_b_hbm) | copy-start | bytes 110596
  37.2 25.4 %all-to-all-start = ((bf16[16,6,4,1024]{3,2,1,0:T(4,128)(2,1)}), bf16[16,6,4,1024]{3,2,1,0:T(4,128)(2,1)S(1)}, u32[]{:S(2)}, u32[]{:S(2)}) async-start(bf16[16,6,4,1024]{3,2,1,0:T(4,128)(2,1)} %output_segments.1), calls=%async_computation | async-start | bytes 1572864 | tf_op jit(solution)/shard_map/all_to_all | solution.py:675
  42.7 12.7 %collective-permute-start.7 = (bf16[176,1280]{1,0:T(8,128)(2,1)S(1)}, bf16[176,1280]{1,0:T(8,128)(2,1)S(1)}, u32[]{:S(2)}, u32[]{:S(2)}) collective-permute-start(bf16[176,1280]{1,0:T(8,128)(2,1)S(1)} %boundary_message.1), channel_id=1, source_target_pairs={{0,1},{1,0},{2,3},{3,2},{4,5},{5,4},{6,7},{7,6},{8,9},{9,8},{10,11... | collective-permute-start | bytes 1351688 | tf_op jit(solution)/shard_map/ppermute | solution.py:685

commit v4 on v3

--- a/solution.py
+++ b/solution.py
@@ -32,7 +32,7 @@
 HALO_QUERIES = PAD_SIDE + 2 * SIDE
 EDGE = SIDE + CORNER
 STATS = 128
-MESSAGE = D + 2 * STATS
+MESSAGE = D + STATS
 MIB = 1024 * 1024
 BF = jnp.bfloat16
 F32 = jnp.float32
@@ -162,17 +162,11 @@
     return jnp.where(hit, 1.0, 0.0).astype(BF)
 
 
-def halves(values):
-    high = values.astype(BF)
-    return high, (values - high.astype(F32)).astype(BF)
-
-
 def spread(stat, j):
     a = lax.broadcasted_iota(jnp.int32, (STATS, QUAD), 0)
     b = lax.broadcasted_iota(jnp.int32, (STATS, QUAD), 1)
     picks = jnp.where(a == b // HEAD_DIM + j * QUAD_HEADS, 1.0, 0.0).astype(BF)
-    high, low = halves(stat)
-    return dot(high, picks) + dot(low, picks)
+    return dot(stat.astype(BF), picks)
 
 
 def where():
@@ -285,18 +279,14 @@
     start, wait = copies.by_step(
         lambda j: [(w3_hbm.at[:, lane_block(k * STEPS, j)], w3_ref.at[j, :, pl.ds(k * QUAD, QUAD)]) for k in range(3)]
     )
+    for j in range(STEPS):
+        start(j)
     grad_loads = copies.load_tokens(up_hbm, up_ref, lat) + [copies.start(wo_hbm, wo_ref)]
-    for j in range(STEPS):
-        start(j)
     outputs = [(qhat_ref, qhat_hbm), (rawq_ref, rawq_hbm), (rawk_ref, rawk_hbm), (kv_ref, kv_hbm)]
     store, stored = copies.by_step(lambda j: [(ref.at[j], hbm.at[j]) for ref, hbm in outputs])
     wait_all(loads)
     xn_ref[:TOKENS] = normed(x_ref[...], gain_ref[...]).astype(BF)
     xn_ref[TOKENS:] = normed(rim_ref[...], gain_ref[...]).astype(BF)
-    wait_all(grad_loads)
-    dout = dot_nt(up_ref[...], wo_ref[...]).astype(BF)
-    for j in range(STEPS):
-        dout_ref[j] = dout[:, j * QUAD : (j + 1) * QUAD]
     for j in range(STEPS):
         wait(j)
         raw = dot(xn_ref[...], w3_ref[j])
@@ -308,6 +298,10 @@
         kv_ref[j, 0] = units[TOKENS:].astype(BF)
         kv_ref[j, 1] = raw[:, 2 * QUAD :].astype(BF)
         store(j)
+    wait_all(grad_loads)
+    dout = dot_nt(up_ref[...], wo_ref[...]).astype(BF)
+    for j in range(STEPS):
+        dout_ref[j] = dout[:, j * QUAD : (j + 1) * QUAD]
     for j in range(STEPS):
         stored(j)
 
@@ -367,16 +361,13 @@
         dprime = (dout_ref[j].astype(F32) * linv_ref[j]).astype(BF)
         dprime_ref[j] = dprime
         inner = dprime.astype(F32) * mixed_ref[:, rows_at(j)].astype(F32)
-        high, low = halves(linv_ref[j])
-        picks = head_lanes(j * QUAD_HEADS, True)
-        stat = stat + dot(high, picks) + dot(low, picks) + dot(inner.astype(BF), head_lanes(HEADS + j * QUAD_HEADS, False))
+        stat = stat + dot(linv_ref[j].astype(BF), head_lanes(j * QUAD_HEADS, True))
+        stat = stat + dot(inner.astype(BF), head_lanes(HEADS + j * QUAD_HEADS, False))
         store(j)
     stat_ref[...] = stat
     stores.append(copies.start(stat_ref, stat_hbm))
     loads[1].wait()
-    high, low = halves(stat)
-    picks = sel_ref[: 2 * EDGE, :TOKENS]
-    picked = dot(picks, high) + dot(picks, low)
+    picked = dot(sel_ref[: 2 * EDGE, :TOKENS], stat.astype(BF))
     stat_a_ref[...] = picked[:SIDE]
     stat_b_ref[...] = picked[EDGE : EDGE + SIDE]
     for j in range(STEPS):
@@ -422,11 +413,9 @@
     picks = jnp.where((b == row + inside * (1 - lat) + side * SIDE) & (row < inside), 1.0, 0.0).astype(BF)
     out_ref[:BAND, :D] = up_ref[...]
     out_ref[BAND:, :D] = dot(picks, upn_ref[...]).astype(BF)
-    high, low = halves(jnp.concatenate([stat_a_ref[...], stat_b_ref[...]], axis=0))
-    stats = jnp.concatenate([stat_ref[...], dot(picks, high) + dot(picks, low)], axis=0)
-    high, low = halves(stats)
-    out_ref[:, D : D + STATS] = high
-    out_ref[:, D + STATS :] = low
+    edges = jnp.concatenate([stat_a_ref[...], stat_b_ref[...]], axis=0).astype(BF)
+    out_ref[:BAND, D:] = stat_ref[...].astype(BF)
+    out_ref[BAND:, D:] = dot(picks, edges).astype(BF)
 
 
 def inner_rows(row_ref, j):
@@ -445,14 +434,23 @@
 def query_kernel(
     sharp_ref, flag_ref, xn_hbm, upn_hbm, tab_hbm, w3_hbm, wo_hbm, qhat_hbm, kv_hbm, halo_hbm, weight_hbm, dprime_hbm,
     rawq_hbm, rawk_hbm, stat_hbm, stat_a_hbm, stat_b_hbm,
-    gqn_ref, query_ref, grad_ref, far_ref, mask_ref, wk_ref, wv_ref, wo_ref, kv_ref, rawk_ref, row_ref,
+    gqn_ref, query_ref, grad_ref, far_ref, mask_ref, wkv_ref, wo_ref, kv_ref, rawk_ref, row_ref,
     xn_ref, upn_ref, tab_ref, wq_ref, qhat_ref, halo_ref, weight_ref, dprime_ref, rawq_ref, stat_ref, stat_a_ref, stat_b_ref,
     key_ref, value_ref, dq_ref, raw_ref, dout_ref, grad_q_ref, sems,
 ):
     lat, spot = where()
     copies = Copies(sems)
-    first = [copies.start(xn_hbm, xn_ref), copies.start(w3_hbm.at[:, pl.ds(0, D)], wq_ref)]
-    second = [copies.start(upn_hbm, upn_ref), copies.start(wo_hbm, wo_ref)]
+    early = [
+        copies.start(hbm, ref)
+        for hbm, ref in (
+            (tab_hbm.at[spot], tab_ref.at[0]), (stat_hbm, stat_ref), (stat_a_hbm, stat_a_ref), (stat_b_hbm, stat_b_ref),
+        )
+    ]
+    first = [copies.start(xn_hbm, xn_ref)]
+    pieces = [pl.ds(k * D // 2, D // 2) for k in range(2)]
+    query_loads = [copies.start(w3_hbm.at[:, piece], wq_ref.at[:, piece]) for piece in pieces]
+    first.append(copies.start(upn_hbm, upn_ref))
+    output_load = copies.start(wo_hbm, wo_ref)
     start, wait = copies.by_step(
         lambda j: [
             (qhat_hbm.at[j], qhat_ref.at[j]),
@@ -464,27 +462,22 @@
         ]
     )
     start(0)
-    third = [
-        copies.start(hbm, ref)
-        for hbm, ref in (
-            (stat_hbm, stat_ref), (stat_a_hbm, stat_a_ref), (stat_b_hbm, stat_b_ref), (tab_hbm.at[spot], tab_ref.at[0]),
-        )
-    ]
     for j in range(1, STEPS):
         start(j)
     later = [
         copies.start(rawk_hbm, rawk_ref),
-        copies.start(w3_hbm.at[:, pl.ds(D, D)], wk_ref),
-        copies.start(w3_hbm.at[:, pl.ds(2 * D, D)], wv_ref),
+        copies.start(w3_hbm.at[:, pl.ds(D, 2 * D)], wkv_ref),
     ]
-    wait_all(first)
-    raw_ref[...] = dot(xn_ref[...], wq_ref[...])
-    wait_all(second)
-    dout_ref[...] = dot_nt(upn_ref[...], wo_ref[...]).astype(BF)
-    wait_all(third)
+    wait_all(early)
     near_mask(mask_ref, tab_ref, flag_ref, lat)
     edges = jnp.concatenate([stat_a_ref[...], stat_b_ref[...]], axis=0)
     row_ref[...] = jnp.concatenate([stat_ref[...], edges], axis=0).T
+    wait_all(first)
+    for piece, load in zip(pieces, query_loads):
+        load.wait()
+        raw_ref[:, piece] = dot(xn_ref[...], wq_ref[:, piece])
+    output_load.wait()
+    dout_ref[...] = dot_nt(upn_ref[...], wo_ref[...]).astype(BF)
     for j in range(STEPS):
         halo_q = (unit(raw_ref[:, rows_at(j)]) * multiplier(sharp_ref, j)).astype(BF)
         query_ref[j, :PAD_SIDE] = halo_q[:PAD_SIDE]
@@ -515,16 +508,16 @@
 
 
 def key_kernel(
-    x_hbm, up_hbm, gain_hbm, gqn_ref, query_ref, grad_ref, far_ref, mask_ref, wk_ref, wv_ref, wo_ref, kv_ref, rawk_ref, row_ref,
+    x_hbm, up_hbm, gain_hbm, gqn_ref, query_ref, grad_ref, far_ref, mask_ref, wkv_ref, wo_ref, kv_ref, rawk_ref, row_ref,
     message_ref,
     out_hbm,
-    x_ref, up_ref, gain_ref, out_ref, all_row_ref, all_ref, dk_ref, dout_ref, grad_k_ref, grad_v_ref, sems,
+    x_ref, up_ref, gain_ref, out_ref, all_row_ref, all_ref, dk_ref, dout_ref, grad_kv_ref, sems,
 ):
     lat, spot = where()
     copies = Copies(sems)
     loads = copies.load_tokens(x_hbm, x_ref, lat) + copies.load_tokens(up_hbm, up_ref, lat)
     loads.append(copies.start(gain_hbm, gain_ref))
-    message = message_ref[:, D : D + STATS].astype(F32) + message_ref[:, D + STATS :].astype(F32)
+    message = message_ref[:, D:].astype(F32)
     all_row_ref[...] = jnp.concatenate([message.T, row_ref[...]], axis=1)
     dout_ref[...] = dot_nt(message_ref[:, :D], wo_ref[...]).astype(BF)
     for j in range(STEPS):
@@ -535,10 +528,10 @@
             kv_ref[j, 0, :HALF, :], kv_ref[j, 1, :HALF, :], query_ref[j], all_ref[slot], mask_ref[0], inner_rows(all_row_ref, j)
         )
         dk_ref[slot, HALF:, :] = far_ref[j, 0]
-        grad_k_ref[:, rows_at(j)] = unit_back(rawk_ref[j], dk_ref[slot]).astype(BF)
-        grad_v_ref[:HALF, rows_at(j)] = near_dv.astype(BF)
-        grad_v_ref[HALF:, rows_at(j)] = far_ref[j, 1].astype(BF)
-    total = gqn_ref[...] + dot_nt(grad_k_ref[...], wk_ref[...]) + dot_nt(grad_v_ref[...], wv_ref[...])
+        grad_kv_ref[:, rows_at(j)] = unit_back(rawk_ref[j], dk_ref[slot]).astype(BF)
+        grad_kv_ref[:HALF, rows_at(STEPS + j)] = near_dv.astype(BF)
+        grad_kv_ref[HALF:, rows_at(STEPS + j)] = far_ref[j, 1].astype(BF)
+    total = gqn_ref[...] + dot_nt(grad_kv_ref[...], wkv_ref[...])
     wait_all(loads)
     tokens = x_ref[...].astype(F32)
     inverse = lax.rsqrt(jnp.mean(tokens * tokens, axis=-1, keepdims=True) + 1e-05)
@@ -689,12 +682,12 @@
         scalars(score_sharpness, flags)
         + hbm(xn_halo, up_halo, keys, w3, wo, qhat, kv, halo_kv, weights, dprime, rawq, rawk, stat, stat_a, stat_b),
         near(like(TOKENS, D, dtype=F32), like(STEPS, SPAN, QUAD), like(STEPS, MIDDLE, QUAD), like(STEPS, 2, HALF, QUAD, dtype=F32),
-             like(2, HALF, SPAN, dtype=F32), like(D, D), like(D, D), like(D, D), kv_like, quads, like(STATS, MIDDLE, dtype=F32)),
+             like(2, HALF, SPAN, dtype=F32), like(D, 2 * D), like(D, D), kv_like, quads, like(STATS, MIDDLE, dtype=F32)),
         [vmem(HALO_QUERIES, D), vmem(2 * SIDE, D), vmem(1, 8, KEYS, dtype=jnp.int32), vmem(D, D),
          vmem(STEPS, TOKENS, QUAD), vmem(STEPS, 2, HALO_ROWS, QUAD), vmem(STEPS, 2, STACK, SPAN), vmem(STEPS, TOKENS, QUAD),
          vmem(STEPS, TOKENS, QUAD), vmem(TOKENS, STATS, dtype=F32), vmem(SIDE, STATS, dtype=F32),
          vmem(SIDE, STATS, dtype=F32), vmem(2, KEYS, QUAD), vmem(2, KEYS, QUAD), vmem(2, TOKENS, QUAD, dtype=F32),
-         vmem(HALO_QUERIES, D, dtype=F32), vmem(2 * SIDE, D), vmem(TOKENS, D), sems(4 + 6 * STEPS + 4 + 3)],
+         vmem(HALO_QUERIES, D, dtype=F32), vmem(2 * SIDE, D), vmem(TOKENS, D), sems(4 + 5 + 6 * STEPS + 2)],
         limit=24, flops=2 * 1024 * 1024 * 4000, name="query_gradient",
     )
 
@@ -703,7 +696,7 @@
         hbm(x, up, gain) + near(*handed, message),
         hbm(like(TOKENS, D)),
         [vmem(TOKENS, D), vmem(TOKENS, D), vmem(1, D, dtype=F32), vmem(TOKENS, D), vmem(STATS, SPAN, dtype=F32),
-         vmem(2, SPAN, QUAD), vmem(2, TOKENS, QUAD, dtype=F32), vmem(PAD_SIDE, D), vmem(TOKENS, D), vmem(TOKENS, D), sems(7)],
+         vmem(2, SPAN, QUAD), vmem(2, TOKENS, QUAD, dtype=F32), vmem(PAD_SIDE, D), vmem(TOKENS, 2 * D), sems(7)],
         limit=24, flops=2 * 1024 * 1024 * 2000, name="key_gradient",
     )
     return (

time: 63.8 us -> 62.6 us (0.981)
  Pallas kernels: 42.4 us -> 41.1 us
  starting transfers between devices: 17.9 us -> 18.8 us
  waiting for transfers between devices: 1.43 us -> 0.56 us
    pallas_call x7, Pallas kernels: 42.4 us -> 41.1 us  [call(): pl.pallas_call(kernel, in_specs=specs(inputs), out_specs=specs(outputs),...]
  transfers between devices with their start and end apart: 9 -> 9, of which waited for: 2 -> 1; matrix products, arithmetic and copies ran while one was open for 0% -> 0% of each run, Pallas kernels for 46% -> 45%
where the time goes in v4:
time: 62.6 us; the launch traced here: 62.3 us
  Pallas kernels  41.1 us (66%)
  starting transfers between devices  18.8 us (30%)
  local copies, waits for them, and re-layouts  1 us (2%)
  between operations  0.8 us (1%)
    pallas_call x7, Pallas kernels, call(): pl.pallas_call(kernel, in_specs=specs(inputs), out_specs=specs(outputs),...  41.1 us
    ppermute x1, starting transfers between devices, per_device(): edge_b = lax.ppermute(edge_b, 'lon', side_b)  5.67 us
    all_to_all x1, starting transfers between devices, per_device(): lax.all_to_all(going, 'lon', split_axis=0, concat_axis=0, tiled=True)  4.59 us
    ppermute x1, starting transfers between devices, per_device(): stat_b = lax.ppermute(stat_b, 'lon', side_b)  3.26 us
    ppermute x1, starting transfers between devices, per_device(): corner_b = lax.ppermute(corner_b, ('lon', 'lat'), across(side_b))  1.69 us
    ppermute x1, starting transfers between devices, per_device(): message = lax.ppermute(message, 'lat', [(0, 1), (1, 0)])  1.54 us
    ppermute x1, starting transfers between devices, per_device(): band = lax.ppermute(band, 'lat', [(0, 1), (1, 0)])  1.48 us
  transfers between devices with their start and end apart: 9, of which 1 were waited for; matrix products, arithmetic and copies ran while one was open for 0% of the time, Pallas kernels for 45%

profile of v4, /device:TPU:0, one launch (start us, length us, event | category | flops | bytes accessed | tf_op | source)
XLA Modules:
  0.0 62.3 jit_solution(9097504560107509271)
XLA Ops:
  0.6 0.0 copy-start
  0.6 2.9 %edge_tokens.1 = (bf16[184,1024]{1,0:T(8,128)(2,1)}, bf16[184,1024]{1,0:T(8,128)(2,1)}, bf16[96,1024]{1,0:T(8,128)(2,1)}, bf16[40,1024]{1,0:T(8,128)(2,1)}, bf16[40,1024]{1,0:T(8,128)(2,1)}) custom-call(bf16[192,1024]{1,0:T(8,128)(2,1)} %bitcast.13, bf16[192,1024]{1,0:T(8,128)(2,1)} %bitcast.6, bf16[2,96,1024]{2,1,0:T(8,128)(2,1)} %bitcast.11, ...), custom_call_target="tpu_custom_call" | custom-call | bytes 8388608 | tf_op jit(solution)/shard_map/edge_tokens/pallas_call | solution.py:552
  3.6 0.5 collective-permute-start.1
  4.1 5.7 %collective-permute-start.2 = (bf16[184,1024]{1,0:T(8,128)(2,1)}, bf16[184,1024]{1,0:T(8,128)(2,1)}, u32[]{:S(2)}, u32[]{:S(2)}) collective-permute-start(bf16[184,1024]{1,0:T(8,128)(2,1)} %get-tuple-element.42), channel_id=1, source_target_pairs={{0,30},{2,4},{4,2},{6,8},{8,6},{10,12},{12,10},{14,16},{16,14},{18... | collective-permute-start | bytes 1130504 | tf_op jit(solution)/shard_map/ppermute | solution.py:626
  9.7 1.5 %collective-permute-start = (bf16[96,1024]{1,0:T(8,128)(2,1)}, bf16[96,1024]{1,0:T(8,128)(2,1)S(1)}, u32[]{:S(2)}, u32[]{:S(2)}) collective-permute-start(bf16[96,1024]{1,0:T(8,128)(2,1)} %get-tuple-element.40), channel_id=1, source_target_pairs={{0,1},{1,0},{2,3},{3,2},{4,5},{5,4},{6,7},{7,6},{8,9},{9,8},{10,11... | collective-permute-start | bytes 589832 | tf_op jit(solution)/shard_map/ppermute | solution.py:623
  11.2 0.0 collective-permute-start.3
  11.2 1.7 %collective-permute-start.4 = (bf16[40,1024]{1,0:T(8,128)(2,1)}, bf16[40,1024]{1,0:T(8,128)(2,1)}, u32[]{:S(2)}, u32[]{:S(2)}) collective-permute-start(bf16[40,1024]{1,0:T(8,128)(2,1)} %get-tuple-element.44), channel_id=1, source_target_pairs={{0,31},{1,30},{2,5},{3,4},{4,3},{5,2},{6,9},{7,8},{8,7},{9,6},{10,... | collective-permute-start | bytes 245768 | tf_op jit(solution)/shard_map/ppermute | solution.py:625
  12.9 0.0 copy-done
  12.9 0.0 copy-start.4
  12.9 0.0 copy-start.1
  12.9 6.6 %own_projections.1 = (bf16[4,192,256]{2,1,0:T(8,128)(2,1)S(1)}, bf16[4,192,256]{2,1,0:T(8,128)(2,1)S(1)}, bf16[1024,1024]{1,0:T(8,128)(2,1)S(1)}, bf16[192,1024]...) custom-call(f32[16]{0:T(128)S(1)} %copy-done, ...), custom_call_target="tpu_custom_call" | custom-call | flops 2013265920 | bytes 8388608 | tf_op jit(solution)/shard_map/own_projections/pallas_call | solution.py:552
  19.5 0.0 copy-done.4
  19.5 0.1 copy.13.owner_ref
  19.6 0.0 collective-permute-done.3.corner_a_ref
  19.6 0.0 collective-permute-done.4.corner_b_ref
  19.6 0.0 collective-permute-done.band_ref
  19.6 0.0 collective-permute-done.1.edge_a_ref
  19.7 0.0 collective-permute-done.2.edge_b_ref
  19.7 0.0 copy-done.1
  19.7 10.0 %attention_forward.1 = (bf16[192,1024]{1,0:T(8,128)(2,1)S(1)}, f32[72,128]{1,0:T(8,128)S(1)}, f32[72,128]{1,0:T(8,128)S(1)}, bf16[4,2,400,256]{3,2,1,0:T(8,128)(...) custom-call(s32[2,6]{1,0:T(2,128)S(1)} %copy-done.1, ...), custom_call_target="tpu_custom_call" | custom-call | flops 4194304000 | bytes 8388608 | tf_op jit(solution)/shard_map/attention_forward/pallas_call | solution.py:552
  29.7 0.1 collective-permute-start.5
  29.8 3.3 %collective-permute-start.6 = (f32[72,128]{1,0:T(8,128)S(1)}, f32[72,128]{1,0:T(8,128)S(1)}, u32[]{:S(2)}, u32[]{:S(2)}) collective-permute-start(f32[72,128]{1,0:T(8,128)S(1)} %get-tuple-element.51), channel_id=1, source_target_pairs={{0,30},{2,4},{4,2},{6,8},{8,6},{10,12},{12,10},{14,16},{16,14},{18... | collective-permute-start | bytes 110600 | tf_op jit(solution)/shard_map/ppermute | solution.py:657
  33.1 2.3 %output_segments.1 = bf16[16,6,4,1024]{3,2,1,0:T(4,128)(2,1)} custom-call(s32[12,4]{1,0:T(8,128)S(1)} %copy.13.owner_ref, bf16[192,1024]{1,0:T(8,128)(2,1)S(1)} %get-tuple-element.38.x_ref, bf16[192,1024]{1,0:T(8,128)(2,1)S(1)} %get-tuple-element.48.mixed_ref, bf16[1024,1024]{1,0:T(8,128)(2,1)S(1)} %get-tuple-element.49.wo_ref), custom_call_target="tpu_custom_call" | custom-call | flops 419430400 | bytes 8388608 | tf_op jit(solution)/shard_map/output_segments/pallas_call | solution.py:552
  35.4 0.0 collective-permute-done.5.stat_a_hbm
  35.4 0.0 copy-start.2
  35.4 0.5 collective-permute-done.6.stat_b_hbm
  35.9 0.0 copy-start.3
  35.9 4.6 %all-to-all-start = ((bf16[16,6,4,1024]{3,2,1,0:T(4,128)(2,1)}), bf16[16,6,4,1024]{3,2,1,0:T(4,128)(2,1)S(1)}, u32[]{:S(2)}, u32[]{:S(2)}) async-start(bf16[16,6,4,1024]{3,2,1,0:T(4,128)(2,1)} %output_segments.1), calls=%async_computation | async-start | bytes 1572864 | tf_op jit(solution)/shard_map/all_to_all | solution.py:668
  40.5 0.0 copy-done.2
  40.6 0.0 copy-done.3
  40.6 1.3 %boundary_message.1 = bf16[176,1152]{1,0:T(8,128)(2,1)S(1)} custom-call(bf16[192,1024]{1,0:T(8,128)(2,1)} %bitcast.8, bf16[144,1024]{1,0:T(8,128)(2,1)} %get-tuple-element.54.upn_hbm, f32[192,128]{1,0:T(8,128)} %get-tuple-element.61.stat_hbm, f32[72,128]{1,0:T(8,128)} %copy-done.2, f32[72,128]{1,0:T(8,128)} %copy-done.3), custom_call_target="tpu_custom_call" | custom-call | flops 1024 | bytes 8388608 | tf_op jit(solution)/shard_map/boundary_message/pallas_call | solution.py:552
  41.9 1.5 %collective-permute-start.7 = (bf16[176,1152]{1,0:T(8,128)(2,1)S(1)}, bf16[176,1152]{1,0:T(8,128)(2,1)S(1)}, u32[]{:S(2)}, u32[]{:S(2)}) collective-permute-start(bf16[176,1152]{1,0:T(8,128)(2,1)S(1)} %boundary_message.1), channel_id=1, source_target_pairs={{0,1},{1,0},{2,3},{3,2},{4,5},{5,4},{6,7},{7,6},{8,9},{9,8},{10,11... | collective-permute-start | bytes 1216520 | tf_op jit(solution)/shard_map/ppermute | solution.py:678
  43.5 10.6 %query_gradient.1 = (f32[192,1024]{1,0:T(8,128)S(1)}, bf16[4,512,256]{2,1,0:T(8,128)(2,1)S(1)}, bf16[4,336,256]{2,1,0:T(8,128)(2,1)S(1)}, f32[4,2,96,256]{3,2,1,...) custom-call(f32[16]{0:T(128)S(1)} %copy-done, ...), custom_call_target="tpu_custom_call" | custom-call | flops 8388608000 | bytes 8388608 | tf_op jit(solution)/shard_map/query_gradient/pallas_call | solution.py:552
  54.1 0.0 collective-permute-done.7.message_ref
  54.1 7.3 %key_gradient.1 = bf16[192,1024]{1,0:T(8,128)(2,1)} custom-call(bf16[192,1024]{1,0:T(8,128)(2,1)} %bitcast.15, bf16[192,1024]{1,0:T(8,128)(2,1)} %bitcast.9, f32[1,1024]{1,0:T(1,128)} %bitcast.17, f32[192,1024]{1,0:T(8,128)S(1)} %get-tuple-element.64.gqn_ref, bf16[4,512,256]{2,1,0:T(8,128)(2,1)S(1)} %get-tuple-element.65.query_ref, ...), custom_call_target="tpu_custom_call" | custom-call | flops 4194304000 | bytes 8388608 | tf_op jit(solution)/shard_map/key_gradient/pallas_call | solution.py:552
  61.4 0.0 all-to-all-done
  61.4 0.9 %copy.15 = bf16[1,1,16,6,4,1024]{5,4,3,2,1,0:T(4,128)(2,1)} copy(bf16[1,1,16,6,4,1024]{5,4,3,2,1,0:T(4,128)(2,1)S(1)} %bitcast.10) | data formatting | bytes 1572864
Async XLA Ops:
  0.6 12.3 %copy-start = (f32[16]{0:T(128)S(1)}, f32[16]{0:T(128)}, u32[]{:S(2)}) copy-start(f32[16]{0:T(128)} %sharp_ref.3) | copy-start | bytes 196
  3.6 16.1 %collective-permute-start.1 = (bf16[184,1024]{1,0:T(8,128)(2,1)}, bf16[184,1024]{1,0:T(8,128)(2,1)}, u32[]{:S(2)}, u32[]{:S(2)}) collective-permute-start(bf16[184,1024]{1,0:T(8,128)(2,1)} %get-tuple-element.41), channel_id=1, source_target_pairs={{0,2},{2,0},{4,6},{6,4},{8,10},{10,8},{12,14},{14,12},{16,18},{18,... | collective-permute-start | bytes 1130504 | tf_op jit(solution)/shard_map/ppermute | solution.py:627
  4.1 15.6 %collective-permute-start.2 = (bf16[184,1024]{1,0:T(8,128)(2,1)}, bf16[184,1024]{1,0:T(8,128)(2,1)}, u32[]{:S(2)}, u32[]{:S(2)}) collective-permute-start(bf16[184,1024]{1,0:T(8,128)(2,1)} %get-tuple-element.42), channel_id=1, source_target_pairs={{0,30},{2,4},{4,2},{6,8},{8,6},{10,12},{12,10},{14,16},{16,14},{18... | collective-permute-start | bytes 1130504 | tf_op jit(solution)/shard_map/ppermute | solution.py:626
  9.7 9.9 %collective-permute-start = (bf16[96,1024]{1,0:T(8,128)(2,1)}, bf16[96,1024]{1,0:T(8,128)(2,1)S(1)}, u32[]{:S(2)}, u32[]{:S(2)}) collective-permute-start(bf16[96,1024]{1,0:T(8,128)(2,1)} %get-tuple-element.40), channel_id=1, source_target_pairs={{0,1},{1,0},{2,3},{3,2},{4,5},{5,4},{6,7},{7,6},{8,9},{9,8},{10,11... | collective-permute-start | bytes 589832 | tf_op jit(solution)/shard_map/ppermute | solution.py:623
  11.2 8.4 %collective-permute-start.3 = (bf16[40,1024]{1,0:T(8,128)(2,1)}, bf16[40,1024]{1,0:T(8,128)(2,1)}, u32[]{:S(2)}, u32[]{:S(2)}) collective-permute-start(bf16[40,1024]{1,0:T(8,128)(2,1)} %get-tuple-element.43), channel_id=1, source_target_pairs={{0,3},{1,2},{2,1},{3,0},{4,7},{5,6},{6,5},{7,4},{8,11},{9,10},{10,... | collective-permute-start | bytes 245768 | tf_op jit(solution)/shard_map/ppermute | solution.py:624
  11.2 8.4 %collective-permute-start.4 = (bf16[40,1024]{1,0:T(8,128)(2,1)}, bf16[40,1024]{1,0:T(8,128)(2,1)}, u32[]{:S(2)}, u32[]{:S(2)}) collective-permute-start(bf16[40,1024]{1,0:T(8,128)(2,1)} %get-tuple-element.44), channel_id=1, source_target_pairs={{0,31},{1,30},{2,5},{3,4},{4,3},{5,2},{6,9},{7,8},{8,7},{9,6},{10,... | collective-permute-start | bytes 245768 | tf_op jit(solution)/shard_map/ppermute | solution.py:625
  12.9 6.6 %copy-start.4 = (s32[12,4]{0,1:T(4,128)S(1)}, s32[12,4]{0,1:T(4,128)}, u32[]{:S(2)}) copy-start(s32[12,4]{0,1:T(4,128)} %param.19) | copy-start | bytes 580
  12.9 6.7 %copy-start.1 = (s32[2,6]{1,0:T(2,128)S(1)}, s32[2,6]{1,0:T(2,128)}, u32[]{:S(2)}) copy-start(s32[2,6]{1,0:T(2,128)} %flag_ref.3) | copy-start | bytes 148
  29.7 5.7 %collective-permute-start.5 = (f32[72,128]{1,0:T(8,128)S(1)}, f32[72,128]{1,0:T(8,128)S(1)}, u32[]{:S(2)}, u32[]{:S(2)}) collective-permute-start(f32[72,128]{1,0:T(8,128)S(1)} %get-tuple-element.50), channel_id=1, source_target_pairs={{0,2},{2,0},{4,6},{6,4},{8,10},{10,8},{12,14},{14,12},{16,18},{18,... | collective-permute-start | bytes 110600 | tf_op jit(solution)/shard_map/ppermute | solution.py:658
  29.8 6.1 %collective-permute-start.6 = (f32[72,128]{1,0:T(8,128)S(1)}, f32[72,128]{1,0:T(8,128)S(1)}, u32[]{:S(2)}, u32[]{:S(2)}) collective-permute-start(f32[72,128]{1,0:T(8,128)S(1)} %get-tuple-element.51), channel_id=1, source_target_pairs={{0,30},{2,4},{4,2},{6,8},{8,6},{10,12},{12,10},{14,16},{16,14},{18... | collective-permute-start | bytes 110600 | tf_op jit(solution)/shard_map/ppermute | solution.py:657
  35.4 5.1 %copy-start.2 = (f32[72,128]{1,0:T(8,128)}, f32[72,128]{1,0:T(8,128)S(1)}, u32[]{:S(2)}) copy-start(f32[72,128]{1,0:T(8,128)S(1)} %collective-permute-done.5.stat_a_hbm) | copy-start | bytes 110596
  35.9 4.6 %copy-start.3 = (f32[72,128]{1,0:T(8,128)}, f32[72,128]{1,0:T(8,128)S(1)}, u32[]{:S(2)}) copy-start(f32[72,128]{1,0:T(8,128)S(1)} %collective-permute-done.6.stat_b_hbm) | copy-start | bytes 110596
  35.9 25.4 %all-to-all-start = ((bf16[16,6,4,1024]{3,2,1,0:T(4,128)(2,1)}), bf16[16,6,4,1024]{3,2,1,0:T(4,128)(2,1)S(1)}, u32[]{:S(2)}, u32[]{:S(2)}) async-start(bf16[16,6,4,1024]{3,2,1,0:T(4,128)(2,1)} %output_segments.1), calls=%async_computation | async-start | bytes 1572864 | tf_op jit(solution)/shard_map/all_to_all | solution.py:668
  41.9 12.2 %collective-permute-start.7 = (bf16[176,1152]{1,0:T(8,128)(2,1)S(1)}, bf16[176,1152]{1,0:T(8,128)(2,1)S(1)}, u32[]{:S(2)}, u32[]{:S(2)}) collective-permute-start(bf16[176,1152]{1,0:T(8,128)(2,1)S(1)} %boundary_message.1), channel_id=1, source_target_pairs={{0,1},{1,0},{2,3},{3,2},{4,5},{5,4},{6,7},{7,6},{8,9},{9,8},{10,11... | collective-permute-start | bytes 1216520 | tf_op jit(solution)/shard_map/ppermute | solution.py:678

commit v5 on v4

--- a/solution.py
+++ b/solution.py
@@ -213,9 +213,6 @@
     def load_tokens(self, hbm, ref, lat):
         return [self.start(hbm.at[pl.ds(half_start(lat, k), HALF)], ref.at[pl.ds(k * HALF, HALF)]) for k in range(2)]
 
-    def store_tokens(self, ref, hbm, lat):
-        return [self.start(ref.at[pl.ds(k * HALF, HALF)], hbm.at[pl.ds(half_start(lat, k), HALF)]) for k in range(2)]
-
     def by_step(self, pairs):
         base, width = self.used, len(pairs(0))
         self.used += STEPS * width
@@ -255,11 +252,12 @@
     copies = Copies(sems)
     loads = copies.load_tokens(x_hbm, x_ref, lat)
     loads += [copies.start(sel_hbm.at[spot], sel_ref), copies.start(rim_hbm.at[lat], rim_ref)]
-    loads += copies.load_tokens(up_hbm, up_ref, lat)
+    grad_loads = copies.load_tokens(up_hbm, up_ref, lat)
     wait_all(loads)
     band_ref[...] = x_ref[:BAND]
     picks = sel_ref[...]
     features = dot(picks, jnp.concatenate([x_ref[...], rim_ref[...]], axis=0))
+    wait_all(grad_loads)
     grads = dot(picks[: 2 * EDGE, :TOKENS], up_ref[...])
     for side, (ref, corner_ref) in enumerate(((edge_a_ref, corner_a_ref), (edge_b_ref, corner_b_ref))):
         at = side * EDGE
@@ -338,13 +336,15 @@
     near_mask(mask_ref, tab_ref, flag_ref, lat)
     stat = jnp.zeros((TOKENS, STATS), F32)
     for j in range(STEPS):
-        wait(j)
+        if j < 2:
+            for k in (0,) if j == 0 else range(1, STEPS):
+                wait(k)
+                wait_kv(k)
         raw = dot(xn_ref[...], wkv_ref[j])
         halo_k = unit(raw[:, :QUAD]).astype(BF)
         halo_v = raw[:, QUAD:].astype(BF)
         halo_ref[j, 0] = halo_k
         halo_ref[j, 1] = halo_v
-        wait_kv(j)
         lay_keys(key_ref.at[j % 2], kv_ref[j, 0], halo_k)
         lay_keys(value_ref.at[j % 2], kv_ref[j, 1], halo_v)
         for half in range(2):
@@ -377,18 +377,25 @@
 
 def output_kernel(owner_ref, x_ref, mixed_ref, wo_ref, going_hbm, acc_ref, going_ref, count_ref, sems):
     lat, spot = where()
-    rows = x_ref[...].astype(F32) + dot(mixed_ref[...], wo_ref[...])
-    for half in range(2):
-        acc_ref[pl.ds(half_start(lat, half), HALF), :] = rows[half * HALF : (half + 1) * HALF]
-    going_ref[...] = jnp.zeros_like(going_ref)
+    copies = Copies(sems)
     for o in range(going_ref.shape[0]):
         count_ref[o] = 0
+    slots = []
     for s in range(TOKENS // SEG):
         owner = owner_ref[s // (COLS // SEG), s % (COLS // SEG)]
-        slot = count_ref[owner]
-        count_ref[owner] = slot + 1
-        going_ref[owner, slot] = acc_ref[s * SEG : (s + 1) * SEG, :].astype(BF)
-    Copies(sems).start(going_ref, going_hbm).wait()
+        slots.append((owner, count_ref[owner]))
+        count_ref[owner] = slots[-1][1] + 1
+    stores = []
+    for part in range(2):
+        cols = pl.ds(part * D // 2, D // 2)
+        going_ref[:, :, :, cols] = jnp.zeros(going_ref.shape[:3] + (D // 2,), BF)
+        rows = x_ref[:, cols].astype(F32) + dot(mixed_ref[...], wo_ref[:, cols])
+        for half in range(2):
+            acc_ref[pl.ds(half_start(lat, half), HALF), cols] = rows[half * HALF : (half + 1) * HALF]
+        for s, (owner, slot) in enumerate(slots):
+            going_ref[owner, slot, :, cols] = acc_ref[s * SEG : (s + 1) * SEG, cols].astype(BF)
+        stores.append(copies.start(going_ref.at[:, :, :, cols], going_hbm.at[:, :, :, cols]))
+    wait_all(stores)
 
 
 def message_kernel(
@@ -483,7 +490,9 @@
         query_ref[j, :PAD_SIDE] = halo_q[:PAD_SIDE]
         query_ref[j, PAD_SIDE + TOKENS :] = halo_q[PAD_SIDE:]
         grad_ref[j, TOKENS:] = (dout_ref[:, rows_at(j)].astype(F32) * spread(edges, j)).astype(BF)
-        wait(j)
+        if j < 2:
+            for k in (0,) if j == 0 else range(1, STEPS):
+                wait(k)
         query_ref[j, PAD_SIDE : PAD_SIDE + TOKENS] = qhat_ref[j]
         grad_ref[j, :TOKENS] = dprime_ref[j]
         lay_keys(key_ref.at[j % 2], kv_ref[j, 0], halo_ref[j, 0])
@@ -533,13 +542,17 @@
         grad_kv_ref[HALF:, rows_at(STEPS + j)] = far_ref[j, 1].astype(BF)
     total = gqn_ref[...] + dot_nt(grad_kv_ref[...], wkv_ref[...])
     wait_all(loads)
-    tokens = x_ref[...].astype(F32)
-    inverse = lax.rsqrt(jnp.mean(tokens * tokens, axis=-1, keepdims=True) + 1e-05)
-    grad = total * gain_ref[...]
-    value = tokens * inverse
-    back = inverse * (grad - value * jnp.mean(value * grad, axis=-1, keepdims=True))
-    out_ref[...] = (up_ref[...].astype(F32) + back).astype(BF)
-    wait_all(copies.store_tokens(out_ref, out_hbm, lat))
+    stores = []
+    for half in range(2):
+        piece = slice(half * HALF, (half + 1) * HALF)
+        tokens = x_ref[piece, :].astype(F32)
+        inverse = lax.rsqrt(jnp.mean(tokens * tokens, axis=-1, keepdims=True) + 1e-05)
+        grad = total[piece] * gain_ref[...]
+        value = tokens * inverse
+        back = inverse * (grad - value * jnp.mean(value * grad, axis=-1, keepdims=True))
+        out_ref[piece, :] = (up_ref[piece, :].astype(F32) + back).astype(BF)
+        stores.append(copies.start(out_ref.at[pl.ds(half * HALF, HALF)], out_hbm.at[pl.ds(half_start(lat, half), HALF)]))
+    wait_all(stores)
 
 
 def call(kernel, inputs, outputs, scratch=(), limit=32, flops=0, name=None):
@@ -661,7 +674,7 @@
         output_kernel,
         scalars(column_group_decoder_longitude) + near(x_near, mixed, wo_near),
         hbm(like(count, cap, SEG, D)),
-        [vmem(TOKENS, D, dtype=F32), vmem(count, cap, SEG, D), pltpu.SMEM((count,), jnp.int32), sems(1)],
+        [vmem(TOKENS, D, dtype=F32), vmem(count, cap, SEG, D), pltpu.SMEM((count,), jnp.int32), sems(2)],
         limit=24, flops=2 * 1024 * 1024 * 200, name="output_segments",
     )
     going, stat_a, stat_b = lax.optimization_barrier((going, stat_a, stat_b))

time: 62.6 us -> 61.9 us (0.989)
  Pallas kernels: 41.1 us -> 40.3 us
    pallas_call x7, Pallas kernels: 41.1 us -> 40.3 us  [call(): pl.pallas_call(kernel, in_specs=specs(inputs), out_specs=specs(outputs),...]
where the time goes in v5:
time: 61.9 us; the launch traced here: 61.6 us
  Pallas kernels  40.3 us (65%)
  starting transfers between devices  18.8 us (30%)
  local copies, waits for them, and re-layouts  1 us (2%)
  between operations  0.8 us (1%)
  waiting for transfers between devices  0.74 us (1%)
    pallas_call x7, Pallas kernels, call(): pl.pallas_call(kernel, in_specs=specs(inputs), out_specs=specs(outputs),...  40.3 us
    ppermute x1, starting transfers between devices, per_device(): edge_b = lax.ppermute(edge_b, 'lon', side_b)  5.67 us
    all_to_all x1, starting transfers between devices, per_device(): lax.all_to_all(going, 'lon', split_axis=0, concat_axis=0, tiled=True)  4.58 us
    ppermute x1, starting transfers between devices, per_device(): stat_b = lax.ppermute(stat_b, 'lon', side_b)  3.26 us
    ppermute x1, starting transfers between devices, per_device(): corner_b = lax.ppermute(corner_b, ('lon', 'lat'), across(side_b))  1.68 us
    ppermute x1, starting transfers between devices, per_device(): message = lax.ppermute(message, 'lat', [(0, 1), (1, 0)])  1.56 us
    ppermute x1, starting transfers between devices, per_device(): band = lax.ppermute(band, 'lat', [(0, 1), (1, 0)])  1.5 us
  transfers between devices with their start and end apart: 9, of which 1 were waited for; matrix products, arithmetic and copies ran while one was open for 0% of the time, Pallas kernels for 45%

profile of v5, /device:TPU:0, one launch (start us, length us, event | category | flops | bytes accessed | tf_op | source)
XLA Modules:
  0.0 61.6 jit_solution(14175346067937962136)
XLA Ops:
  0.6 0.0 copy-start
  0.6 3.0 %edge_tokens.1 = (bf16[184,1024]{1,0:T(8,128)(2,1)}, bf16[184,1024]{1,0:T(8,128)(2,1)}, bf16[96,1024]{1,0:T(8,128)(2,1)}, bf16[40,1024]{1,0:T(8,128)(2,1)}, bf16[40,1024]{1,0:T(8,128)(2,1)}) custom-call(bf16[192,1024]{1,0:T(8,128)(2,1)} %bitcast.13, bf16[192,1024]{1,0:T(8,128)(2,1)} %bitcast.6, bf16[2,96,1024]{2,1,0:T(8,128)(2,1)} %bitcast.11, ...), custom_call_target="tpu_custom_call" | custom-call | bytes 8388608 | tf_op jit(solution)/shard_map/edge_tokens/pallas_call | solution.py:565
  3.6 0.5 collective-permute-start.1
  4.2 5.7 %collective-permute-start.2 = (bf16[184,1024]{1,0:T(8,128)(2,1)}, bf16[184,1024]{1,0:T(8,128)(2,1)}, u32[]{:S(2)}, u32[]{:S(2)}) collective-permute-start(bf16[184,1024]{1,0:T(8,128)(2,1)} %get-tuple-element.42), channel_id=1, source_target_pairs={{0,30},{2,4},{4,2},{6,8},{8,6},{10,12},{12,10},{14,16},{16,14},{18... | collective-permute-start | bytes 1130504 | tf_op jit(solution)/shard_map/ppermute | solution.py:639
  9.8 1.5 %collective-permute-start = (bf16[96,1024]{1,0:T(8,128)(2,1)}, bf16[96,1024]{1,0:T(8,128)(2,1)S(1)}, u32[]{:S(2)}, u32[]{:S(2)}) collective-permute-start(bf16[96,1024]{1,0:T(8,128)(2,1)} %get-tuple-element.40), channel_id=1, source_target_pairs={{0,1},{1,0},{2,3},{3,2},{4,5},{5,4},{6,7},{7,6},{8,9},{9,8},{10,11... | collective-permute-start | bytes 589832 | tf_op jit(solution)/shard_map/ppermute | solution.py:636
  11.3 0.0 collective-permute-start.3
  11.3 1.7 %collective-permute-start.4 = (bf16[40,1024]{1,0:T(8,128)(2,1)}, bf16[40,1024]{1,0:T(8,128)(2,1)}, u32[]{:S(2)}, u32[]{:S(2)}) collective-permute-start(bf16[40,1024]{1,0:T(8,128)(2,1)} %get-tuple-element.44), channel_id=1, source_target_pairs={{0,31},{1,30},{2,5},{3,4},{4,3},{5,2},{6,9},{7,8},{8,7},{9,6},{10,... | collective-permute-start | bytes 245768 | tf_op jit(solution)/shard_map/ppermute | solution.py:638
  13.0 0.0 copy-done
  13.0 0.0 copy-start.4
  13.0 0.0 copy-start.1
  13.0 6.6 %own_projections.1 = (bf16[4,192,256]{2,1,0:T(8,128)(2,1)S(1)}, bf16[4,192,256]{2,1,0:T(8,128)(2,1)S(1)}, bf16[1024,1024]{1,0:T(8,128)(2,1)S(1)}, bf16[192,1024]...) custom-call(f32[16]{0:T(128)S(1)} %copy-done, ...), custom_call_target="tpu_custom_call" | custom-call | flops 2013265920 | bytes 8388608 | tf_op jit(solution)/shard_map/own_projections/pallas_call | solution.py:565
  19.6 0.0 copy-done.4
  19.6 0.1 copy.13.owner_ref
  19.7 0.0 collective-permute-done.3.corner_a_ref
  19.7 0.0 collective-permute-done.4.corner_b_ref
  19.7 0.0 collective-permute-done.band_ref
  19.7 0.0 collective-permute-done.1.edge_a_ref
  19.7 0.0 collective-permute-done.2.edge_b_ref
  19.8 0.0 copy-done.1
  19.8 9.6 %attention_forward.1 = (bf16[192,1024]{1,0:T(8,128)(2,1)S(1)}, f32[72,128]{1,0:T(8,128)S(1)}, f32[72,128]{1,0:T(8,128)S(1)}, bf16[4,2,400,256]{3,2,1,0:T(8,128)(...) custom-call(s32[2,6]{1,0:T(2,128)S(1)} %copy-done.1, ...), custom_call_target="tpu_custom_call" | custom-call | flops 4194304000 | bytes 8388608 | tf_op jit(solution)/shard_map/attention_forward/pallas_call | solution.py:565
  29.4 0.1 collective-permute-start.5
  29.5 3.3 %collective-permute-start.6 = (f32[72,128]{1,0:T(8,128)S(1)}, f32[72,128]{1,0:T(8,128)S(1)}, u32[]{:S(2)}, u32[]{:S(2)}) collective-permute-start(f32[72,128]{1,0:T(8,128)S(1)} %get-tuple-element.51), channel_id=1, source_target_pairs={{0,30},{2,4},{4,2},{6,8},{8,6},{10,12},{12,10},{14,16},{16,14},{18... | collective-permute-start | bytes 110600 | tf_op jit(solution)/shard_map/ppermute | solution.py:670
  32.8 2.1 %output_segments.1 = bf16[16,6,4,1024]{3,2,1,0:T(4,128)(2,1)} custom-call(s32[12,4]{1,0:T(8,128)S(1)} %copy.13.owner_ref, bf16[192,1024]{1,0:T(8,128)(2,1)S(1)} %get-tuple-element.38.x_ref, bf16[192,1024]{1,0:T(8,128)(2,1)S(1)} %get-tuple-element.48.mixed_ref, bf16[1024,1024]{1,0:T(8,128)(2,1)S(1)} %get-tuple-element.49.wo_ref), custom_call_target="tpu_custom_call" | custom-call | flops 419430400 | bytes 8388608 | tf_op jit(solution)/shard_map/output_segments/pallas_call | solution.py:565
  34.9 0.0 collective-permute-done.5.stat_a_hbm
  34.9 0.0 copy-start.2
  34.9 0.7 %collective-permute-done.6.stat_b_hbm = f32[72,128]{1,0:T(8,128)S(1)} collective-permute-done((f32[72,128]{1,0:T(8,128)S(1)}, f32[72,128]{1,0:T(8,128)S(1)}, u32[]{:S(2)}, u32[]{:S(2)}) %collective-permute-start.6) | collective-permute-done | bytes 36896 | tf_op jit(solution)/shard_map/ppermute | solution.py:670
  35.6 0.0 copy-start.3
  35.6 4.6 %all-to-all-start = ((bf16[16,6,4,1024]{3,2,1,0:T(4,128)(2,1)}), bf16[16,6,4,1024]{3,2,1,0:T(4,128)(2,1)S(1)}, u32[]{:S(2)}, u32[]{:S(2)}) async-start(bf16[16,6,4,1024]{3,2,1,0:T(4,128)(2,1)} %output_segments.1), calls=%async_computation | async-start | bytes 1572864 | tf_op jit(solution)/shard_map/all_to_all | solution.py:681
  40.2 0.0 copy-done.2
  40.2 0.0 copy-done.3
  40.3 1.3 %boundary_message.1 = bf16[176,1152]{1,0:T(8,128)(2,1)S(1)} custom-call(bf16[192,1024]{1,0:T(8,128)(2,1)} %bitcast.8, bf16[144,1024]{1,0:T(8,128)(2,1)} %get-tuple-element.54.upn_hbm, f32[192,128]{1,0:T(8,128)} %get-tuple-element.61.stat_hbm, f32[72,128]{1,0:T(8,128)} %copy-done.2, f32[72,128]{1,0:T(8,128)} %copy-done.3), custom_call_target="tpu_custom_call" | custom-call | flops 1024 | bytes 8388608 | tf_op jit(solution)/shard_map/boundary_message/pallas_call | solution.py:565
  41.6 1.6 %collective-permute-start.7 = (bf16[176,1152]{1,0:T(8,128)(2,1)S(1)}, bf16[176,1152]{1,0:T(8,128)(2,1)S(1)}, u32[]{:S(2)}, u32[]{:S(2)}) collective-permute-start(bf16[176,1152]{1,0:T(8,128)(2,1)S(1)} %boundary_message.1), channel_id=1, source_target_pairs={{0,1},{1,0},{2,3},{3,2},{4,5},{5,4},{6,7},{7,6},{8,9},{9,8},{10,11... | collective-permute-start | bytes 1216520 | tf_op jit(solution)/shard_map/ppermute | solution.py:691
  43.2 10.4 %query_gradient.1 = (f32[192,1024]{1,0:T(8,128)S(1)}, bf16[4,512,256]{2,1,0:T(8,128)(2,1)S(1)}, bf16[4,336,256]{2,1,0:T(8,128)(2,1)S(1)}, f32[4,2,96,256]{3,2,1,...) custom-call(f32[16]{0:T(128)S(1)} %copy-done, ...), custom_call_target="tpu_custom_call" | custom-call | flops 8388608000 | bytes 8388608 | tf_op jit(solution)/shard_map/query_gradient/pallas_call | solution.py:565
  53.5 0.0 collective-permute-done.7.message_ref
  53.5 7.2 %key_gradient.1 = bf16[192,1024]{1,0:T(8,128)(2,1)} custom-call(bf16[192,1024]{1,0:T(8,128)(2,1)} %bitcast.15, bf16[192,1024]{1,0:T(8,128)(2,1)} %bitcast.9, f32[1,1024]{1,0:T(1,128)} %bitcast.17, f32[192,1024]{1,0:T(8,128)S(1)} %get-tuple-element.64.gqn_ref, bf16[4,512,256]{2,1,0:T(8,128)(2,1)S(1)} %get-tuple-element.65.query_ref, ...), custom_call_target="tpu_custom_call" | custom-call | flops 4194304000 | bytes 8388608 | tf_op jit(solution)/shard_map/key_gradient/pallas_call | solution.py:565
  60.7 0.0 all-to-all-done
  60.7 0.9 %copy.15 = bf16[1,1,16,6,4,1024]{5,4,3,2,1,0:T(4,128)(2,1)} copy(bf16[1,1,16,6,4,1024]{5,4,3,2,1,0:T(4,128)(2,1)S(1)} %bitcast.10) | data formatting | bytes 1572864
Async XLA Ops:
  0.6 12.4 %copy-start = (f32[16]{0:T(128)S(1)}, f32[16]{0:T(128)}, u32[]{:S(2)}) copy-start(f32[16]{0:T(128)} %sharp_ref.3) | copy-start | bytes 196
  3.6 16.1 %collective-permute-start.1 = (bf16[184,1024]{1,0:T(8,128)(2,1)}, bf16[184,1024]{1,0:T(8,128)(2,1)}, u32[]{:S(2)}, u32[]{:S(2)}) collective-permute-start(bf16[184,1024]{1,0:T(8,128)(2,1)} %get-tuple-element.41), channel_id=1, source_target_pairs={{0,2},{2,0},{4,6},{6,4},{8,10},{10,8},{12,14},{14,12},{16,18},{18,... | collective-permute-start | bytes 1130504 | tf_op jit(solution)/shard_map/ppermute | solution.py:640
  4.2 15.6 %collective-permute-start.2 = (bf16[184,1024]{1,0:T(8,128)(2,1)}, bf16[184,1024]{1,0:T(8,128)(2,1)}, u32[]{:S(2)}, u32[]{:S(2)}) collective-permute-start(bf16[184,1024]{1,0:T(8,128)(2,1)} %get-tuple-element.42), channel_id=1, source_target_pairs={{0,30},{2,4},{4,2},{6,8},{8,6},{10,12},{12,10},{14,16},{16,14},{18... | collective-permute-start | bytes 1130504 | tf_op jit(solution)/shard_map/ppermute | solution.py:639
  9.8 9.9 %collective-permute-start = (bf16[96,1024]{1,0:T(8,128)(2,1)}, bf16[96,1024]{1,0:T(8,128)(2,1)S(1)}, u32[]{:S(2)}, u32[]{:S(2)}) collective-permute-start(bf16[96,1024]{1,0:T(8,128)(2,1)} %get-tuple-element.40), channel_id=1, source_target_pairs={{0,1},{1,0},{2,3},{3,2},{4,5},{5,4},{6,7},{7,6},{8,9},{9,8},{10,11... | collective-permute-start | bytes 589832 | tf_op jit(solution)/shard_map/ppermute | solution.py:636
  11.3 8.4 %collective-permute-start.3 = (bf16[40,1024]{1,0:T(8,128)(2,1)}, bf16[40,1024]{1,0:T(8,128)(2,1)}, u32[]{:S(2)}, u32[]{:S(2)}) collective-permute-start(bf16[40,1024]{1,0:T(8,128)(2,1)} %get-tuple-element.43), channel_id=1, source_target_pairs={{0,3},{1,2},{2,1},{3,0},{4,7},{5,6},{6,5},{7,4},{8,11},{9,10},{10,... | collective-permute-start | bytes 245768 | tf_op jit(solution)/shard_map/ppermute | solution.py:637
  11.3 8.4 %collective-permute-start.4 = (bf16[40,1024]{1,0:T(8,128)(2,1)}, bf16[40,1024]{1,0:T(8,128)(2,1)}, u32[]{:S(2)}, u32[]{:S(2)}) collective-permute-start(bf16[40,1024]{1,0:T(8,128)(2,1)} %get-tuple-element.44), channel_id=1, source_target_pairs={{0,31},{1,30},{2,5},{3,4},{4,3},{5,2},{6,9},{7,8},{8,7},{9,6},{10,... | collective-permute-start | bytes 245768 | tf_op jit(solution)/shard_map/ppermute | solution.py:638
  13.0 6.6 %copy-start.4 = (s32[12,4]{0,1:T(4,128)S(1)}, s32[12,4]{0,1:T(4,128)}, u32[]{:S(2)}) copy-start(s32[12,4]{0,1:T(4,128)} %param.19) | copy-start | bytes 580
  13.0 6.7 %copy-start.1 = (s32[2,6]{1,0:T(2,128)S(1)}, s32[2,6]{1,0:T(2,128)}, u32[]{:S(2)}) copy-start(s32[2,6]{1,0:T(2,128)} %flag_ref.3) | copy-start | bytes 148
  29.4 5.5 %collective-permute-start.5 = (f32[72,128]{1,0:T(8,128)S(1)}, f32[72,128]{1,0:T(8,128)S(1)}, u32[]{:S(2)}, u32[]{:S(2)}) collective-permute-start(f32[72,128]{1,0:T(8,128)S(1)} %get-tuple-element.50), channel_id=1, source_target_pairs={{0,2},{2,0},{4,6},{6,4},{8,10},{10,8},{12,14},{14,12},{16,18},{18,... | collective-permute-start | bytes 110600 | tf_op jit(solution)/shard_map/ppermute | solution.py:671
  29.5 6.1 %collective-permute-start.6 = (f32[72,128]{1,0:T(8,128)S(1)}, f32[72,128]{1,0:T(8,128)S(1)}, u32[]{:S(2)}, u32[]{:S(2)}) collective-permute-start(f32[72,128]{1,0:T(8,128)S(1)} %get-tuple-element.51), channel_id=1, source_target_pairs={{0,30},{2,4},{4,2},{6,8},{8,6},{10,12},{12,10},{14,16},{16,14},{18... | collective-permute-start | bytes 110600 | tf_op jit(solution)/shard_map/ppermute | solution.py:670
  34.9 5.3 %copy-start.2 = (f32[72,128]{1,0:T(8,128)}, f32[72,128]{1,0:T(8,128)S(1)}, u32[]{:S(2)}) copy-start(f32[72,128]{1,0:T(8,128)S(1)} %collective-permute-done.5.stat_a_hbm) | copy-start | bytes 110596
  35.6 4.6 %copy-start.3 = (f32[72,128]{1,0:T(8,128)}, f32[72,128]{1,0:T(8,128)S(1)}, u32[]{:S(2)}) copy-start(f32[72,128]{1,0:T(8,128)S(1)} %collective-permute-done.6.stat_b_hbm) | copy-start | bytes 110596
  35.6 25.1 %all-to-all-start = ((bf16[16,6,4,1024]{3,2,1,0:T(4,128)(2,1)}), bf16[16,6,4,1024]{3,2,1,0:T(4,128)(2,1)S(1)}, u32[]{:S(2)}, u32[]{:S(2)}) async-start(bf16[16,6,4,1024]{3,2,1,0:T(4,128)(2,1)} %output_segments.1), calls=%async_computation | async-start | bytes 1572864 | tf_op jit(solution)/shard_map/all_to_all | solution.py:681
  41.6 11.9 %collective-permute-start.7 = (bf16[176,1152]{1,0:T(8,128)(2,1)S(1)}, bf16[176,1152]{1,0:T(8,128)(2,1)S(1)}, u32[]{:S(2)}, u32[]{:S(2)}) collective-permute-start(bf16[176,1152]{1,0:T(8,128)(2,1)S(1)} %boundary_message.1), channel_id=1, source_target_pairs={{0,1},{1,0},{2,3},{3,2},{4,5},{5,4},{6,7},{7,6},{8,9},{9,8},{10,11... | collective-permute-start | bytes 1216520 | tf_op jit(solution)/shard_map/ppermute | solution.py:691

commit v6 on v5

--- a/solution.py
+++ b/solution.py
@@ -286,7 +286,8 @@
     xn_ref[:TOKENS] = normed(x_ref[...], gain_ref[...]).astype(BF)
     xn_ref[TOKENS:] = normed(rim_ref[...], gain_ref[...]).astype(BF)
     for j in range(STEPS):
-        wait(j)
+        for k in ((0,), (1,), (2, 3), ())[j]:
+            wait(k)
         raw = dot(xn_ref[...], w3_ref[j])
         raw_q, raw_k = raw[:TOKENS, :QUAD], raw[:, QUAD : 2 * QUAD]
         units = unit(jnp.concatenate([raw_q, raw_k], axis=0))

time: 61.9 us -> 61.9 us (level)
  transfers between devices with their start and end apart: 9 -> 9, of which waited for: 1 -> 1; matrix products, arithmetic and copies ran while one was open for 0% -> 0% of each run, Pallas kernels for 45% -> 44%
where the time goes in v6:
time: 61.9 us; the launch traced here: 61.6 us
  Pallas kernels  39.9 us (64%)
  starting transfers between devices  19.4 us (31%)
  local copies, waits for them, and re-layouts  1 us (2%)
  between operations  0.8 us (1%)
    pallas_call x7, Pallas kernels, call(): pl.pallas_call(kernel, in_specs=specs(inputs), out_specs=specs(outputs),...  39.9 us
    ppermute x1, starting transfers between devices, per_device(): edge_b = lax.ppermute(edge_b, 'lon', side_b)  5.67 us
    all_to_all x1, starting transfers between devices, per_device(): lax.all_to_all(going, 'lon', split_axis=0, concat_axis=0, tiled=True)  4.89 us
    ppermute x1, starting transfers between devices, per_device(): stat_b = lax.ppermute(stat_b, 'lon', side_b)  3.56 us
    ppermute x1, starting transfers between devices, per_device(): corner_b = lax.ppermute(corner_b, ('lon', 'lat'), across(side_b))  1.68 us
    ppermute x1, starting transfers between devices, per_device(): message = lax.ppermute(message, 'lat', [(0, 1), (1, 0)])  1.56 us
    ppermute x1, starting transfers between devices, per_device(): band = lax.ppermute(band, 'lat', [(0, 1), (1, 0)])  1.5 us
  transfers between devices with their start and end apart: 9, of which 1 were waited for; matrix products, arithmetic and copies ran while one was open for 0% of the time, Pallas kernels for 44%

profile of v6, /device:TPU:0, one launch (start us, length us, event | category | flops | bytes accessed | tf_op | source)
XLA Modules:
  0.0 61.6 jit_solution(9010829208372736925)
XLA Ops:
  0.6 0.0 copy-start
  0.6 3.0 %edge_tokens.1 = (bf16[184,1024]{1,0:T(8,128)(2,1)}, bf16[184,1024]{1,0:T(8,128)(2,1)}, bf16[96,1024]{1,0:T(8,128)(2,1)}, bf16[40,1024]{1,0:T(8,128)(2,1)}, bf16[40,1024]{1,0:T(8,128)(2,1)}) custom-call(bf16[192,1024]{1,0:T(8,128)(2,1)} %bitcast.13, bf16[192,1024]{1,0:T(8,128)(2,1)} %bitcast.6, bf16[2,96,1024]{2,1,0:T(8,128)(2,1)} %bitcast.11, ...), custom_call_target="tpu_custom_call" | custom-call | bytes 8388608 | tf_op jit(solution)/shard_map/edge_tokens/pallas_call | solution.py:566
  3.6 0.5 collective-permute-start.1
  4.2 5.7 %collective-permute-start.2 = (bf16[184,1024]{1,0:T(8,128)(2,1)}, bf16[184,1024]{1,0:T(8,128)(2,1)}, u32[]{:S(2)}, u32[]{:S(2)}) collective-permute-start(bf16[184,1024]{1,0:T(8,128)(2,1)} %get-tuple-element.42), channel_id=1, source_target_pairs={{0,30},{2,4},{4,2},{6,8},{8,6},{10,12},{12,10},{14,16},{16,14},{18... | collective-permute-start | bytes 1130504 | tf_op jit(solution)/shard_map/ppermute | solution.py:640
  9.8 1.5 %collective-permute-start = (bf16[96,1024]{1,0:T(8,128)(2,1)}, bf16[96,1024]{1,0:T(8,128)(2,1)S(1)}, u32[]{:S(2)}, u32[]{:S(2)}) collective-permute-start(bf16[96,1024]{1,0:T(8,128)(2,1)} %get-tuple-element.40), channel_id=1, source_target_pairs={{0,1},{1,0},{2,3},{3,2},{4,5},{5,4},{6,7},{7,6},{8,9},{9,8},{10,11... | collective-permute-start | bytes 589832 | tf_op jit(solution)/shard_map/ppermute | solution.py:637
  11.3 0.0 collective-permute-start.3
  11.3 1.7 %collective-permute-start.4 = (bf16[40,1024]{1,0:T(8,128)(2,1)}, bf16[40,1024]{1,0:T(8,128)(2,1)}, u32[]{:S(2)}, u32[]{:S(2)}) collective-permute-start(bf16[40,1024]{1,0:T(8,128)(2,1)} %get-tuple-element.44), channel_id=1, source_target_pairs={{0,31},{1,30},{2,5},{3,4},{4,3},{5,2},{6,9},{7,8},{8,7},{9,6},{10,... | collective-permute-start | bytes 245768 | tf_op jit(solution)/shard_map/ppermute | solution.py:639
  13.0 0.0 copy-done
  13.0 0.0 copy-start.4
  13.0 0.0 copy-start.1
  13.0 6.3 %own_projections.1 = (bf16[4,192,256]{2,1,0:T(8,128)(2,1)S(1)}, bf16[4,192,256]{2,1,0:T(8,128)(2,1)S(1)}, bf16[1024,1024]{1,0:T(8,128)(2,1)S(1)}, bf16[192,1024]...) custom-call(f32[16]{0:T(128)S(1)} %copy-done, ...), custom_call_target="tpu_custom_call" | custom-call | flops 2013265920 | bytes 8388608 | tf_op jit(solution)/shard_map/own_projections/pallas_call | solution.py:566
  19.3 0.0 copy-done.4
  19.3 0.1 copy.13.owner_ref
  19.4 0.0 collective-permute-done.3.corner_a_ref
  19.4 0.0 collective-permute-done.4.corner_b_ref
  19.4 0.0 collective-permute-done.band_ref
  19.4 0.0 collective-permute-done.1.edge_a_ref
  19.4 0.0 collective-permute-done.2.edge_b_ref
  19.4 0.0 copy-done.1
  19.5 9.6 %attention_forward.1 = (bf16[192,1024]{1,0:T(8,128)(2,1)S(1)}, f32[72,128]{1,0:T(8,128)S(1)}, f32[72,128]{1,0:T(8,128)S(1)}, bf16[4,2,400,256]{3,2,1,0:T(8,128)(...) custom-call(s32[2,6]{1,0:T(2,128)S(1)} %copy-done.1, ...), custom_call_target="tpu_custom_call" | custom-call | flops 4194304000 | bytes 8388608 | tf_op jit(solution)/shard_map/attention_forward/pallas_call | solution.py:566
  29.1 0.1 collective-permute-start.5
  29.2 3.6 %collective-permute-start.6 = (f32[72,128]{1,0:T(8,128)S(1)}, f32[72,128]{1,0:T(8,128)S(1)}, u32[]{:S(2)}, u32[]{:S(2)}) collective-permute-start(f32[72,128]{1,0:T(8,128)S(1)} %get-tuple-element.51), channel_id=1, source_target_pairs={{0,30},{2,4},{4,2},{6,8},{8,6},{10,12},{12,10},{14,16},{16,14},{18... | collective-permute-start | bytes 110600 | tf_op jit(solution)/shard_map/ppermute | solution.py:671
  32.8 2.1 %output_segments.1 = bf16[16,6,4,1024]{3,2,1,0:T(4,128)(2,1)} custom-call(s32[12,4]{1,0:T(8,128)S(1)} %copy.13.owner_ref, bf16[192,1024]{1,0:T(8,128)(2,1)S(1)} %get-tuple-element.38.x_ref, bf16[192,1024]{1,0:T(8,128)(2,1)S(1)} %get-tuple-element.48.mixed_ref, bf16[1024,1024]{1,0:T(8,128)(2,1)S(1)} %get-tuple-element.49.wo_ref), custom_call_target="tpu_custom_call" | custom-call | flops 419430400 | bytes 8388608 | tf_op jit(solution)/shard_map/output_segments/pallas_call | solution.py:566
  34.9 0.0 collective-permute-done.5.stat_a_hbm
  34.9 0.0 copy-start.2
  34.9 0.4 collective-permute-done.6.stat_b_hbm
  35.3 0.0 copy-start.3
  35.3 4.9 %all-to-all-start = ((bf16[16,6,4,1024]{3,2,1,0:T(4,128)(2,1)}), bf16[16,6,4,1024]{3,2,1,0:T(4,128)(2,1)S(1)}, u32[]{:S(2)}, u32[]{:S(2)}) async-start(bf16[16,6,4,1024]{3,2,1,0:T(4,128)(2,1)} %output_segments.1), calls=%async_computation | async-start | bytes 1572864 | tf_op jit(solution)/shard_map/all_to_all | solution.py:682
  40.2 0.0 copy-done.2
  40.2 0.0 copy-done.3
  40.3 1.3 %boundary_message.1 = bf16[176,1152]{1,0:T(8,128)(2,1)S(1)} custom-call(bf16[192,1024]{1,0:T(8,128)(2,1)} %bitcast.8, bf16[144,1024]{1,0:T(8,128)(2,1)} %get-tuple-element.54.upn_hbm, f32[192,128]{1,0:T(8,128)} %get-tuple-element.61.stat_hbm, f32[72,128]{1,0:T(8,128)} %copy-done.2, f32[72,128]{1,0:T(8,128)} %copy-done.3), custom_call_target="tpu_custom_call" | custom-call | flops 1024 | bytes 8388608 | tf_op jit(solution)/shard_map/boundary_message/pallas_call | solution.py:566
  41.6 1.6 %collective-permute-start.7 = (bf16[176,1152]{1,0:T(8,128)(2,1)S(1)}, bf16[176,1152]{1,0:T(8,128)(2,1)S(1)}, u32[]{:S(2)}, u32[]{:S(2)}) collective-permute-start(bf16[176,1152]{1,0:T(8,128)(2,1)S(1)} %boundary_message.1), channel_id=1, source_target_pairs={{0,1},{1,0},{2,3},{3,2},{4,5},{5,4},{6,7},{7,6},{8,9},{9,8},{10,11... | collective-permute-start | bytes 1216520 | tf_op jit(solution)/shard_map/ppermute | solution.py:692
  43.2 10.4 %query_gradient.1 = (f32[192,1024]{1,0:T(8,128)S(1)}, bf16[4,512,256]{2,1,0:T(8,128)(2,1)S(1)}, bf16[4,336,256]{2,1,0:T(8,128)(2,1)S(1)}, f32[4,2,96,256]{3,2,1,...) custom-call(f32[16]{0:T(128)S(1)} %copy-done, ...), custom_call_target="tpu_custom_call" | custom-call | flops 8388608000 | bytes 8388608 | tf_op jit(solution)/shard_map/query_gradient/pallas_call | solution.py:566
  53.5 0.0 collective-permute-done.7.message_ref
  53.5 7.2 %key_gradient.1 = bf16[192,1024]{1,0:T(8,128)(2,1)} custom-call(bf16[192,1024]{1,0:T(8,128)(2,1)} %bitcast.15, bf16[192,1024]{1,0:T(8,128)(2,1)} %bitcast.9, f32[1,1024]{1,0:T(1,128)} %bitcast.17, f32[192,1024]{1,0:T(8,128)S(1)} %get-tuple-element.64.gqn_ref, bf16[4,512,256]{2,1,0:T(8,128)(2,1)S(1)} %get-tuple-element.65.query_ref, ...), custom_call_target="tpu_custom_call" | custom-call | flops 4194304000 | bytes 8388608 | tf_op jit(solution)/shard_map/key_gradient/pallas_call | solution.py:566
  60.7 0.0 all-to-all-done
  60.7 0.9 %copy.15 = bf16[1,1,16,6,4,1024]{5,4,3,2,1,0:T(4,128)(2,1)} copy(bf16[1,1,16,6,4,1024]{5,4,3,2,1,0:T(4,128)(2,1)S(1)} %bitcast.10) | data formatting | bytes 1572864
Async XLA Ops:
  0.6 12.4 %copy-start = (f32[16]{0:T(128)S(1)}, f32[16]{0:T(128)}, u32[]{:S(2)}) copy-start(f32[16]{0:T(128)} %sharp_ref.3) | copy-start | bytes 196
  3.6 15.8 %collective-permute-start.1 = (bf16[184,1024]{1,0:T(8,128)(2,1)}, bf16[184,1024]{1,0:T(8,128)(2,1)}, u32[]{:S(2)}, u32[]{:S(2)}) collective-permute-start(bf16[184,1024]{1,0:T(8,128)(2,1)} %get-tuple-element.41), channel_id=1, source_target_pairs={{0,2},{2,0},{4,6},{6,4},{8,10},{10,8},{12,14},{14,12},{16,18},{18,... | collective-permute-start | bytes 1130504 | tf_op jit(solution)/shard_map/ppermute | solution.py:641
  4.2 15.3 %collective-permute-start.2 = (bf16[184,1024]{1,0:T(8,128)(2,1)}, bf16[184,1024]{1,0:T(8,128)(2,1)}, u32[]{:S(2)}, u32[]{:S(2)}) collective-permute-start(bf16[184,1024]{1,0:T(8,128)(2,1)} %get-tuple-element.42), channel_id=1, source_target_pairs={{0,30},{2,4},{4,2},{6,8},{8,6},{10,12},{12,10},{14,16},{16,14},{18... | collective-permute-start | bytes 1130504 | tf_op jit(solution)/shard_map/ppermute | solution.py:640
  9.8 9.6 %collective-permute-start = (bf16[96,1024]{1,0:T(8,128)(2,1)}, bf16[96,1024]{1,0:T(8,128)(2,1)S(1)}, u32[]{:S(2)}, u32[]{:S(2)}) collective-permute-start(bf16[96,1024]{1,0:T(8,128)(2,1)} %get-tuple-element.40), channel_id=1, source_target_pairs={{0,1},{1,0},{2,3},{3,2},{4,5},{5,4},{6,7},{7,6},{8,9},{9,8},{10,11... | collective-permute-start | bytes 589832 | tf_op jit(solution)/shard_map/ppermute | solution.py:637
  11.3 8.1 %collective-permute-start.3 = (bf16[40,1024]{1,0:T(8,128)(2,1)}, bf16[40,1024]{1,0:T(8,128)(2,1)}, u32[]{:S(2)}, u32[]{:S(2)}) collective-permute-start(bf16[40,1024]{1,0:T(8,128)(2,1)} %get-tuple-element.43), channel_id=1, source_target_pairs={{0,3},{1,2},{2,1},{3,0},{4,7},{5,6},{6,5},{7,4},{8,11},{9,10},{10,... | collective-permute-start | bytes 245768 | tf_op jit(solution)/shard_map/ppermute | solution.py:638
  11.3 8.1 %collective-permute-start.4 = (bf16[40,1024]{1,0:T(8,128)(2,1)}, bf16[40,1024]{1,0:T(8,128)(2,1)}, u32[]{:S(2)}, u32[]{:S(2)}) collective-permute-start(bf16[40,1024]{1,0:T(8,128)(2,1)} %get-tuple-element.44), channel_id=1, source_target_pairs={{0,31},{1,30},{2,5},{3,4},{4,3},{5,2},{6,9},{7,8},{8,7},{9,6},{10,... | collective-permute-start | bytes 245768 | tf_op jit(solution)/shard_map/ppermute | solution.py:639
  13.0 6.3 %copy-start.4 = (s32[12,4]{0,1:T(4,128)S(1)}, s32[12,4]{0,1:T(4,128)}, u32[]{:S(2)}) copy-start(s32[12,4]{0,1:T(4,128)} %param.19) | copy-start | bytes 580
  13.0 6.4 %copy-start.1 = (s32[2,6]{1,0:T(2,128)S(1)}, s32[2,6]{1,0:T(2,128)}, u32[]{:S(2)}) copy-start(s32[2,6]{1,0:T(2,128)} %flag_ref.3) | copy-start | bytes 148
  29.1 5.8 %collective-permute-start.5 = (f32[72,128]{1,0:T(8,128)S(1)}, f32[72,128]{1,0:T(8,128)S(1)}, u32[]{:S(2)}, u32[]{:S(2)}) collective-permute-start(f32[72,128]{1,0:T(8,128)S(1)} %get-tuple-element.50), channel_id=1, source_target_pairs={{0,2},{2,0},{4,6},{6,4},{8,10},{10,8},{12,14},{14,12},{16,18},{18,... | collective-permute-start | bytes 110600 | tf_op jit(solution)/shard_map/ppermute | solution.py:672
  29.2 6.1 %collective-permute-start.6 = (f32[72,128]{1,0:T(8,128)S(1)}, f32[72,128]{1,0:T(8,128)S(1)}, u32[]{:S(2)}, u32[]{:S(2)}) collective-permute-start(f32[72,128]{1,0:T(8,128)S(1)} %get-tuple-element.51), channel_id=1, source_target_pairs={{0,30},{2,4},{4,2},{6,8},{8,6},{10,12},{12,10},{14,16},{16,14},{18... | collective-permute-start | bytes 110600 | tf_op jit(solution)/shard_map/ppermute | solution.py:671
  34.9 5.3 %copy-start.2 = (f32[72,128]{1,0:T(8,128)}, f32[72,128]{1,0:T(8,128)S(1)}, u32[]{:S(2)}) copy-start(f32[72,128]{1,0:T(8,128)S(1)} %collective-permute-done.5.stat_a_hbm) | copy-start | bytes 110596
  35.3 4.9 %copy-start.3 = (f32[72,128]{1,0:T(8,128)}, f32[72,128]{1,0:T(8,128)S(1)}, u32[]{:S(2)}) copy-start(f32[72,128]{1,0:T(8,128)S(1)} %collective-permute-done.6.stat_b_hbm) | copy-start | bytes 110596
  35.3 25.4 %all-to-all-start = ((bf16[16,6,4,1024]{3,2,1,0:T(4,128)(2,1)}), bf16[16,6,4,1024]{3,2,1,0:T(4,128)(2,1)S(1)}, u32[]{:S(2)}, u32[]{:S(2)}) async-start(bf16[16,6,4,1024]{3,2,1,0:T(4,128)(2,1)} %output_segments.1), calls=%async_computation | async-start | bytes 1572864 | tf_op jit(solution)/shard_map/all_to_all | solution.py:682
  41.6 11.9 %collective-permute-start.7 = (bf16[176,1152]{1,0:T(8,128)(2,1)S(1)}, bf16[176,1152]{1,0:T(8,128)(2,1)S(1)}, u32[]{:S(2)}, u32[]{:S(2)}) collective-permute-start(bf16[176,1152]{1,0:T(8,128)(2,1)S(1)} %boundary_message.1), channel_id=1, source_target_pairs={{0,1},{1,0},{2,3},{3,2},{4,5},{5,4},{6,7},{7,6},{8,9},{9,8},{10,11... | collective-permute-start | bytes 1216520 | tf_op jit(solution)/shard_map/ppermute | solution.py:692

commit v7 on v6

--- a/solution.py
+++ b/solution.py
@@ -279,7 +279,9 @@
     )
     for j in range(STEPS):
         start(j)
-    grad_loads = copies.load_tokens(up_hbm, up_ref, lat) + [copies.start(wo_hbm, wo_ref)]
+    grad_loads = copies.load_tokens(up_hbm, up_ref, lat)
+    parts = [pl.ds(k * D // 2, D // 2) for k in range(2)]
+    wo_loads = [copies.start(wo_hbm.at[part], wo_ref.at[part]) for part in parts]
     outputs = [(qhat_ref, qhat_hbm), (rawq_ref, rawq_hbm), (rawk_ref, rawk_hbm), (kv_ref, kv_hbm)]
     store, stored = copies.by_step(lambda j: [(ref.at[j], hbm.at[j]) for ref, hbm in outputs])
     wait_all(loads)
@@ -298,9 +300,11 @@
         kv_ref[j, 1] = raw[:, 2 * QUAD :].astype(BF)
         store(j)
     wait_all(grad_loads)
-    dout = dot_nt(up_ref[...], wo_ref[...]).astype(BF)
-    for j in range(STEPS):
-        dout_ref[j] = dout[:, j * QUAD : (j + 1) * QUAD]
+    for k, load in enumerate(wo_loads):
+        load.wait()
+        dout = dot_nt(up_ref[...], wo_ref[parts[k]]).astype(BF)
+        for j in range(STEPS // 2):
+            dout_ref[k * STEPS // 2 + j] = dout[:, j * QUAD : (j + 1) * QUAD]
     for j in range(STEPS):
         stored(j)
 

time: 61.9 us -> 61.9 us (level)
  transfers between devices with their start and end apart: 9 -> 9, of which waited for: 1 -> 1; matrix products, arithmetic and copies ran while one was open for 0% -> 0% of each run, Pallas kernels for 44% -> 45%
where the time goes in v7:
time: 61.9 us; the launch traced here: 61.6 us
  Pallas kernels  40.1 us (65%)
  starting transfers between devices  19.1 us (31%)
  local copies, waits for them, and re-layouts  1 us (2%)
  between operations  0.8 us (1%)
    pallas_call x7, Pallas kernels, call(): pl.pallas_call(kernel, in_specs=specs(inputs), out_specs=specs(outputs),...  40.1 us
    ppermute x1, starting transfers between devices, per_device(): edge_b = lax.ppermute(edge_b, 'lon', side_b)  5.67 us
    all_to_all x1, starting transfers between devices, per_device(): lax.all_to_all(going, 'lon', split_axis=0, concat_axis=0, tiled=True)  4.72 us
    ppermute x1, starting transfers between devices, per_device(): stat_b = lax.ppermute(stat_b, 'lon', side_b)  3.4 us
    ppermute x1, starting transfers between devices, per_device(): corner_b = lax.ppermute(corner_b, ('lon', 'lat'), across(side_b))  1.68 us
    ppermute x1, starting transfers between devices, per_device(): message = lax.ppermute(message, 'lat', [(0, 1), (1, 0)])  1.56 us
    ppermute x1, starting transfers between devices, per_device(): band = lax.ppermute(band, 'lat', [(0, 1), (1, 0)])  1.5 us
  transfers between devices with their start and end apart: 9, of which 1 were waited for; matrix products, arithmetic and copies ran while one was open for 0% of the time, Pallas kernels for 45%

profile of v7, /device:TPU:0, one launch (start us, length us, event | category | flops | bytes accessed | tf_op | source)
XLA Modules:
  0.0 61.6 jit_solution(9838129255303227242)
XLA Ops:
  0.6 0.0 copy-start
  0.6 3.0 %edge_tokens.1 = (bf16[184,1024]{1,0:T(8,128)(2,1)}, bf16[184,1024]{1,0:T(8,128)(2,1)}, bf16[96,1024]{1,0:T(8,128)(2,1)}, bf16[40,1024]{1,0:T(8,128)(2,1)}, bf16[40,1024]{1,0:T(8,128)(2,1)}) custom-call(bf16[192,1024]{1,0:T(8,128)(2,1)} %bitcast.13, bf16[192,1024]{1,0:T(8,128)(2,1)} %bitcast.6, bf16[2,96,1024]{2,1,0:T(8,128)(2,1)} %bitcast.11, ...), custom_call_target="tpu_custom_call" | custom-call | bytes 8388608 | tf_op jit(solution)/shard_map/edge_tokens/pallas_call | solution.py:570
  3.6 0.5 collective-permute-start.1
  4.2 5.7 %collective-permute-start.2 = (bf16[184,1024]{1,0:T(8,128)(2,1)}, bf16[184,1024]{1,0:T(8,128)(2,1)}, u32[]{:S(2)}, u32[]{:S(2)}) collective-permute-start(bf16[184,1024]{1,0:T(8,128)(2,1)} %get-tuple-element.42), channel_id=1, source_target_pairs={{0,30},{2,4},{4,2},{6,8},{8,6},{10,12},{12,10},{14,16},{16,14},{18... | collective-permute-start | bytes 1130504 | tf_op jit(solution)/shard_map/ppermute | solution.py:644
  9.8 1.5 %collective-permute-start = (bf16[96,1024]{1,0:T(8,128)(2,1)}, bf16[96,1024]{1,0:T(8,128)(2,1)S(1)}, u32[]{:S(2)}, u32[]{:S(2)}) collective-permute-start(bf16[96,1024]{1,0:T(8,128)(2,1)} %get-tuple-element.40), channel_id=1, source_target_pairs={{0,1},{1,0},{2,3},{3,2},{4,5},{5,4},{6,7},{7,6},{8,9},{9,8},{10,11... | collective-permute-start | bytes 589832 | tf_op jit(solution)/shard_map/ppermute | solution.py:641
  11.3 0.0 collective-permute-start.3
  11.3 1.7 %collective-permute-start.4 = (bf16[40,1024]{1,0:T(8,128)(2,1)}, bf16[40,1024]{1,0:T(8,128)(2,1)}, u32[]{:S(2)}, u32[]{:S(2)}) collective-permute-start(bf16[40,1024]{1,0:T(8,128)(2,1)} %get-tuple-element.44), channel_id=1, source_target_pairs={{0,31},{1,30},{2,5},{3,4},{4,3},{5,2},{6,9},{7,8},{8,7},{9,6},{10,... | collective-permute-start | bytes 245768 | tf_op jit(solution)/shard_map/ppermute | solution.py:643
  13.0 0.0 copy-done
  13.0 0.0 copy-start.4
  13.0 0.0 copy-start.1
  13.0 6.5 %own_projections.1 = (bf16[4,192,256]{2,1,0:T(8,128)(2,1)S(1)}, bf16[4,192,256]{2,1,0:T(8,128)(2,1)S(1)}, bf16[1024,1024]{1,0:T(8,128)(2,1)S(1)}, bf16[192,1024]...) custom-call(f32[16]{0:T(128)S(1)} %copy-done, ...), custom_call_target="tpu_custom_call" | custom-call | flops 2013265920 | bytes 8388608 | tf_op jit(solution)/shard_map/own_projections/pallas_call | solution.py:570
  19.5 0.0 copy-done.4
  19.5 0.1 copy.13.owner_ref
  19.6 0.0 collective-permute-done.3.corner_a_ref
  19.6 0.0 collective-permute-done.4.corner_b_ref
  19.6 0.0 collective-permute-done.band_ref
  19.6 0.0 collective-permute-done.1.edge_a_ref
  19.6 0.0 collective-permute-done.2.edge_b_ref
  19.6 0.0 copy-done.1
  19.6 9.6 %attention_forward.1 = (bf16[192,1024]{1,0:T(8,128)(2,1)S(1)}, f32[72,128]{1,0:T(8,128)S(1)}, f32[72,128]{1,0:T(8,128)S(1)}, bf16[4,2,400,256]{3,2,1,0:T(8,128)(...) custom-call(s32[2,6]{1,0:T(2,128)S(1)} %copy-done.1, ...), custom_call_target="tpu_custom_call" | custom-call | flops 4194304000 | bytes 8388608 | tf_op jit(solution)/shard_map/attention_forward/pallas_call | solution.py:570
  29.3 0.1 collective-permute-start.5
  29.4 3.4 %collective-permute-start.6 = (f32[72,128]{1,0:T(8,128)S(1)}, f32[72,128]{1,0:T(8,128)S(1)}, u32[]{:S(2)}, u32[]{:S(2)}) collective-permute-start(f32[72,128]{1,0:T(8,128)S(1)} %get-tuple-element.51), channel_id=1, source_target_pairs={{0,30},{2,4},{4,2},{6,8},{8,6},{10,12},{12,10},{14,16},{16,14},{18... | collective-permute-start | bytes 110600 | tf_op jit(solution)/shard_map/ppermute | solution.py:675
  32.8 2.1 %output_segments.1 = bf16[16,6,4,1024]{3,2,1,0:T(4,128)(2,1)} custom-call(s32[12,4]{1,0:T(8,128)S(1)} %copy.13.owner_ref, bf16[192,1024]{1,0:T(8,128)(2,1)S(1)} %get-tuple-element.38.x_ref, bf16[192,1024]{1,0:T(8,128)(2,1)S(1)} %get-tuple-element.48.mixed_ref, bf16[1024,1024]{1,0:T(8,128)(2,1)S(1)} %get-tuple-element.49.wo_ref), custom_call_target="tpu_custom_call" | custom-call | flops 419430400 | bytes 8388608 | tf_op jit(solution)/shard_map/output_segments/pallas_call | solution.py:570
  34.9 0.0 collective-permute-done.5.stat_a_hbm
  34.9 0.0 copy-start.2
  34.9 0.6 collective-permute-done.6.stat_b_hbm
  35.5 0.0 copy-start.3
  35.5 4.7 %all-to-all-start = ((bf16[16,6,4,1024]{3,2,1,0:T(4,128)(2,1)}), bf16[16,6,4,1024]{3,2,1,0:T(4,128)(2,1)S(1)}, u32[]{:S(2)}, u32[]{:S(2)}) async-start(bf16[16,6,4,1024]{3,2,1,0:T(4,128)(2,1)} %output_segments.1), calls=%async_computation | async-start | bytes 1572864 | tf_op jit(solution)/shard_map/all_to_all | solution.py:686
  40.2 0.0 copy-done.2
  40.2 0.0 copy-done.3
  40.3 1.3 %boundary_message.1 = bf16[176,1152]{1,0:T(8,128)(2,1)S(1)} custom-call(bf16[192,1024]{1,0:T(8,128)(2,1)} %bitcast.8, bf16[144,1024]{1,0:T(8,128)(2,1)} %get-tuple-element.54.upn_hbm, f32[192,128]{1,0:T(8,128)} %get-tuple-element.61.stat_hbm, f32[72,128]{1,0:T(8,128)} %copy-done.2, f32[72,128]{1,0:T(8,128)} %copy-done.3), custom_call_target="tpu_custom_call" | custom-call | flops 1024 | bytes 8388608 | tf_op jit(solution)/shard_map/boundary_message/pallas_call | solution.py:570
  41.6 1.6 %collective-permute-start.7 = (bf16[176,1152]{1,0:T(8,128)(2,1)S(1)}, bf16[176,1152]{1,0:T(8,128)(2,1)S(1)}, u32[]{:S(2)}, u32[]{:S(2)}) collective-permute-start(bf16[176,1152]{1,0:T(8,128)(2,1)S(1)} %boundary_message.1), channel_id=1, source_target_pairs={{0,1},{1,0},{2,3},{3,2},{4,5},{5,4},{6,7},{7,6},{8,9},{9,8},{10,11... | collective-permute-start | bytes 1216520 | tf_op jit(solution)/shard_map/ppermute | solution.py:696
  43.2 10.4 %query_gradient.1 = (f32[192,1024]{1,0:T(8,128)S(1)}, bf16[4,512,256]{2,1,0:T(8,128)(2,1)S(1)}, bf16[4,336,256]{2,1,0:T(8,128)(2,1)S(1)}, f32[4,2,96,256]{3,2,1,...) custom-call(f32[16]{0:T(128)S(1)} %copy-done, ...), custom_call_target="tpu_custom_call" | custom-call | flops 8388608000 | bytes 8388608 | tf_op jit(solution)/shard_map/query_gradient/pallas_call | solution.py:570
  53.5 0.0 collective-permute-done.7.message_ref
  53.5 7.2 %key_gradient.1 = bf16[192,1024]{1,0:T(8,128)(2,1)} custom-call(bf16[192,1024]{1,0:T(8,128)(2,1)} %bitcast.15, bf16[192,1024]{1,0:T(8,128)(2,1)} %bitcast.9, f32[1,1024]{1,0:T(1,128)} %bitcast.17, f32[192,1024]{1,0:T(8,128)S(1)} %get-tuple-element.64.gqn_ref, bf16[4,512,256]{2,1,0:T(8,128)(2,1)S(1)} %get-tuple-element.65.query_ref, ...), custom_call_target="tpu_custom_call" | custom-call | flops 4194304000 | bytes 8388608 | tf_op jit(solution)/shard_map/key_gradient/pallas_call | solution.py:570
  60.7 0.0 all-to-all-done
  60.7 0.9 %copy.15 = bf16[1,1,16,6,4,1024]{5,4,3,2,1,0:T(4,128)(2,1)} copy(bf16[1,1,16,6,4,1024]{5,4,3,2,1,0:T(4,128)(2,1)S(1)} %bitcast.10) | data formatting | bytes 1572864
Async XLA Ops:
  0.6 12.4 %copy-start = (f32[16]{0:T(128)S(1)}, f32[16]{0:T(128)}, u32[]{:S(2)}) copy-start(f32[16]{0:T(128)} %sharp_ref.3) | copy-start | bytes 196
  3.6 15.9 %collective-permute-start.1 = (bf16[184,1024]{1,0:T(8,128)(2,1)}, bf16[184,1024]{1,0:T(8,128)(2,1)}, u32[]{:S(2)}, u32[]{:S(2)}) collective-permute-start(bf16[184,1024]{1,0:T(8,128)(2,1)} %get-tuple-element.41), channel_id=1, source_target_pairs={{0,2},{2,0},{4,6},{6,4},{8,10},{10,8},{12,14},{14,12},{16,18},{18,... | collective-permute-start | bytes 1130504 | tf_op jit(solution)/shard_map/ppermute | solution.py:645
  4.2 15.4 %collective-permute-start.2 = (bf16[184,1024]{1,0:T(8,128)(2,1)}, bf16[184,1024]{1,0:T(8,128)(2,1)}, u32[]{:S(2)}, u32[]{:S(2)}) collective-permute-start(bf16[184,1024]{1,0:T(8,128)(2,1)} %get-tuple-element.42), channel_id=1, source_target_pairs={{0,30},{2,4},{4,2},{6,8},{8,6},{10,12},{12,10},{14,16},{16,14},{18... | collective-permute-start | bytes 1130504 | tf_op jit(solution)/shard_map/ppermute | solution.py:644
  9.8 9.8 %collective-permute-start = (bf16[96,1024]{1,0:T(8,128)(2,1)}, bf16[96,1024]{1,0:T(8,128)(2,1)S(1)}, u32[]{:S(2)}, u32[]{:S(2)}) collective-permute-start(bf16[96,1024]{1,0:T(8,128)(2,1)} %get-tuple-element.40), channel_id=1, source_target_pairs={{0,1},{1,0},{2,3},{3,2},{4,5},{5,4},{6,7},{7,6},{8,9},{9,8},{10,11... | collective-permute-start | bytes 589832 | tf_op jit(solution)/shard_map/ppermute | solution.py:641
  11.3 8.3 %collective-permute-start.3 = (bf16[40,1024]{1,0:T(8,128)(2,1)}, bf16[40,1024]{1,0:T(8,128)(2,1)}, u32[]{:S(2)}, u32[]{:S(2)}) collective-permute-start(bf16[40,1024]{1,0:T(8,128)(2,1)} %get-tuple-element.43), channel_id=1, source_target_pairs={{0,3},{1,2},{2,1},{3,0},{4,7},{5,6},{6,5},{7,4},{8,11},{9,10},{10,... | collective-permute-start | bytes 245768 | tf_op jit(solution)/shard_map/ppermute | solution.py:642
  11.3 8.3 %collective-permute-start.4 = (bf16[40,1024]{1,0:T(8,128)(2,1)}, bf16[40,1024]{1,0:T(8,128)(2,1)}, u32[]{:S(2)}, u32[]{:S(2)}) collective-permute-start(bf16[40,1024]{1,0:T(8,128)(2,1)} %get-tuple-element.44), channel_id=1, source_target_pairs={{0,31},{1,30},{2,5},{3,4},{4,3},{5,2},{6,9},{7,8},{8,7},{9,6},{10,... | collective-permute-start | bytes 245768 | tf_op jit(solution)/shard_map/ppermute | solution.py:643
  13.0 6.5 %copy-start.4 = (s32[12,4]{0,1:T(4,128)S(1)}, s32[12,4]{0,1:T(4,128)}, u32[]{:S(2)}) copy-start(s32[12,4]{0,1:T(4,128)} %param.19) | copy-start | bytes 580
  13.0 6.6 %copy-start.1 = (s32[2,6]{1,0:T(2,128)S(1)}, s32[2,6]{1,0:T(2,128)}, u32[]{:S(2)}) copy-start(s32[2,6]{1,0:T(2,128)} %flag_ref.3) | copy-start | bytes 148
  29.3 5.6 %collective-permute-start.5 = (f32[72,128]{1,0:T(8,128)S(1)}, f32[72,128]{1,0:T(8,128)S(1)}, u32[]{:S(2)}, u32[]{:S(2)}) collective-permute-start(f32[72,128]{1,0:T(8,128)S(1)} %get-tuple-element.50), channel_id=1, source_target_pairs={{0,2},{2,0},{4,6},{6,4},{8,10},{10,8},{12,14},{14,12},{16,18},{18,... | collective-permute-start | bytes 110600 | tf_op jit(solution)/shard_map/ppermute | solution.py:676
  29.4 6.1 %collective-permute-start.6 = (f32[72,128]{1,0:T(8,128)S(1)}, f32[72,128]{1,0:T(8,128)S(1)}, u32[]{:S(2)}, u32[]{:S(2)}) collective-permute-start(f32[72,128]{1,0:T(8,128)S(1)} %get-tuple-element.51), channel_id=1, source_target_pairs={{0,30},{2,4},{4,2},{6,8},{8,6},{10,12},{12,10},{14,16},{16,14},{18... | collective-permute-start | bytes 110600 | tf_op jit(solution)/shard_map/ppermute | solution.py:675
  34.9 5.3 %copy-start.2 = (f32[72,128]{1,0:T(8,128)}, f32[72,128]{1,0:T(8,128)S(1)}, u32[]{:S(2)}) copy-start(f32[72,128]{1,0:T(8,128)S(1)} %collective-permute-done.5.stat_a_hbm) | copy-start | bytes 110596
  35.5 4.7 %copy-start.3 = (f32[72,128]{1,0:T(8,128)}, f32[72,128]{1,0:T(8,128)S(1)}, u32[]{:S(2)}) copy-start(f32[72,128]{1,0:T(8,128)S(1)} %collective-permute-done.6.stat_b_hbm) | copy-start | bytes 110596
  35.5 25.2 %all-to-all-start = ((bf16[16,6,4,1024]{3,2,1,0:T(4,128)(2,1)}), bf16[16,6,4,1024]{3,2,1,0:T(4,128)(2,1)S(1)}, u32[]{:S(2)}, u32[]{:S(2)}) async-start(bf16[16,6,4,1024]{3,2,1,0:T(4,128)(2,1)} %output_segments.1), calls=%async_computation | async-start | bytes 1572864 | tf_op jit(solution)/shard_map/all_to_all | solution.py:686
  41.6 11.9 %collective-permute-start.7 = (bf16[176,1152]{1,0:T(8,128)(2,1)S(1)}, bf16[176,1152]{1,0:T(8,128)(2,1)S(1)}, u32[]{:S(2)}, u32[]{:S(2)}) collective-permute-start(bf16[176,1152]{1,0:T(8,128)(2,1)S(1)} %boundary_message.1), channel_id=1, source_target_pairs={{0,1},{1,0},{2,3},{3,2},{4,5},{5,4},{6,7},{7,6},{8,9},{9,8},{10,11... | collective-permute-start | bytes 1216520 | tf_op jit(solution)/shard_map/ppermute | solution.py:696
